TPU v7x, 128 devices: a whole 4x4x4 slice. The times are simulated.
128 devices in a mesh: ctx: 64 (over z, x, y), tensor: 2 (over core).
Axes of the slice: x: 4, y: 4, z: 4, core: 2. Of those that a mesh axis runs over, the one named last changes fastest.
Arguments:
- queries: bfloat16 [16384, 2048], P('ctx', 'tensor'), may hold values from -4 to 4
- keys: bfloat16 [16384, 2048], P('ctx', 'tensor'), may hold values from -4 to 4
- values: bfloat16 [16384, 2048], P('ctx', 'tensor'), may hold values from -48 to 48
- rates: float32 [16, 16384], P('tensor', 'ctx'), as said below
- init_weight: float32 [16, 128, 128], P('tensor'), may hold values from -0.5 to 0.5
- gain: float32 [2048], P('tensor'), may hold values from 0.5 to 1.5
- cotangent: bfloat16 [16384, 2048], P('ctx', 'tensor'), may hold values from -5 to 5
Outputs:
- normed: bfloat16 [16384, 2048], P('ctx', 'tensor')
- grad_queries: bfloat16 [16384, 2048], P('ctx', 'tensor')
- grad_keys: bfloat16 [16384, 2048], P('ctx', 'tensor')
- grad_values: bfloat16 [16384, 2048], P('ctx', 'tensor')
- grad_rates: float32 [16, 16384], P('tensor', 'ctx')
- grad_init: float32 [16, 16384], P('tensor', 'ctx')
Inputs may be any that keep to these rules, and one draw needn't show every extreme that they name: `rates`: every rate times 128 lies between 0.0006 and 1.12.
All inputs are finite; a program needn't handle non-finite values.
Results may differ from a plain program's by a relative error of at most 0.022.
Values sent between devices are 32-bit elements; how exact they have to be, the bound alone decides.
No kernel may reach another device: no remote copies, remote signals or barrier semaphores. Data moves between devices by JAX's collectives and lax.ppermute only.
A program may use at most 256 MiB of HBM per device.

v0:
```python
import jax
import jax.numpy as jnp
from jax import lax
from jax.experimental import pallas as pl
from jax.experimental.pallas import tpu as pltpu
from jax.sharding import PartitionSpec as P

HEAD = 128
MB = 16
EPSILON = 1e-06
GROUP = 8
F32 = jnp.float32
BF16 = jnp.bfloat16


def low(a):
    return a.astype(BF16)


def dot(a, b):
    return jnp.dot(a, b, preferred_element_type=F32)


def dot_nt(a, b):
    return lax.dot_general(a, b, (((1,), (1,)), ((), ())), preferred_element_type=F32)


def dot_tn(a, b):
    return lax.dot_general(a, b, (((0,), (0,)), ((), ())), preferred_element_type=F32)


def halves(a):
    high = low(a)
    return high, low(a - high.astype(F32))


def exact(a, b, product=dot):
    (ah, al), (bh, bl) = a, b
    return product(ah, bh) + (product(ah, bl) + product(al, bh))


def call(kernel, outs, args, smem=0, scratch=(), limit=32):
    specs = [pl.BlockSpec(memory_space=pltpu.SMEM)] * smem
    specs += [pl.BlockSpec(memory_space=pltpu.VMEM)] * (len(args) - smem)
    size = sum(a.size * a.dtype.itemsize for a in args)
    size += sum(o.size * o.dtype.itemsize for o in outs)
    return pl.pallas_call(
        kernel,
        out_shape=outs,
        in_specs=specs,
        out_specs=[pl.BlockSpec(memory_space=pltpu.VMEM)] * len(outs),
        scratch_shapes=list(scratch),
        compiler_params=pltpu.CompilerParams(vmem_limit_bytes=limit * 2**20),
        cost_estimate=pl.CostEstimate(flops=2 * 10**9, bytes_accessed=size, transcendentals=0),
        name=kernel.__name__,
    )(*args)


def columns(h):
    return slice(h * HEAD, (h + 1) * HEAD)


def map_kernel(k_ref, v_ref, e_ref, ab_ref, t_ref, tkv_ref):
    n = k_ref.shape[0]
    heads = e_ref.shape[0]
    row = lax.broadcasted_iota(jnp.int32, (n, n), 0)
    col = lax.broadcasted_iota(jnp.int32, (n, n), 1)
    eye = (row == col).astype(F32)
    small = (
        lax.broadcasted_iota(jnp.int32, (HEAD, HEAD), 0)
        == lax.broadcasted_iota(jnp.int32, (HEAD, HEAD), 1)
    ).astype(F32)
    masks = []
    width = MB
    while width < n:
        masks.append((row // (2 * width) == col // (2 * width)) & (row // width > col // width))
        width *= 2
    for first in range(0, heads, 4):
        batch = range(first, first + 4)
        ks = [k_ref[:, columns(h)] for h in batch]
        rates = [e_ref[h : h + 1, :] for h in batch]
        grams = [dot_nt(k, k) * e for k, e in zip(ks, rates)]
        inverses = [eye - jnp.where(masks[0], g, 0.0) for g in grams]
        for mask in masks[1:]:
            lows = [low(t) for t in inverses]
            mids = [dot(low(jnp.where(mask, g, 0.0)), t) for g, t in zip(grams, lows)]
            inverses = [t - dot(b, low(m)) for t, b, m in zip(inverses, lows, mids)]
        lows = [low(t) for t in inverses]
        tkvs = [
            low(dot(t, jnp.concatenate([k, v_ref[:, columns(h)]], axis=1)))
            for t, k, h in zip(lows, ks, batch)
        ]
        scaled = [low(jnp.transpose(k.astype(F32)) * e) for k, e in zip(ks, rates)]
        abs_ = [dot(s, x) for s, x in zip(scaled, tkvs)]
        for i, h in enumerate(batch):
            ab_ref[h, :, :HEAD] = small - abs_[i][:, :HEAD]
            ab_ref[h, :, HEAD:] = abs_[i][:, HEAD:]
            t_ref[h] = lows[i]
            tkv_ref[h] = tkvs[i]


def prepare_kernel(q_ref, k_ref, e_ref, t_ref, tkv_ref, qt_ref, c_ref, se_ref, tek_ref):
    n = k_ref.shape[0]
    heads = e_ref.shape[0]
    row = lax.broadcasted_iota(jnp.int32, (n, n), 0)
    col = lax.broadcasted_iota(jnp.int32, (n, n), 1)
    causal = row >= col
    for h in range(heads):
        q = q_ref[:, columns(h)]
        k = k_ref[:, columns(h)]
        e = e_ref[h : h + 1, :]
        se = low(jnp.where(causal, dot_nt(q, k) * e, 0.0))
        sx = dot(se, tkv_ref[h])
        qt_ref[h] = low(q.astype(F32) - sx[:, :HEAD])
        c_ref[h] = sx[:, HEAD:]
        se_ref[h] = se
        wide = jnp.transpose(jnp.broadcast_to(e, (HEAD, n)))
        tek_ref[h] = low(dot_tn(t_ref[h], low(k.astype(F32) * wide)))


def compose(early, late):
    wide = exact(halves(late[:, :HEAD]), halves(early))
    return jnp.concatenate([wide[:, :HEAD], wide[:, HEAD:] + late[:, HEAD:]], axis=1)


def group_kernel(ab_ref, all_ref, tree_ref):
    pairs = [compose(ab_ref[2 * i], ab_ref[2 * i + 1]) for i in range(4)]
    quads = [compose(pairs[2 * i], pairs[2 * i + 1]) for i in range(2)]
    whole = compose(quads[0], quads[1])
    for i, a in enumerate(pairs + quads):
        tree_ref[i] = a
    for i in range(GROUP):
        all_ref[i] = whole


def apply_map(ab, w):
    return exact(halves(ab[:, :HEAD]), halves(w)) + ab[:, HEAD:]


def start_kernel(group_ref, ab_ref, tree_ref, groups_ref, init_ref, w_ref):
    w0 = lax.fori_loop(
        0, group_ref[0], lambda g, w: apply_map(groups_ref[g], w), init_ref[...]
    )
    w4 = apply_map(tree_ref[4], w0)
    w2 = apply_map(tree_ref[0], w0)
    w6 = apply_map(tree_ref[2], w4)
    for i, w in zip((0, 2, 4, 6), (w0, w2, w4, w6)):
        w_ref[i] = w
        w_ref[i + 1] = apply_map(ab_ref[i], w)


def hidden_kernel(qt_ref, c_ref, w_ref, cot_ref, gain_ref, z_ref, stats_ref):
    heads, n = qt_ref.shape[:2]
    squares = jnp.zeros((n, HEAD), F32)
    products = jnp.zeros((n, HEAD), F32)
    for h in range(heads):
        z = dot(qt_ref[h], low(w_ref[h])) + c_ref[h]
        z_ref[:, columns(h)] = z
        squares += z * z
        products += z * (cot_ref[:, columns(h)].astype(F32) * gain_ref[:, columns(h)])
    lane = lax.broadcasted_iota(jnp.int32, (n, HEAD), 1)
    stats_ref[...] = jnp.where(
        lane < HEAD // 2,
        jnp.sum(squares, axis=1, keepdims=True),
        jnp.sum(products, axis=1, keepdims=True),
    )


def norm_kernel(z_ref, cot_ref, gain_ref, own_ref, other_ref, qt_ref, normed_ref, dz_ref, g_ref):
    heads = qt_ref.shape[0]
    width = 2 * z_ref.shape[1]
    stats = own_ref[...] + other_ref[...]
    inv = lax.rsqrt(stats[:, 0:1] / width + EPSILON)
    shift = inv * inv * inv * stats[:, HEAD // 2 : HEAD // 2 + 1] / width
    for h in range(heads):
        z = z_ref[:, columns(h)]
        gain = gain_ref[:, columns(h)]
        normed_ref[:, columns(h)] = low(z * inv * gain)
        dz = low(inv * (cot_ref[:, columns(h)].astype(F32) * gain) - z * shift)
        dz_ref[:, columns(h)] = dz
        g_ref[h] = dot_tn(qt_ref[h], dz)


def query_kernel(
    q_ref, k_ref, e_ref, t_ref, tkv_ref, se_ref, w_ref, dz_ref, dq_ref, u_ref, dk_ref, r_ref
):
    n = k_ref.shape[0]
    heads = e_ref.shape[0]
    row = lax.broadcasted_iota(jnp.int32, (n, n), 0)
    col = lax.broadcasted_iota(jnp.int32, (n, n), 1)
    causal = row >= col
    for h in range(heads):
        e = e_ref[h : h + 1, :]
        w = low(w_ref[h])
        dz = dz_ref[:, columns(h)]
        r = low(dot(tkv_ref[h, :, :HEAD], w) - tkv_ref[h, :, HEAD:].astype(F32))
        r_ref[h] = r
        ds = low(jnp.where(causal, dot_nt(dz, r) * -e, 0.0))
        dq_ref[:, columns(h)] = low(dot_nt(dz, w) + dot(ds, k_ref[:, columns(h)]))
        dk_ref[h] = dot_tn(ds, q_ref[:, columns(h)])
        u_ref[h] = -dot_tn(t_ref[h], low(dot_tn(se_ref[h], dz)))


def transposed_map(a, later, own):
    return exact(halves(a), halves(later), dot_tn) + own


def gather_kernel(ab_ref, tree_ref, g_ref, all_ref, sums_ref):
    pairs = [
        transposed_map(ab_ref[2 * i, :, :HEAD], g_ref[2 * i + 1], g_ref[2 * i]) for i in range(4)
    ]
    quads = [
        transposed_map(tree_ref[2 * i, :, :HEAD], pairs[2 * i + 1], pairs[2 * i])
        for i in range(2)
    ]
    whole = transposed_map(tree_ref[4, :, :HEAD], quads[1], quads[0])
    for i, a in enumerate(pairs + quads):
        sums_ref[i] = a
    for i in range(GROUP):
        all_ref[i] = whole


def end_kernel(
    group_ref, ab_ref, tree_ref, groups_ref, g_ref, sums_ref, later_ref, d_ref, init_ref
):
    group = group_ref[0]

    def step(i, d):
        g = GROUP - 1 - i
        return transposed_map(groups_ref[g, :, :HEAD], d, later_ref[g])

    d7 = lax.fori_loop(0, GROUP - 1 - group, step, jnp.zeros((HEAD, HEAD), F32))
    init_ref[...] = lax.fori_loop(GROUP - 1 - group, GROUP, step, d7)
    d3 = transposed_map(tree_ref[5, :, :HEAD], d7, sums_ref[5])
    d1 = transposed_map(tree_ref[1, :, :HEAD], d3, sums_ref[1])
    d5 = transposed_map(tree_ref[3, :, :HEAD], d7, sums_ref[3])
    for i, d in zip((1, 3, 5, 7), (d1, d3, d5, d7)):
        d_ref[i, :HEAD, :] = d
        d_ref[i - 1, :HEAD, :] = transposed_map(ab_ref[i, :, :HEAD], d, g_ref[i])
    rows = init_ref[pl.ds(pl.multiple_of(group * 16, 16), 16), :]
    for i in range(GROUP):
        d_ref[i, HEAD:, :] = jnp.zeros((8, HEAD), F32)
        d_ref[i, HEAD : HEAD + 2, :] = rows[2 * i : 2 * i + 2]


def key_kernel(
    k_ref, e_ref, tek_ref, w_ref, r_ref, u_ref, dkp_ref, d_ref, dk_ref, dv_ref, de_ref, gi_ref
):
    n = k_ref.shape[0]
    heads = e_ref.shape[0]
    row = lax.broadcasted_iota(jnp.int32, (n, n), 0)
    col = lax.broadcasted_iota(jnp.int32, (n, n), 1)
    before = row // MB > col // MB
    ones = jnp.ones((8, HEAD), BF16)
    for h in range(heads):
        e = e_ref[h : h + 1, :]
        k = k_ref[:, columns(h)]
        r = r_ref[h]
        d = low(d_ref[h, :HEAD, :])
        uf = u_ref[h] - dot(tek_ref[h], d)
        u = low(uf)
        dv_ref[:, columns(h)] = low(-uf)
        ph, pl_ = halves(uf * r.astype(F32))
        de_ref[h : h + 1, :] = (dot_nt(ones, ph) + dot_nt(ones, pl_))[0:1] / e
        x = low(jnp.where(before, dot_nt(u, r) * e, 0.0))
        wide = jnp.transpose(jnp.broadcast_to(e, (HEAD, n)))
        dk = dkp_ref[h] + dot_nt(u, low(w_ref[h])) - wide * dot_nt(r, d)
        dk_ref[:, columns(h)] = low(dk - dot(x, k) - dot_tn(x, k))
        gi_ref[h : h + 1, :HEAD] = d_ref[h, HEAD : HEAD + 1, :]
        gi_ref[h : h + 1, HEAD:] = d_ref[h, HEAD + 1 : HEAD + 2, :]


def local(queries, keys, values, rates, init_weight, gain, cotangent):
    n, width = keys.shape
    heads = width // HEAD
    count = lax.axis_size("ctx") // GROUP
    near = [[g * GROUP + i for i in range(GROUP)] for g in range(count)]
    far = [[g * GROUP + i for g in range(count)] for i in range(GROUP)]
    place = lax.axis_index("ctx")
    group = (place // GROUP).astype(jnp.int32).reshape(1)
    own_init = lax.dynamic_index_in_dim(init_weight, place % GROUP, 0, False)
    gain_row = gain.reshape(1, width)

    def shape(dims, dtype=F32):
        return jax.ShapeDtypeStruct(dims, dtype)

    def swap(a, groups):
        return lax.all_to_all(a, "ctx", 0, 0, axis_index_groups=groups)

    square = (GROUP, HEAD, HEAD)
    wide = (GROUP, HEAD, 2 * HEAD)
    tall = (heads, n, HEAD)
    full = (heads, n, n)

    maps, inverse, tkv = call(
        map_kernel, [shape(wide), shape(full, BF16), shape((heads, n, 2 * HEAD), BF16)],
        [keys, values, rates],
    )
    own_maps = swap(maps, near)
    qt, offset, scores, tek = call(
        prepare_kernel, [shape(tall, BF16), shape(tall), shape(full, BF16), shape(tall, BF16)],
        [queries, keys, rates, inverse, tkv],
    )
    sent, tree = call(group_kernel, [shape(wide), shape((6, HEAD, 2 * HEAD))], [own_maps])
    group_maps = swap(sent, far)
    (starts,) = call(
        start_kernel, [shape(square)], [group, own_maps, tree, group_maps, own_init], smem=1
    )
    weights = swap(starts, near)
    hidden, stats = call(
        hidden_kernel, [shape((n, width)), shape((n, HEAD))],
        [qt, offset, weights, cotangent, gain_row],
    )
    other = lax.ppermute(stats, "tensor", [(0, 1), (1, 0)])
    normed, dz, local_grad = call(
        norm_kernel, [shape((n, width), BF16), shape((n, width), BF16), shape(square)],
        [hidden, cotangent, gain_row, stats, other, qt],
    )
    own_grads = swap(local_grad, near)
    grad_queries, u, dk_part, residual = call(
        query_kernel,
        [shape((n, width), BF16), shape(tall), shape(tall), shape(tall, BF16)],
        [queries, keys, rates, inverse, tkv, scores, weights, dz],
    )
    sent, sums = call(
        gather_kernel, [shape(square), shape((6, HEAD, HEAD))], [own_maps, tree, own_grads]
    )
    group_grads = swap(sent, far)
    (ends,) = call(
        end_kernel, [shape((GROUP, HEAD + 8, HEAD))],
        [group, own_maps, tree, group_maps, own_grads, sums, group_grads], smem=1,
        scratch=[pltpu.VMEM((HEAD, HEAD), F32)],
    )
    adjoint = swap(ends, near)
    grad_keys, grad_values, grad_rates, grad_init = call(
        key_kernel,
        [shape((n, width), BF16), shape((n, width), BF16), shape((heads, n)), shape((heads, n))],
        [keys, rates, tek, weights, residual, u, dk_part, adjoint],
    )
    return (normed, grad_queries, grad_keys, grad_values, grad_rates, grad_init)


def solution(mesh):
    in_specs = (
        P("ctx", "tensor"),
        P("ctx", "tensor"),
        P("ctx", "tensor"),
        P("tensor", "ctx"),
        P("tensor", None, None),
        P("tensor"),
        P("ctx", "tensor"),
    )
    out_specs = (
        P("ctx", "tensor"),
        P("ctx", "tensor"),
        P("ctx", "tensor"),
        P("ctx", "tensor"),
        P("tensor", "ctx"),
        P("tensor", "ctx"),
    )
    return jax.shard_map(local, mesh=mesh, in_specs=in_specs, out_specs=out_specs, check_vma=False)
```

profile of v0, /device:TPU:0, one launch (start us, length us, event | category | flops | bytes accessed | tf_op | source)
XLA Modules:
  0.0 136.7 jit_solution(1273802995497328283)
XLA Ops:
  0.7 1.1 copy-done.3
  1.7 1.0 copy-done.7
  3.5 3.7 %map_kernel.1 = (f32[8,128,256]{2,1,0:T(8,128)S(1)}, bf16[8,256,256]{2,1,0:T(8,128)(2,1)S(1)}, bf16[8,256,256]{2,1,0:T(8,128)(2,1)S(1)}) custom-call(bf16[256,1024]{1,0:T(8,128)(2,1)S(1)} %copy-done.7, bf16[256,1024]{1,0:T(8,128)(2,1)S(1)} %copy-done.3, f32[8,256]{1,0:T(8,128)S(1)} %copy-done.11), custom_call_target="tpu_custom_call" | custom-call | flops 2000000000 | bytes 4202496 | tf_op jit(solution)/shard_map/map_kernel/pallas_call | solution.py:47
  9.1 21.0 %all_to_all.30.ab_ref = f32[8,128,256]{2,1,0:T(8,128)S(1)} all-to-all(f32[8,128,256]{2,1,0:T(8,128)S(1)} %get-tuple-element.34), channel_id=1, replica_groups={{0,2,4,6,8,10,12,14},{16,18,20,22,24,26,28,30},{32,34,36,38,40,42,44,46..., dimensions={0} | all-to-all | bytes 2097152 | tf_op jit(solution)/shard_map/all_to_all | solution.py:288
  32.0 7.5 %all-to-all-start.1 = ((f32[8,128,256]{2,1,0:T(8,128)}), f32[8,128,256]{2,1,0:T(8,128)S(1)}, u32[]{:S(2)}, u32[]{:S(2)}) async-start(f32[8,128,256]{2,1,0:T(8,128)} %copy-done.1), calls=%async_computation.1 | async-start | bytes 2097152 | tf_op jit(solution)/shard_map/all_to_all | solution.py:288
  39.5 15.4 %all-to-all-done.1.groups_ref = f32[8,128,256]{2,1,0:T(8,128)S(1)} async-done(((f32[8,128,256]{2,1,0:T(8,128)}), f32[8,128,256]{2,1,0:T(8,128)S(1)}, u32[]{:S(2)}, u32[]{:S(2)}) %all-to-all-start.1) | async-done | bytes 1048608 | tf_op jit(solution)/shard_map/all_to_all | solution.py:288
  56.3 3.6 %all-to-all-start.2 = ((f32[8,128,128]{2,1,0:T(8,128)}), f32[8,128,128]{2,1,0:T(8,128)S(1)}, u32[]{:S(2)}, u32[]{:S(2)}) async-start(f32[8,128,128]{2,1,0:T(8,128)} %copy-done.2), calls=%async_computation.2 | async-start | bytes 1048576 | tf_op jit(solution)/shard_map/all_to_all | solution.py:288
  59.9 1.0 copy-done.5
  60.9 1.0 copy-done.8
  62.0 1.2 copy-done.15
  63.2 1.2 copy-done.18
  64.4 1.7 %prepare_kernel.1 = (bf16[8,256,128]{2,1,0:T(8,128)(2,1)S(1)}, f32[8,256,128]{2,1,0:T(8,128)S(1)}, bf16[8,256,256]{2,1,0:T(8,128)(2,1)S(1)}, bf16[8,256,128]{2,1,0:T(8,128)(2,1)S(1)}) custom-call(bf16[256,1024]{1,0:T(8,128)(2,1)S(1)} %copy-done.5, bf16[256,1024]{1,0:T(8,128)(2,1)S(1)} %copy-done.8, f32[8,256]{1,0:T(8,128)S(1)} %copy-done.12, ...), custom_call_target="tpu_custom_call" | custom-call | flops 2000000000 | bytes 6299648 | tf_op jit(solution)/shard_map/prepare_kernel/pallas_call | solution.py:47
  70.4 1.0 copy-done.4
  71.4 1.2 copy-done.35
  72.6 1.0 copy-done.37
  74.2 1.3 collective-permute-done.other_ref
  75.6 1.3 norm_kernel.1
  77.7 15.9 %all_to_all.31.g_ref = f32[8,128,128]{2,1,0:T(8,128)S(1)} all-to-all(f32[8,128,128]{2,1,0:T(8,128)S(1)} %get-tuple-element.47), channel_id=1, replica_groups={{0,2,4,6,8,10,12,14},{16,18,20,22,24,26,28,30},{32,34,36,38,40,42,44,46..., dimensions={0} | all-to-all | bytes 1048576 | tf_op jit(solution)/shard_map/all_to_all | solution.py:288
  94.3 13.9 %all_to_all.32.later_ref = f32[8,128,128]{2,1,0:T(8,128)S(1)} all-to-all(f32[8,128,128]{2,1,0:T(8,128)S(1)} %get-tuple-element.49), channel_id=1, replica_groups={{0,16,32,48,64,80,96,112},{2,18,34,50,66,82,98,114},{4,20,36,52,68,84,1..., dimensions={0} | all-to-all | bytes 1048576 | tf_op jit(solution)/shard_map/all_to_all | solution.py:288
  108.2 3.2 %end_kernel.1 = f32[8,136,128]{2,1,0:T(8,128)} custom-call(s32[1]{0:T(128)} %bitcast.group_ref, f32[8,128,256]{2,1,0:T(8,128)S(1)} %all_to_all.30.ab_ref, f32[6,128,256]{2,1,0:T(8,128)S(1)} %copy-done.27, f32[8,128,256]{2,1,0:T(8,128)S(1)} %all-to-all-done.1.groups_ref, f32[8,128,128]{2,1,0:T(8,128)S(1)} %all_to_all.31.g_ref, ...), custom_call_target="tpu_custom_call" | custom-call | flops 2000000000 | bytes 4882436 | tf_op jit(solution)/shard_map/end_kernel/pallas_call | solution.py:47
  111.3 3.8 %all-to-all-start.5 = ((f32[8,136,128]{2,1,0:T(8,128)}), f32[8,136,128]{2,1,0:T(8,128)S(1)}, u32[]{:S(2)}, u32[]{:S(2)}) async-start(f32[8,136,128]{2,1,0:T(8,128)} %end_kernel.1), calls=%async_computation.5 | async-start | bytes 1114112 | tf_op jit(solution)/shard_map/all_to_all | solution.py:288
  116.2 1.0 copy-done.9
  117.3 1.2 copy-done.19
  118.5 1.2 copy-done.21
  119.7 1.0 copy-done.29
  120.8 3.7 %query_kernel.1 = (bf16[256,1024]{1,0:T(8,128)(2,1)}, f32[8,256,128]{2,1,0:T(8,128)S(1)}, f32[8,256,128]{2,1,0:T(8,128)S(1)}, bf16[8,256,128]{2,1,0:T(8,128)(2,1)S(1)}) custom-call(bf16[256,1024]{1,0:T(8,128)(2,1)S(1)} %copy-done.6, bf16[256,1024]{1,0:T(8,128)(2,1)S(1)} %copy-done.9, f32[8,256]{1,0:T(8,128)S(1)} %copy-done.12, ...), custom_call_target="tpu_custom_call" | custom-call | flops 2000000000 | bytes 8396800 | tf_op jit(solution)/shard_map/query_kernel/pallas_call | solution.py:47
  127.3 1.0 copy-done.10
  128.3 1.2 copy-done.23
  129.5 1.2 copy-done.25
  130.8 1.0 copy-done.31
  131.8 1.0 copy-done.33
  132.9 3.8 %key_kernel.1 = (bf16[256,1024]{1,0:T(8,128)(2,1)}, bf16[256,1024]{1,0:T(8,128)(2,1)}, f32[8,256]{1,0:T(8,128)}, f32[8,256]{1,0:T(8,128)}) custom-call(bf16[256,1024]{1,0:T(8,128)(2,1)S(1)} %copy-done.10, f32[8,256]{1,0:T(8,128)S(1)} %copy-done.12, bf16[8,256,128]{2,1,0:T(8,128)(2,1)S(1)} %copy-done.33, f32[8,128,128]{2,1,0:T(8,128)S(1)} %all-to-all-done.2.w_ref, ...), custom_call_target="tpu_custom_call" | custom-call | flops 2000000000 | bytes 5824512 | tf_op jit(solution)/shard_map/key_kernel/pallas_call | solution.py:47
  (68 shorter events, 15.9 us)
Async XLA Ops:
  0.6 38.8 %copy-start = (f32[8,128,128]{2,1,0:T(8,128)S(1)}, f32[8,128,128]{2,1,0:T(8,128)}, u32[]{:S(2)}) copy-start(f32[8,128,128]{2,1,0:T(8,128)} %param.11) | copy-start | bytes 1572868
  0.6 1.1 copy-start.3
  1.7 1.0 copy-start.7
  7.2 1.0 copy-start.14
  32.0 22.9 %copy-start.26 = (f32[6,128,256]{2,1,0:T(8,128)}, f32[6,128,256]{2,1,0:T(8,128)S(1)}, u32[]{:S(2)}) copy-start(f32[6,128,256]{2,1,0:T(8,128)S(1)} %get-tuple-element.35.tree_ref) | copy-start | bytes 2359300
  32.0 22.9 %all-to-all-start.1 = ((f32[8,128,256]{2,1,0:T(8,128)}), f32[8,128,256]{2,1,0:T(8,128)S(1)}, u32[]{:S(2)}, u32[]{:S(2)}) async-start(f32[8,128,256]{2,1,0:T(8,128)} %copy-done.1), calls=%async_computation.1 | async-start | bytes 2097152 | tf_op jit(solution)/shard_map/all_to_all | solution.py:288
  56.3 3.6 %copy-start.12 = (f32[8,256]{1,0:T(8,128)S(1)}, f32[8,256]{1,0:T(8,128)}, u32[]{:S(2)}) copy-start(f32[8,256]{1,0:T(8,128)} %e_ref.7) | copy-start | bytes 24580
  56.3 13.4 %all-to-all-start.2 = ((f32[8,128,128]{2,1,0:T(8,128)}), f32[8,128,128]{2,1,0:T(8,128)S(1)}, u32[]{:S(2)}, u32[]{:S(2)}) async-start(f32[8,128,128]{2,1,0:T(8,128)} %copy-done.2), calls=%async_computation.2 | async-start | bytes 1048576 | tf_op jit(solution)/shard_map/all_to_all | solution.py:288
  59.9 1.0 copy-start.5
  60.9 1.0 copy-start.8
  62.0 1.2 copy-start.15
  63.2 1.2 copy-start.18
  67.9 1.0 copy-start.34
  70.4 1.0 copy-start.4
  71.4 1.2 copy-start.35
  72.6 1.0 copy-start.37
  73.7 1.9 %copy-start.38 = (bf16[8,256,128]{2,1,0:T(8,128)(2,1)S(1)}, bf16[8,256,128]{2,1,0:T(8,128)(2,1)}, u32[]{:S(2)}) copy-start(bf16[8,256,128]{2,1,0:T(8,128)(2,1)} %copy-done.36) | copy-start | bytes 1572868
  74.1 1.4 %collective-permute-start = (f32[256,128]{1,0:T(8,128)S(1)}, f32[256,128]{1,0:T(8,128)S(1)}, u32[]{:S(2)}, u32[]{:S(2)}) collective-permute-start(f32[256,128]{1,0:T(8,128)S(1)} %get-tuple-element.38.own_ref), channel_id=1, source_target_pairs={{0,1},{1,0},{2,3},{3,2},{4,5},{5,4},{6,7},{7,6},{8,9},{9,8},{10,11... | collective-permute-start | bytes 393224 | tf_op jit(solution)/shard_map/ppermute | solution.py:314
  77.7 15.9 %copy-start.27 = (f32[6,128,256]{2,1,0:T(8,128)S(1)}, f32[6,128,256]{2,1,0:T(8,128)}, u32[]{:S(2)}) copy-start(f32[6,128,256]{2,1,0:T(8,128)} %copy-done.26) | copy-start | bytes 2359300
  111.3 3.9 %copy-start.16 = (bf16[8,256,256]{2,1,0:T(8,128)(2,1)S(1)}, bf16[8,256,256]{2,1,0:T(8,128)(2,1)}, u32[]{:S(2)}) copy-start(bf16[8,256,256]{2,1,0:T(8,128)(2,1)} %copy-done.14) | copy-start | bytes 3145732
  111.3 15.9 %all-to-all-start.5 = ((f32[8,136,128]{2,1,0:T(8,128)}), f32[8,136,128]{2,1,0:T(8,128)S(1)}, u32[]{:S(2)}, u32[]{:S(2)}) async-start(f32[8,136,128]{2,1,0:T(8,128)} %end_kernel.1), calls=%async_computation.5 | async-start | bytes 1114112 | tf_op jit(solution)/shard_map/all_to_all | solution.py:288
  115.2 1.0 copy-start.6
  116.2 1.0 copy-start.9
  117.3 1.2 copy-start.19
  118.5 1.2 copy-start.21
  119.7 1.0 copy-start.29
  124.5 1.0 copy-start.22
  127.3 1.0 copy-start.10
  128.3 1.2 copy-start.23
  129.5 1.2 copy-start.25
  130.8 1.0 copy-start.31
  131.8 1.0 copy-start.33
  (11 other events, 9.2 us)
where the time goes:
time: 138 us; the launch traced here: 137 us
  blocking collectives  50.8 us (37%)
  local copies, waits for them, and re-layouts  33.3 us (24%)
  Pallas kernels  19.9 us (14%)
  waiting for transfers between devices  16.8 us (12%)
  starting transfers between devices  15 us (11%)
    all_to_all x3, blocking collectives, swap(): return lax.all_to_all(a, 'ctx', 0, 0, axis_index_groups=groups)  50.8 us
    unnamed x78, local copies, waits for them, and re-layouts  33.3 us
    pallas_call x10, Pallas kernels, call(): pl.pallas_call(kernel, out_shape=outs, in_specs=specs, out_specs=[pl.Bloc...  19.9 us
    all_to_all x3, waiting for transfers between devices, swap(): return lax.all_to_all(a, 'ctx', 0, 0, axis_index_groups=groups)  15.4 us
    all_to_all x3, starting transfers between devices, swap(): return lax.all_to_all(a, 'ctx', 0, 0, axis_index_groups=groups)  14.9 us
  transfers between devices with their start and end apart: 4, of which 2 were waited for; matrix products, arithmetic and copies ran while one was open for 0% of the time, Pallas kernels for 4%

commit v1 on v0

v1 whole, which is shorter than its diff:
```python
import jax
import jax.numpy as jnp
from jax import lax
from jax.experimental import pallas as pl
from jax.experimental.pallas import tpu as pltpu
from jax.sharding import PartitionSpec as P

HEAD = 128
MB = 16
EPSILON = 1e-06
GROUP = 8
F32 = jnp.float32
BF16 = jnp.bfloat16


def low(a):
    return a.astype(BF16)


def dot(a, b):
    return jnp.dot(a, b, preferred_element_type=F32)


def dot_nt(a, b):
    return lax.dot_general(a, b, (((1,), (1,)), ((), ())), preferred_element_type=F32)


def dot_tn(a, b):
    return lax.dot_general(a, b, (((0,), (0,)), ((), ())), preferred_element_type=F32)


def halves(a):
    high = low(a)
    return high, low(a - high.astype(F32))


def exact(a, b, product=dot):
    (ah, al), (bh, bl) = a, b
    return product(ah, bh) + (product(ah, bl) + product(al, bh))


def call(kernel, outs, args, scratch=(), copies=0, limit=24):
    spaces = {"s": pltpu.SMEM, "v": pltpu.VMEM, "h": pltpu.HBM, "a": pltpu.VMEM}
    values = [pltpu.with_memory_space_constraint(a, pltpu.HBM) if p in "ha" else a for a, p in args]
    results = [
        pltpu.HBM(shape, dtype) if p in "ha" else jax.ShapeDtypeStruct(shape, dtype)
        for shape, dtype, p in outs
    ]
    size = sum(a.size * a.dtype.itemsize for a in values)
    scratch = list(scratch)
    if copies:
        scratch.append(pltpu.SemaphoreType.DMA((copies,)))
    return pl.pallas_call(
        kernel,
        out_shape=results,
        in_specs=[pl.BlockSpec(memory_space=spaces[p]) for _, p in args],
        out_specs=[pl.BlockSpec(memory_space=spaces[p]) for _, _, p in outs],
        scratch_shapes=scratch,
        compiler_params=pltpu.CompilerParams(vmem_limit_bytes=limit * 2**20),
        cost_estimate=pl.CostEstimate(
            flops=2 * 10**9, bytes_accessed=2 * size, transcendentals=0
        ),
        name=kernel.__name__,
    )(*values)


class Copies:
    def __init__(self, semaphores):
        self.semaphores = semaphores
        self.started = []

    def start(self, source, target):
        copy = pltpu.make_async_copy(source, target, self.semaphores.at[len(self.started)])
        copy.start()
        self.started.append(copy)
        return copy


def columns(h):
    return slice(h * HEAD, (h + 1) * HEAD)


def span(first, last):
    return slice(first * HEAD, last * HEAD)


BATCH = 4


def map_kernel(
    k_hbm, v_hbm, e_hbm, ab_hbm, t_hbm, n_hbm, tkv_hbm,
    k_ref, v_ref, e_ref, ab_ref, t_ref, n_ref, tkv_ref, sems,
):
    heads = e_ref.shape[0]
    half = t_ref.shape[-1]
    copies = Copies(sems)
    arrivals = []
    for first in range(0, heads, BATCH):
        part = span(first, first + BATCH)
        key = copies.start(k_hbm.at[:, part], k_ref.at[:, part])
        if first == 0:
            rates = copies.start(e_hbm, e_ref)
        arrivals.append((key, copies.start(v_hbm.at[:, part], v_ref.at[:, part])))
    row = lax.broadcasted_iota(jnp.int32, (half, half), 0)
    col = lax.broadcasted_iota(jnp.int32, (half, half), 1)
    eye = (row == col).astype(F32)
    masks = []
    width = MB
    while width < half:
        masks.append((row // (2 * width) == col // (2 * width)) & (row // width > col // width))
        width *= 2
    sent = []
    ks, es, blocks, crosses, scaled = [], [], [], [], []
    for first, (key, _) in zip(range(0, heads, BATCH), arrivals):
        key.wait()
        if first == 0:
            rates.wait()
        for h in range(first, first + BATCH):
            k = k_ref[:, columns(h)]
            e = e_ref[h : h + 1, :]
            top = -(dot_nt(k[:half], k[:half]) * e[:, :half])
            bottom = -(dot_nt(k[half:], k) * e)
            blocks += [top, bottom[:, half:]]
            crosses.append(low(bottom[:, :half]))
            ks.append(k)
            es.append(e)
    inverses = [low(eye + jnp.where(masks[0], b, 0.0)) for b in blocks]
    for mask in masks[1:]:
        mids = [low(dot(low(jnp.where(mask, b, 0.0)), t)) for b, t in zip(blocks, inverses)]
        inverses = [t + low(dot(t, m)) for t, m in zip(inverses, mids)]
    for h in range(heads):
        t_ref[h, 0] = inverses[2 * h]
        t_ref[h, 1] = inverses[2 * h + 1]
        n_ref[h] = crosses[h]
    sent.append(copies.start(t_ref, t_hbm))
    sent.append(copies.start(n_ref, n_hbm))
    for _, value in arrivals:
        value.wait()
    kvs = [jnp.concatenate([ks[h], v_ref[:, columns(h)]], axis=1) for h in range(heads)]
    tops = [low(dot(t, kv[:half])) for t, kv in zip(inverses[::2], kvs)]
    scaled = [low(jnp.transpose(k.astype(F32)) * e) for k, e in zip(ks, es)]
    mids = [low(kv[half:].astype(F32) + dot(c, x)) for kv, c, x in zip(kvs, crosses, tops)]
    bottoms = [low(dot(t, m)) for t, m in zip(inverses[1::2], mids)]
    for h in range(heads):
        tkv_ref[h, :half] = tops[h]
        tkv_ref[h, half:] = bottoms[h]
    sent.append(copies.start(tkv_ref, tkv_hbm))
    for h in range(heads):
        ab = dot(scaled[h], tkv_ref[h])
        ab_ref[h, :, :HEAD] = eye - ab[:, :HEAD]
        ab_ref[h, :, HEAD:] = ab[:, HEAD:]
        if h % 2 == 1:
            sent.append(copies.start(ab_ref.at[h - 1 : h + 1], ab_hbm.at[h - 1 : h + 1]))
    for copy in sent:
        copy.wait()


def prepare_kernel(
    q_ref, k_ref, e_ref, t_ref, n_ref, tkv_ref, init_hbm,
    qt_ref, qtt_ref, c_ref, st_ref, tek_ref, own_hbm, token_ref, sems,
):
    initial = Copies(sems).start(init_hbm.at[lax.axis_index("ctx") % GROUP], own_hbm)
    n = k_ref.shape[0]
    half = n // 2
    heads = e_ref.shape[0]
    row = lax.broadcasted_iota(jnp.int32, (n, n), 0)
    col = lax.broadcasted_iota(jnp.int32, (n, n), 1)
    causal = row >= col
    token_ref[...] = jnp.zeros_like(token_ref)
    for h in range(heads):
        q = q_ref[:, columns(h)]
        k = k_ref[:, columns(h)]
        e = e_ref[h : h + 1, :]
        se = low(jnp.where(causal, dot_nt(q, k) * e, 0.0))
        sx = dot(se, tkv_ref[h])
        qt = q.astype(F32) - sx[:, :HEAD]
        qt_ref[h] = low(qt)
        qtt_ref[h] = low(jnp.transpose(qt))
        c_ref[h] = sx[:, HEAD:]
        top, bottom = t_ref[h, 0], t_ref[h, 1]
        cross = low(dot(bottom, low(dot(n_ref[h], top))))
        t = jnp.concatenate(
            [
                jnp.concatenate([top, jnp.zeros((half, half), BF16)], axis=1),
                jnp.concatenate([cross, bottom], axis=1),
            ],
            axis=0,
        )
        st_ref[h] = low(-dot(se, t))
        wide = jnp.transpose(jnp.broadcast_to(e, (HEAD, n)))
        tek_ref[h] = low(dot_tn(t, low(k.astype(F32) * wide)))
    initial.wait()


def compose(early, late):
    wide = exact(halves(late[:, :HEAD]), halves(early))
    return jnp.concatenate([wide[:, :HEAD], wide[:, HEAD:] + late[:, HEAD:]], axis=1)


def broadcast(copies, source, targets):
    sent = [copies.start(source, targets.at[i]) for i in range(GROUP)]
    for copy in sent:
        copy.wait()


def group_kernel(ab_ref, token_ref, all_ref, tree_hbm, tree_ref, sems):
    copies = Copies(sems)
    pairs = [compose(ab_ref[2 * i], ab_ref[2 * i + 1]) for i in range(4)]
    quads = [compose(pairs[2 * i], pairs[2 * i + 1]) for i in range(2)]
    for i, a in enumerate(pairs + quads):
        tree_ref[i] = a
    tree = copies.start(tree_ref, tree_hbm)
    whole = compose(quads[0], quads[1])
    for i in range(GROUP):
        all_ref[i] = whole
    tree.wait()


def apply_map(ab, w):
    return exact(halves(ab[:, :HEAD]), halves(w)) + ab[:, HEAD:]


def start_kernel(ab_ref, tree_ref, groups_ref, init_ref, w_ref):
    group = lax.axis_index("ctx") // GROUP
    w0 = lax.fori_loop(0, group, lambda g, w: apply_map(groups_ref[g], w), init_ref[...])
    w4 = apply_map(tree_ref[4], w0)
    w2 = apply_map(tree_ref[0], w0)
    w6 = apply_map(tree_ref[2], w4)
    for i, w in zip((0, 2, 4, 6), (w0, w2, w4, w6)):
        w_ref[i] = w
        w_ref[i + 1] = apply_map(ab_ref[i], w)


def adjoint_kernel(ab_ref, groups_ref, inside_ref, after_ref, first_ref, token_ref):
    eye = (
        lax.broadcasted_iota(jnp.int32, (HEAD, HEAD), 0)
        == lax.broadcasted_iota(jnp.int32, (HEAD, HEAD), 1)
    ).astype(F32)
    token_ref[...] = jnp.zeros_like(token_ref)
    inside = first = after = eye
    group = lax.axis_index("ctx") // GROUP
    for i in range(GROUP):
        own = GROUP - 1 - i
        inside_ref[own] = inside
        first_ref[i] = first
        later = i > group
        after_ref[i] = jnp.where(later, after, 0.0)
        if i < GROUP - 1:
            inside = exact(halves(ab_ref[own, :, :HEAD]), halves(inside), dot_tn)
            step = halves(groups_ref[i, :, :HEAD])
            first = exact(halves(first), step, dot_nt)
            after = jnp.where(later, exact(halves(after), step, dot_nt), eye)


def hidden_kernel(qt_ref, c_ref, cot_ref, gain_ref, w_ref, z_ref, stats_ref):
    heads, n = qt_ref.shape[:2]
    squares = jnp.zeros((n, HEAD), F32)
    products = jnp.zeros((n, HEAD), F32)
    for h in range(heads):
        z = dot(qt_ref[h], low(w_ref[h])) + c_ref[h]
        z_ref[:, columns(h)] = z
        squares += z * z
        products += z * (cot_ref[:, columns(h)].astype(F32) * gain_ref[:, columns(h)])
    lane = lax.broadcasted_iota(jnp.int32, (n, HEAD), 1)
    stats_ref[...] = jnp.where(
        lane < HEAD // 2,
        jnp.sum(squares, axis=1, keepdims=True),
        jnp.sum(products, axis=1, keepdims=True),
    )


def norm_kernel(
    z_ref, cot_ref, gain_ref, own_ref, other_ref, qtt_ref,
    normed_hbm, dz_hbm, g_hbm, normed_ref, dz_ref, g_ref, sems,
):
    heads = qtt_ref.shape[0]
    width = 2 * z_ref.shape[1]
    copies = Copies(sems)
    stats = own_ref[...] + other_ref[...]
    inv = lax.rsqrt(stats[:, 0:1] / width + EPSILON)
    shift = inv * inv * inv * stats[:, HEAD // 2 : HEAD // 2 + 1] / width
    for h in range(heads):
        go = cot_ref[:, columns(h)].astype(F32) * gain_ref[:, columns(h)]
        dz = low(inv * go - z_ref[:, columns(h)] * shift)
        dz_ref[:, columns(h)] = dz
        g_ref[h] = dot(qtt_ref[h], dz)
        if h % BATCH == BATCH - 1:
            part = slice(h + 1 - BATCH, h + 1)
            copies.start(g_ref.at[part], g_hbm.at[part])
    copies.start(dz_ref, dz_hbm)
    for h in range(heads):
        normed_ref[:, columns(h)] = low(z_ref[:, columns(h)] * inv * gain_ref[:, columns(h)])
    copies.start(normed_ref, normed_hbm)
    for copy in copies.started:
        copy.wait()


def query_kernel(
    q_ref, k_ref, e_ref, tkv_ref, st_ref, w_ref, dz_ref,
    dq_ref, u_ref, dk_ref, er_ref, token_ref,
):
    n = k_ref.shape[0]
    heads = e_ref.shape[0]
    row = lax.broadcasted_iota(jnp.int32, (n, n), 0)
    col = lax.broadcasted_iota(jnp.int32, (n, n), 1)
    causal = row >= col
    token_ref[...] = jnp.zeros_like(token_ref)
    for h in range(heads):
        e = e_ref[h : h + 1, :]
        w = low(w_ref[h])
        dz = dz_ref[:, columns(h)]
        r = dot(tkv_ref[h, :, :HEAD], w) - tkv_ref[h, :, HEAD:].astype(F32)
        er = low(r * jnp.transpose(jnp.broadcast_to(e, (HEAD, n))))
        er_ref[h] = er
        ds = low(jnp.where(causal, -dot_nt(dz, er), 0.0))
        dq_ref[:, columns(h)] = low(dot_nt(dz, w) + dot(ds, k_ref[:, columns(h)]))
        dk_ref[h] = low(dot_tn(ds, q_ref[:, columns(h)]))
        u_ref[h] = low(dot_tn(st_ref[h], dz))


def transposed_map(a, later, own):
    return exact(halves(a), halves(later), dot_tn) + own


def gather_kernel(ab_ref, tree_ref, g_ref, token_ref, all_hbm, whole_ref, sems):
    pairs = [
        transposed_map(ab_ref[2 * i, :, :HEAD], g_ref[2 * i + 1], g_ref[2 * i]) for i in range(4)
    ]
    quads = [
        transposed_map(tree_ref[2 * i, :, :HEAD], pairs[2 * i + 1], pairs[2 * i])
        for i in range(2)
    ]
    whole_ref[...] = transposed_map(tree_ref[4, :, :HEAD], quads[1], quads[0])
    broadcast(Copies(sems), whole_ref, all_hbm)


def tail_kernel(ab_ref, g_ref, sums_ref):
    tail = jnp.zeros((HEAD, HEAD), F32)
    sums_ref[GROUP - 1] = tail
    for i in range(GROUP - 1, 0, -1):
        if i < GROUP - 1:
            tail = transposed_map(ab_ref[i, :, :HEAD], tail, g_ref[i])
        else:
            tail = g_ref[i]
        sums_ref[i - 1] = tail


def end_kernel(
    after_hbm, first_hbm, inside_hbm, sums_hbm, later_ref, d_ref,
    init_ref, after_ref, first_ref, inside_ref, sums_ref, sems,
):
    copies = Copies(sems)
    arrivals = [
        copies.start(source, target)
        for source, target in (
            (after_hbm, after_ref), (first_hbm, first_ref), (inside_hbm, inside_ref),
            (sums_hbm, sums_ref),
        )
    ]
    parts = [halves(later_ref[g]) for g in range(GROUP)]
    arrivals[0].wait()
    end = exact(halves(after_ref[1]), parts[1])
    for g in range(2, GROUP):
        end += exact(halves(after_ref[g]), parts[g])
    arrivals[1].wait()
    start = later_ref[0]
    for g in range(1, GROUP):
        start += exact(halves(first_ref[g]), parts[g])
    init_ref[...] = start
    ends = halves(end)
    for copy in arrivals[2:]:
        copy.wait()
    rows = init_ref[pl.ds(pl.multiple_of(lax.axis_index("ctx") // GROUP * 16, 16), 16), :]
    for i in range(GROUP):
        d = end
        if i < GROUP - 1:
            d = exact(halves(inside_ref[i]), ends) + sums_ref[i]
        d_ref[i, :HEAD, :] = d
        d_ref[i, HEAD:, :] = jnp.zeros((8, HEAD), F32)
        d_ref[i, HEAD : HEAD + 2, :] = rows[2 * i : 2 * i + 2]


def key_kernel(
    k_ref, e_ref, tek_ref, er_ref, u_ref, dkp_ref, w_ref, d_ref,
    dk_hbm, dv_hbm, de_ref, gi_ref, dk_ref, dv_ref, sems,
):
    n = k_ref.shape[0]
    heads = e_ref.shape[0]
    copies = Copies(sems)
    row = lax.broadcasted_iota(jnp.int32, (n, n), 0) // MB
    col = lax.broadcasted_iota(jnp.int32, (n, n), 1) // MB
    before = row > col
    after = row < col
    ones = jnp.ones((8, HEAD), BF16)
    for h in range(heads):
        gi_ref[h : h + 1, :HEAD] = d_ref[h, HEAD : HEAD + 1, :]
        gi_ref[h : h + 1, HEAD:] = d_ref[h, HEAD + 1 : HEAD + 2, :]
    for first in range(0, heads, BATCH):
        batch = range(first, first + BATCH)
        ds = [low(d_ref[h, :HEAD, :]) for h in batch]
        both = [jnp.concatenate([low(w_ref[h]), -d], axis=1) for h, d in zip(batch, ds)]
        ers = [er_ref[h] for h in batch]
        us = [u_ref[h].astype(F32) - dot(tek_ref[h], d) for h, d in zip(batch, ds)]
        lows = [low(u) for u in us]
        for h, u in zip(batch, lows):
            dv_ref[:, columns(h)] = -u
        flat = span(first, first + BATCH)
        copies.start(dv_ref.at[:, flat], dv_hbm.at[:, flat])
        ps = [low(u * er.astype(F32)) for u, er in zip(us, ers)]
        xs = [
            low(jnp.where(before, dot_nt(u, er), jnp.where(after, dot_nt(er, u), 0.0)))
            for u, er in zip(lows, ers)
        ]
        dks = [
            dkp_ref[h].astype(F32) + dot_nt(jnp.concatenate([u, er], axis=1), b)
            for h, u, er, b in zip(batch, lows, ers, both)
        ]
        for h, dk, x, p in zip(batch, dks, xs, ps):
            e = e_ref[h : h + 1, :]
            dk_ref[:, columns(h)] = low(dk - dot(x, k_ref[:, columns(h)]))
            de_ref[h : h + 1, :] = dot_nt(ones, p)[0:1] / (e * e)
        copies.start(dk_ref.at[:, flat], dk_hbm.at[:, flat])
    for copy in copies.started:
        copy.wait()


def local(queries, keys, values, rates, init_weight, gain, cotangent):
    n, width = keys.shape
    heads = width // HEAD
    count = lax.axis_size("ctx") // GROUP
    near = [[g * GROUP + i for i in range(GROUP)] for g in range(count)]
    far = [[g * GROUP + i for g in range(count)] for i in range(GROUP)]
    gain_row = gain.reshape(1, width)

    def swap(a, groups):
        return lax.all_to_all(a, "ctx", 0, 0, axis_index_groups=groups)

    square = (GROUP, HEAD, HEAD)
    wide = (GROUP, HEAD, 2 * HEAD)
    tall = (heads, n, HEAD)
    full = (heads, n, n)
    flat = (n, width)
    branches = (6, HEAD, 2 * HEAD)
    token = ((8, HEAD), F32, "v")
    parts = heads // BATCH
    vm = pltpu.VMEM

    half = n // 2
    inner = (heads, 2, half, half)
    corner = (heads, half, half)
    turned = (heads, HEAD, n)
    maps, inverse, cross, tkv = call(
        map_kernel,
        [
            (wide, F32, "h"), (inner, BF16, "h"), (corner, BF16, "h"),
            ((heads, n, 2 * HEAD), BF16, "h"),
        ],
        [(keys, "h"), (values, "h"), (rates, "h")],
        [
            vm(flat, BF16), vm(flat, BF16), vm((heads, n), F32),
            vm(wide, F32), vm(inner, BF16), vm(corner, BF16), vm((heads, n, 2 * HEAD), BF16),
        ],
        copies=4 + 2 * parts + heads // 2,
    )
    own_maps = swap(maps, near)
    qt, qt_turned, offset, scores, tek, own_init, prepared = call(
        prepare_kernel,
        [
            (tall, BF16, "a"), (turned, BF16, "a"), (tall, F32, "a"), (full, BF16, "a"),
            (tall, BF16, "a"), ((HEAD, HEAD), F32, "h"), token,
        ],
        [
            (queries, "a"), (keys, "a"), (rates, "a"), (inverse, "a"), (cross, "a"), (tkv, "a"),
            (init_weight, "h"),
        ],
        copies=1,
    )
    sent, tree = call(
        group_kernel,
        [(wide, F32, "v"), (branches, F32, "h")],
        [(own_maps, "v"), (prepared, "v")],
        [vm(branches, F32)],
        copies=1,
    )
    group_maps = swap(sent, far)
    (starts,) = call(
        start_kernel,
        [(square, F32, "v")],
        [(own_maps, "v"), (tree, "v"), (group_maps, "v"), (own_init, "v")],
    )
    weights = swap(starts, near)
    hidden, stats = call(
        hidden_kernel,
        [(flat, F32, "v"), ((n, HEAD), F32, "v")],
        [(qt, "v"), (offset, "v"), (cotangent, "v"), (gain_row, "v"), (weights, "v")],
    )
    other = lax.ppermute(stats, "tensor", [(0, 1), (1, 0)])
    normed, dz, local_grad = call(
        norm_kernel,
        [(flat, BF16, "h"), (flat, BF16, "h"), (square, F32, "h")],
        [
            (hidden, "v"), (cotangent, "v"), (gain_row, "v"), (stats, "v"), (other, "v"),
            (qt_turned, "v"),
        ],
        [vm(flat, BF16), vm(flat, BF16), vm(square, F32)],
        copies=2 + parts,
    )
    own_grads = swap(local_grad, near)
    grad_queries, u, dk_part, scaled_residual, queried = call(
        query_kernel,
        [(flat, BF16, "a"), (tall, BF16, "a"), (tall, BF16, "a"), (tall, BF16, "a"), token],
        [
            (queries, "a"), (keys, "a"), (rates, "a"), (tkv, "a"), (scores, "a"),
            (weights, "v"), (dz, "a"),
        ],
    )
    (sent,) = call(
        gather_kernel,
        [(square, F32, "h")],
        [(own_maps, "v"), (tree, "v"), (own_grads, "v"), (queried, "v")],
        [vm((HEAD, HEAD), F32)],
        copies=GROUP,
    )
    group_grads = swap(sent, far)
    inside, after, first = call(
        adjoint_kernel,
        [(square, F32, "a"), (square, F32, "a"), (square, F32, "a"), token],
        [(own_maps, "v"), (group_maps, "v")],
    )[:3]
    (sums,) = call(tail_kernel, [(square, F32, "a")], [(own_maps, "v"), (own_grads, "v")])
    ending = (GROUP, HEAD + 8, HEAD)
    (ends,) = call(
        end_kernel,
        [(ending, F32, "v")],
        [(after, "h"), (first, "h"), (inside, "h"), (sums, "h"), (group_grads, "v")],
        [vm((HEAD, HEAD), F32)] + [vm(square, F32)] * 4,
        copies=4,
    )
    adjoint = swap(ends, near)
    grad_keys, grad_values, grad_rates, grad_init = call(
        key_kernel,
        [(flat, BF16, "h"), (flat, BF16, "h"), ((heads, n), F32, "v"), ((heads, n), F32, "v")],
        [
            (keys, "v"), (rates, "v"), (tek, "v"), (scaled_residual, "v"), (u, "v"),
            (dk_part, "v"), (weights, "v"), (adjoint, "v"),
        ],
        [vm(flat, BF16), vm(flat, BF16)],
        copies=2 * parts,
    )
    return (normed, grad_queries, grad_keys, grad_values, grad_rates, grad_init)


def solution(mesh):
    in_specs = (
        P("ctx", "tensor"),
        P("ctx", "tensor"),
        P("ctx", "tensor"),
        P("tensor", "ctx"),
        P("tensor", None, None),
        P("tensor"),
        P("ctx", "tensor"),
    )
    out_specs = (
        P("ctx", "tensor"),
        P("ctx", "tensor"),
        P("ctx", "tensor"),
        P("ctx", "tensor"),
        P("tensor", "ctx"),
        P("tensor", "ctx"),
    )
    return jax.shard_map(local, mesh=mesh, in_specs=in_specs, out_specs=out_specs, check_vma=False)
```

time: 138 us -> 121 us (0.88)
  local copies, waits for them, and re-layouts: 33.3 us -> 1.87 us
  Pallas kernels: 19.9 us -> 35.4 us
    unnamed x78 -> x28, local copies, waits for them, and re-layouts: 33.3 us -> 1.87 us
    pallas_call x10 -> x12, Pallas kernels: 19.9 us -> 35.4 us  [call(): pl.pallas_call(kernel, out_shape=results, in_specs=[pl.BlockSpec(memory_s...]
  transfers between devices with their start and end apart: 4 -> 4, of which waited for: 2 -> 4; matrix products, arithmetic and copies ran while one was open for 0% -> 0% of each run, Pallas kernels for 4% -> 16%
where the time goes in v1:
time: 121 us
  blocking collectives  50.3 us (42%)
  Pallas kernels  35.4 us (29%)
  waiting for transfers between devices  17.7 us (15%)
  starting transfers between devices  14.2 us (12%)
  local copies, waits for them, and re-layouts  1.87 us (2%)
    all_to_all x3, blocking collectives, swap(): return lax.all_to_all(a, 'ctx', 0, 0, axis_index_groups=groups)  50.3 us
    pallas_call x12, Pallas kernels, call(): pl.pallas_call(kernel, out_shape=results, in_specs=[pl.BlockSpec(memory_s...  35.4 us
    all_to_all x3, waiting for transfers between devices, swap(): return lax.all_to_all(a, 'ctx', 0, 0, axis_index_groups=groups)  16.4 us
    all_to_all x3, starting transfers between devices, swap(): return lax.all_to_all(a, 'ctx', 0, 0, axis_index_groups=groups)  14.1 us
  transfers between devices with their start and end apart: 4, of which 4 were waited for; matrix products, arithmetic and copies ran while one was open for 0% of the time, Pallas kernels for 16%

profile of v1, /device:TPU:0, one launch (start us, length us, event | category | flops | bytes accessed | tf_op | source)
XLA Modules:
  0.0 120.5 jit_solution(2246852545199371475)
XLA Ops:
  0.6 4.2 %map_kernel.1 = (f32[8,128,256]{2,1,0:T(8,128)}, bf16[8,2,128,128]{3,2,1,0:T(8,128)(2,1)}, bf16[8,128,128]{2,1,0:T(8,128)(2,1)}, bf16[8,256,256]{2,1,0:T(8,128)(2,1)}) custom-call(bf16[256,1024]{1,0:T(8,128)(2,1)} %k_ref.5, bf16[256,1024]{1,0:T(8,128)(2,1)} %v_hbm.1, f32[8,256]{1,0:T(8,128)} %e_ref.5), custom_call_target="tpu_custom_call" | custom-call | flops 2000000000 | bytes 2113536 | tf_op jit(solution)/shard_map/map_kernel/pallas_call | solution.py:53
  4.9 5.5 %all-to-all-start = ((f32[8,128,256]{2,1,0:T(8,128)}), f32[8,128,256]{2,1,0:T(8,128)S(1)}, u32[]{:S(2)}, u32[]{:S(2)}) async-start(f32[8,128,256]{2,1,0:T(8,128)} %get-tuple-element.41), calls=%async_computation | async-start | bytes 2097152 | tf_op jit(solution)/shard_map/all_to_all | solution.py:436
  10.4 7.4 %prepare_kernel.1 = (bf16[8,256,128]{2,1,0:T(8,128)(2,1)}, bf16[8,128,256]{2,1,0:T(8,128)(2,1)}, f32[8,256,128]{2,1,0:T(8,128)}, bf16[8,256,256]{2,1,0:T(8,128)(...) custom-call(bf16[256,1024]{1,0:T(8,128)(2,1)} %q_ref.3, bf16[256,1024]{1,0:T(8,128)(2,1)} %k_ref.5, ...), custom_call_target="tpu_custom_call" | custom-call | flops 2000000000 | bytes 6832128 | tf_op jit(solution)/shard_map/prepare_kernel/pallas_call | solution.py:53
  17.8 7.4 %all-to-all-done.ab_ref = f32[8,128,256]{2,1,0:T(8,128)S(1)} async-done(((f32[8,128,256]{2,1,0:T(8,128)}), f32[8,128,256]{2,1,0:T(8,128)S(1)}, u32[]{:S(2)}, u32[]{:S(2)}) %all-to-all-start) | async-done | bytes 1048608 | tf_op jit(solution)/shard_map/all_to_all | solution.py:436
  25.2 1.5 %group_kernel.1 = (f32[8,128,256]{2,1,0:T(8,128)S(1)}, f32[6,128,256]{2,1,0:T(8,128)}) custom-call(f32[8,128,256]{2,1,0:T(8,128)S(1)} %all-to-all-done.ab_ref, f32[8,128]{1,0:T(8,128)S(1)} %get-tuple-element.42.token_ref), custom_call_target="tpu_custom_call" | custom-call | flops 2000000000 | bytes 2105344 | tf_op jit(solution)/shard_map/group_kernel/pallas_call | solution.py:53
  26.7 0.0 copy-start.8
  26.7 0.0 copy-start.13
  26.7 24.4 %all_to_all.30.groups_ref = f32[8,128,256]{2,1,0:T(8,128)S(1)} all-to-all(f32[8,128,256]{2,1,0:T(8,128)S(1)} %get-tuple-element.44), channel_id=1, replica_groups={{0,16,32,48,64,80,96,112},{2,18,34,50,66,82,98,114},{4,20,36,52,68,84,1..., dimensions={0} | all-to-all | bytes 2097152 | tf_op jit(solution)/shard_map/all_to_all | solution.py:436
  51.1 0.0 copy-done.13
  51.1 0.6 start_kernel.1
  51.7 0.0 copy-start
  51.7 0.0 copy-start.12
  51.7 12.1 %all_to_all.31.w_ref = f32[8,128,128]{2,1,0:T(8,128)S(1)} all-to-all(f32[8,128,128]{2,1,0:T(8,128)S(1)} %start_kernel.1), channel_id=1, replica_groups={{0,2,4,6,8,10,12,14},{16,18,20,22,24,26,28,30},{32,34,36,38,40,42,44,46..., dimensions={0} | all-to-all | bytes 1048576 | tf_op jit(solution)/shard_map/all_to_all | solution.py:436
  63.9 0.7 copy-done.3
  64.6 0.5 hidden_kernel.1
  65.1 0.1 collective-permute-start
  65.2 1.3 %collective-permute-done.other_ref = f32[256,128]{1,0:T(8,128)S(1)} collective-permute-done((f32[256,128]{1,0:T(8,128)S(1)}, f32[256,128]{1,0:T(8,128)S(1)}, u32[]{:S(2)}, u32[]{:S(2)}) %collective-permute-start) | collective-permute-done | bytes 131104 | tf_op jit(solution)/shard_map/ppermute | solution.py:497
  66.5 1.8 %norm_kernel.1 = (bf16[256,1024]{1,0:T(8,128)(2,1)}, bf16[256,1024]{1,0:T(8,128)(2,1)}, f32[8,128,128]{2,1,0:T(8,128)}) custom-call(f32[256,1024]{1,0:T(8,128)S(1)} %get-tuple-element.46.z_ref, bf16[256,1024]{1,0:T(8,128)(2,1)S(1)} %copy-done, f32[1,1024]{1,0:T(1,128)S(1)} %bitcast.2, f32[256,128]{1,0:T(8,128)S(1)} %get-tuple-element.47.own_ref, ...), custom_call_target="tpu_custom_call" | custom-call | flops 2000000000 | bytes 4726784 | tf_op jit(solution)/shard_map/norm_kernel/pallas_call | solution.py:53
  68.3 3.5 %all-to-all-start.3 = ((f32[8,128,128]{2,1,0:T(8,128)}), f32[8,128,128]{2,1,0:T(8,128)S(1)}, u32[]{:S(2)}, u32[]{:S(2)}) async-start(f32[8,128,128]{2,1,0:T(8,128)} %get-tuple-element.60), calls=%async_computation.3 | async-start | bytes 1048576 | tf_op jit(solution)/shard_map/all_to_all | solution.py:436
  71.8 6.9 %query_kernel.1 = (bf16[256,1024]{1,0:T(8,128)(2,1)}, bf16[8,256,128]{2,1,0:T(8,128)(2,1)}, bf16[8,256,128]{2,1,0:T(8,128)(2,1)}, bf16[8,256,128]{2,1,0:T(8,128)(2,1)}, f32[8,128]{1,0:T(8,128)S(1)}) custom-call(bf16[256,1024]{1,0:T(8,128)(2,1)} %q_ref.3, bf16[256,1024]{1,0:T(8,128)(2,1)} %k_ref.5, f32[8,256]{1,0:T(8,128)} %e_ref.5, ...), custom_call_target="tpu_custom_call" | custom-call | flops 2000000000 | bytes 8404992 | tf_op jit(solution)/shard_map/query_kernel/pallas_call | solution.py:53
  78.7 3.0 %all-to-all-done.3.g_ref = f32[8,128,128]{2,1,0:T(8,128)S(1)} async-done(((f32[8,128,128]{2,1,0:T(8,128)}), f32[8,128,128]{2,1,0:T(8,128)S(1)}, u32[]{:S(2)}, u32[]{:S(2)}) %all-to-all-start.3) | async-done | bytes 524320 | tf_op jit(solution)/shard_map/all_to_all | solution.py:436
  81.7 1.1 copy-done.9
  82.9 1.6 %gather_kernel.1 = f32[8,128,128]{2,1,0:T(8,128)} custom-call(f32[8,128,256]{2,1,0:T(8,128)S(1)} %all-to-all-done.ab_ref, f32[6,128,256]{2,1,0:T(8,128)S(1)} %copy-done.9, f32[8,128,128]{2,1,0:T(8,128)S(1)} %all-to-all-done.3.g_ref, f32[8,128]{1,0:T(8,128)S(1)} %get-tuple-element.61.token_ref), custom_call_target="tpu_custom_call" | custom-call | flops 2000000000 | bytes 4726784 | tf_op jit(solution)/shard_map/gather_kernel/pallas_call | solution.py:53
  84.4 5.1 %all-to-all-start.4 = ((f32[8,128,128]{2,1,0:T(8,128)}), f32[8,128,128]{2,1,0:T(8,128)}, u32[]{:S(2)}, u32[]{:S(2)}) async-start(f32[8,128,128]{2,1,0:T(8,128)} %gather_kernel.1), calls=%async_computation.4 | async-start | bytes 1048576 | tf_op jit(solution)/shard_map/all_to_all | solution.py:436
  89.5 2.6 %adjoint_kernel.1 = (f32[8,128,128]{2,1,0:T(8,128)}, f32[8,128,128]{2,1,0:T(8,128)}, f32[8,128,128]{2,1,0:T(8,128)}, f32[8,128]{1,0:T(8,128)}) custom-call(f32[8,128,256]{2,1,0:T(8,128)S(1)} %all-to-all-done.ab_ref, f32[8,128,256]{2,1,0:T(8,128)S(1)} %all_to_all.30.groups_ref), custom_call_target="tpu_custom_call" | custom-call | flops 2000000000 | bytes 4194304 | tf_op jit(solution)/shard_map/adjoint_kernel/pallas_call | solution.py:53
  92.1 1.9 %tail_kernel.1.sums_hbm = f32[8,128,128]{2,1,0:T(8,128)} custom-call(f32[8,128,256]{2,1,0:T(8,128)S(1)} %all-to-all-done.ab_ref, f32[8,128,128]{2,1,0:T(8,128)S(1)} %all-to-all-done.3.g_ref), custom_call_target="tpu_custom_call" | custom-call | flops 2000000000 | bytes 3145728 | tf_op jit(solution)/shard_map/tail_kernel/pallas_call | solution.py:53
  94.0 6.0 %all-to-all-done.4.later_ref = f32[8,128,128]{2,1,0:T(8,128)} async-done(((f32[8,128,128]{2,1,0:T(8,128)}), f32[8,128,128]{2,1,0:T(8,128)}, u32[]{:S(2)}, u32[]{:S(2)}) %all-to-all-start.4) | async-done | bytes 524320 | tf_op jit(solution)/shard_map/all_to_all | solution.py:436
  100.0 3.6 %end_kernel.1 = f32[8,136,128]{2,1,0:T(8,128)S(1)} custom-call(f32[8,128,128]{2,1,0:T(8,128)} %get-tuple-element.57.after_hbm, f32[8,128,128]{2,1,0:T(8,128)} %get-tuple-element.58.first_hbm, f32[8,128,128]{2,1,0:T(8,128)} %get-tuple-element.59.inside_hbm, f32[8,128,128]{2,1,0:T(8,128)} %tail_kernel.1.sums_hbm, f32[8,128,128]{2,1,0:T(8,128)} %all-to-all-done.4.later_ref), custom_call_target="tpu_custom_call" | custom-call | flops 2000000000 | bytes 5242880 | tf_op jit(solution)/shard_map/end_kernel/pallas_call | solution.py:53
  103.6 0.0 copy-start.1
  103.6 0.0 copy-start.2
  103.6 13.7 %all_to_all.32.d_ref = f32[8,136,128]{2,1,0:T(8,128)S(1)} all-to-all(f32[8,136,128]{2,1,0:T(8,128)S(1)} %end_kernel.1), channel_id=1, replica_groups={{0,2,4,6,8,10,12,14},{16,18,20,22,24,26,28,30},{32,34,36,38,40,42,44,46..., dimensions={0} | all-to-all | bytes 1114112 | tf_op jit(solution)/shard_map/all_to_all | solution.py:436
  117.4 3.0 %key_kernel.1 = (bf16[256,1024]{1,0:T(8,128)(2,1)}, bf16[256,1024]{1,0:T(8,128)(2,1)}, f32[8,256]{1,0:T(8,128)}, f32[8,256]{1,0:T(8,128)}) custom-call(bf16[256,1024]{1,0:T(8,128)(2,1)S(1)} %copy-done.1, f32[8,256]{1,0:T(8,128)S(1)} %copy-done.2, bf16[8,256,128]{2,1,0:T(8,128)(2,1)S(1)} %copy-done.10, bf16[8,256,128]{2,1,0:T(8,128)(2,1)S(1)} %copy-done.7, ...), custom_call_target="tpu_custom_call" | custom-call | flops 2000000000 | bytes 7421952 | tf_op jit(solution)/shard_map/key_kernel/pallas_call | solution.py:53
  (19 shorter events, 0.0 us)
Async XLA Ops:
  4.9 20.3 %all-to-all-start = ((f32[8,128,256]{2,1,0:T(8,128)}), f32[8,128,256]{2,1,0:T(8,128)S(1)}, u32[]{:S(2)}, u32[]{:S(2)}) async-start(f32[8,128,256]{2,1,0:T(8,128)} %get-tuple-element.41), calls=%async_computation | async-start | bytes 2097152 | tf_op jit(solution)/shard_map/all_to_all | solution.py:436
  26.7 24.5 %copy-start.8 = (f32[6,128,256]{2,1,0:T(8,128)S(1)}, f32[6,128,256]{2,1,0:T(8,128)}, u32[]{:S(2)}) copy-start(f32[6,128,256]{2,1,0:T(8,128)} %get-tuple-element.43.tree_ref) | copy-start | bytes 2359300
  26.7 24.5 %copy-start.13 = (f32[128,128]{1,0:T(8,128)S(1)}, f32[128,128]{1,0:T(8,128)}, u32[]{:S(2)}) copy-start(f32[128,128]{1,0:T(8,128)} %get-tuple-element.45.init_ref) | copy-start | bytes 196612
  51.1 12.7 %copy-start.4 = (f32[8,256,128]{2,1,0:T(8,128)S(1)}, f32[8,256,128]{2,1,0:T(8,128)}, u32[]{:S(2)}) copy-start(f32[8,256,128]{2,1,0:T(8,128)} %get-tuple-element.40.c_ref) | copy-start | bytes 3145732
  51.7 12.2 %copy-start = (bf16[256,1024]{1,0:T(8,128)(2,1)S(1)}, bf16[256,1024]{1,0:T(8,128)(2,1)}, u32[]{:S(2)}) copy-start(bf16[256,1024]{1,0:T(8,128)(2,1)} %cot_ref.3) | copy-start | bytes 1572868
  51.7 12.2 %copy-start.12 = (bf16[8,256,128]{2,1,0:T(8,128)(2,1)S(1)}, bf16[8,256,128]{2,1,0:T(8,128)(2,1)}, u32[]{:S(2)}) copy-start(bf16[8,256,128]{2,1,0:T(8,128)(2,1)} %get-tuple-element.39.qt_ref) | copy-start | bytes 1572868
  63.9 0.7 copy-start.3
  64.6 1.9 %copy-start.11 = (bf16[8,128,256]{2,1,0:T(8,128)(2,1)S(1)}, bf16[8,128,256]{2,1,0:T(8,128)(2,1)}, u32[]{:S(2)}) copy-start(bf16[8,128,256]{2,1,0:T(8,128)(2,1)} %get-tuple-element.48.qtt_ref) | copy-start | bytes 1572868
  65.1 1.4 %collective-permute-start = (f32[256,128]{1,0:T(8,128)S(1)}, f32[256,128]{1,0:T(8,128)S(1)}, u32[]{:S(2)}, u32[]{:S(2)}) collective-permute-start(f32[256,128]{1,0:T(8,128)S(1)} %get-tuple-element.47.own_ref), channel_id=1, source_target_pairs={{0,1},{1,0},{2,3},{3,2},{4,5},{5,4},{6,7},{7,6},{8,9},{9,8},{10,11... | collective-permute-start | bytes 393224 | tf_op jit(solution)/shard_map/ppermute | solution.py:497
  68.3 13.5 %all-to-all-start.3 = ((f32[8,128,128]{2,1,0:T(8,128)}), f32[8,128,128]{2,1,0:T(8,128)S(1)}, u32[]{:S(2)}, u32[]{:S(2)}) async-start(f32[8,128,128]{2,1,0:T(8,128)} %get-tuple-element.60), calls=%async_computation.3 | async-start | bytes 1048576 | tf_op jit(solution)/shard_map/all_to_all | solution.py:436
  81.7 1.1 copy-start.9
  84.4 15.6 %all-to-all-start.4 = ((f32[8,128,128]{2,1,0:T(8,128)}), f32[8,128,128]{2,1,0:T(8,128)}, u32[]{:S(2)}, u32[]{:S(2)}) async-start(f32[8,128,128]{2,1,0:T(8,128)} %gather_kernel.1), calls=%async_computation.4 | async-start | bytes 1048576 | tf_op jit(solution)/shard_map/all_to_all | solution.py:436
  100.0 17.3 %copy-start.6 = (bf16[8,256,128]{2,1,0:T(8,128)(2,1)S(1)}, bf16[8,256,128]{2,1,0:T(8,128)(2,1)}, u32[]{:S(2)}) copy-start(bf16[8,256,128]{2,1,0:T(8,128)(2,1)} %get-tuple-element.56.dkp_ref) | copy-start | bytes 1572868
  100.0 17.3 %copy-start.7 = (bf16[8,256,128]{2,1,0:T(8,128)(2,1)S(1)}, bf16[8,256,128]{2,1,0:T(8,128)(2,1)}, u32[]{:S(2)}) copy-start(bf16[8,256,128]{2,1,0:T(8,128)(2,1)} %get-tuple-element.54.er_ref) | copy-start | bytes 1572868
  100.0 17.3 %copy-start.10 = (bf16[8,256,128]{2,1,0:T(8,128)(2,1)S(1)}, bf16[8,256,128]{2,1,0:T(8,128)(2,1)}, u32[]{:S(2)}) copy-start(bf16[8,256,128]{2,1,0:T(8,128)(2,1)} %get-tuple-element.53.tek_ref) | copy-start | bytes 1572868
  103.6 13.8 %copy-start.1 = (bf16[256,1024]{1,0:T(8,128)(2,1)S(1)}, bf16[256,1024]{1,0:T(8,128)(2,1)}, u32[]{:S(2)}) copy-start(bf16[256,1024]{1,0:T(8,128)(2,1)} %k_ref.5) | copy-start | bytes 1572868
  103.6 13.8 %copy-start.2 = (f32[8,256]{1,0:T(8,128)S(1)}, f32[8,256]{1,0:T(8,128)}, u32[]{:S(2)}) copy-start(f32[8,256]{1,0:T(8,128)} %e_ref.5) | copy-start | bytes 24580
  103.6 13.8 %copy-start.5 = (bf16[8,256,128]{2,1,0:T(8,128)(2,1)S(1)}, bf16[8,256,128]{2,1,0:T(8,128)(2,1)}, u32[]{:S(2)}) copy-start(bf16[8,256,128]{2,1,0:T(8,128)(2,1)} %get-tuple-element.55.u_ref) | copy-start | bytes 1572868

commit v2 on v1

--- a/solution.py
+++ b/solution.py
@@ -220,7 +220,8 @@
     return exact(halves(ab[:, :HEAD]), halves(w)) + ab[:, HEAD:]
 
 
-def start_kernel(ab_ref, tree_ref, groups_ref, init_ref, w_ref):
+def start_kernel(ab_ref, tree_ref, groups_ref, init_ref, gain_hbm, w_ref, gain_ref, sems):
+    weight = Copies(sems).start(gain_hbm, gain_ref)
     group = lax.axis_index("ctx") // GROUP
     w0 = lax.fori_loop(0, group, lambda g, w: apply_map(groups_ref[g], w), init_ref[...])
     w4 = apply_map(tree_ref[4], w0)
@@ -229,24 +230,22 @@
     for i, w in zip((0, 2, 4, 6), (w0, w2, w4, w6)):
         w_ref[i] = w
         w_ref[i + 1] = apply_map(ab_ref[i], w)
-
-
-def adjoint_kernel(ab_ref, groups_ref, inside_ref, after_ref, first_ref, token_ref):
+    weight.wait()
+
+
+def adjoint_kernel(groups_ref, after_ref, first_ref, token_ref):
     eye = (
         lax.broadcasted_iota(jnp.int32, (HEAD, HEAD), 0)
         == lax.broadcasted_iota(jnp.int32, (HEAD, HEAD), 1)
     ).astype(F32)
     token_ref[...] = jnp.zeros_like(token_ref)
-    inside = first = after = eye
+    first = after = eye
     group = lax.axis_index("ctx") // GROUP
     for i in range(GROUP):
-        own = GROUP - 1 - i
-        inside_ref[own] = inside
         first_ref[i] = first
         later = i > group
         after_ref[i] = jnp.where(later, after, 0.0)
         if i < GROUP - 1:
-            inside = exact(halves(ab_ref[own, :, :HEAD]), halves(inside), dot_tn)
             step = halves(groups_ref[i, :, :HEAD])
             first = exact(halves(first), step, dot_nt)
             after = jnp.where(later, exact(halves(after), step, dot_nt), eye)
@@ -296,86 +295,99 @@
 
 
 def query_kernel(
-    q_ref, k_ref, e_ref, tkv_ref, st_ref, w_ref, dz_ref,
-    dq_ref, u_ref, dk_ref, er_ref, token_ref,
+    q_hbm, k_hbm, e_hbm, tkv_hbm, st_hbm, dz_hbm, w_ref,
+    dq_hbm, u_hbm, dk_hbm, er_hbm, token_ref,
+    q_ref, k_ref, e_ref, tkv_ref, st_ref, dz_ref, dq_ref, u_ref, dk_ref, er_ref, sems,
 ):
     n = k_ref.shape[0]
     heads = e_ref.shape[0]
+    copies = Copies(sems)
+    rates = copies.start(e_hbm, e_ref)
+    arrivals = []
+    for first in range(0, heads, BATCH):
+        part = slice(first, first + BATCH)
+        flat = span(first, first + BATCH)
+        arrivals.append((
+            copies.start(tkv_hbm.at[part], tkv_ref.at[part]),
+            copies.start(dz_hbm.at[:, flat], dz_ref.at[:, flat]),
+            copies.start(k_hbm.at[:, flat], k_ref.at[:, flat]),
+            copies.start(q_hbm.at[:, flat], q_ref.at[:, flat]),
+            copies.start(st_hbm.at[part], st_ref.at[part]),
+        ))
     row = lax.broadcasted_iota(jnp.int32, (n, n), 0)
     col = lax.broadcasted_iota(jnp.int32, (n, n), 1)
     causal = row >= col
     token_ref[...] = jnp.zeros_like(token_ref)
-    for h in range(heads):
-        e = e_ref[h : h + 1, :]
-        w = low(w_ref[h])
-        dz = dz_ref[:, columns(h)]
-        r = dot(tkv_ref[h, :, :HEAD], w) - tkv_ref[h, :, HEAD:].astype(F32)
-        er = low(r * jnp.transpose(jnp.broadcast_to(e, (HEAD, n))))
-        er_ref[h] = er
-        ds = low(jnp.where(causal, -dot_nt(dz, er), 0.0))
-        dq_ref[:, columns(h)] = low(dot_nt(dz, w) + dot(ds, k_ref[:, columns(h)]))
-        dk_ref[h] = low(dot_tn(ds, q_ref[:, columns(h)]))
-        u_ref[h] = low(dot_tn(st_ref[h], dz))
+    rates.wait()
+    sent = []
+    for first, arrival in zip(range(0, heads, BATCH), arrivals):
+        batch = range(first, first + BATCH)
+        ws = [low(w_ref[h]) for h in batch]
+        rates_wide = [
+            jnp.transpose(jnp.broadcast_to(e_ref[h : h + 1, :], (HEAD, n))) for h in batch
+        ]
+        for copy in arrival:
+            copy.wait()
+        for h, w, wide in zip(batch, ws, rates_wide):
+            r = dot(tkv_ref[h, :, :HEAD], w) - tkv_ref[h, :, HEAD:].astype(F32)
+            er_ref[h] = low(r * wide)
+        dss = [
+            low(jnp.where(causal, -dot_nt(dz_ref[:, columns(h)], er_ref[h]), 0.0)) for h in batch
+        ]
+        for h, w, ds in zip(batch, ws, dss):
+            dq_ref[:, columns(h)] = low(
+                dot_nt(dz_ref[:, columns(h)], w) + dot(ds, k_ref[:, columns(h)])
+            )
+            dk_ref[h] = low(dot_tn(ds, q_ref[:, columns(h)]))
+            u_ref[h] = low(dot_tn(st_ref[h], dz_ref[:, columns(h)]))
+        part = slice(first, first + BATCH)
+        flat = span(first, first + BATCH)
+        sent.append(copies.start(dq_ref.at[:, flat], dq_hbm.at[:, flat]))
+        for source, target in ((u_ref, u_hbm), (dk_ref, dk_hbm), (er_ref, er_hbm)):
+            sent.append(copies.start(source.at[part], target.at[part]))
+    for copy in sent:
+        copy.wait()
 
 
 def transposed_map(a, later, own):
     return exact(halves(a), halves(later), dot_tn) + own
 
 
-def gather_kernel(ab_ref, tree_ref, g_ref, token_ref, all_hbm, whole_ref, sems):
+def gather_kernel(
+    ab_ref, tree_hbm, g_ref, query_token, adjoint_token, all_ref, sums_ref, tree_ref, sems
+):
+    tree = Copies(sems).start(tree_hbm.at[:, :, :HEAD], tree_ref)
     pairs = [
         transposed_map(ab_ref[2 * i, :, :HEAD], g_ref[2 * i + 1], g_ref[2 * i]) for i in range(4)
     ]
-    quads = [
-        transposed_map(tree_ref[2 * i, :, :HEAD], pairs[2 * i + 1], pairs[2 * i])
-        for i in range(2)
-    ]
-    whole_ref[...] = transposed_map(tree_ref[4, :, :HEAD], quads[1], quads[0])
-    broadcast(Copies(sems), whole_ref, all_hbm)
-
-
-def tail_kernel(ab_ref, g_ref, sums_ref):
-    tail = jnp.zeros((HEAD, HEAD), F32)
-    sums_ref[GROUP - 1] = tail
-    for i in range(GROUP - 1, 0, -1):
-        if i < GROUP - 1:
-            tail = transposed_map(ab_ref[i, :, :HEAD], tail, g_ref[i])
-        else:
-            tail = g_ref[i]
-        sums_ref[i - 1] = tail
+    tree.wait()
+    quads = [transposed_map(tree_ref[2 * i], pairs[2 * i + 1], pairs[2 * i]) for i in range(2)]
+    for i, a in enumerate(pairs + quads):
+        sums_ref[i] = a
+    whole = transposed_map(tree_ref[4], quads[1], quads[0])
+    for i in range(GROUP):
+        all_ref[i] = whole
 
 
 def end_kernel(
-    after_hbm, first_hbm, inside_hbm, sums_hbm, later_ref, d_ref,
-    init_ref, after_ref, first_ref, inside_ref, sums_ref, sems,
-):
-    copies = Copies(sems)
-    arrivals = [
-        copies.start(source, target)
-        for source, target in (
-            (after_hbm, after_ref), (first_hbm, first_ref), (inside_hbm, inside_ref),
-            (sums_hbm, sums_ref),
-        )
-    ]
+    after_ref, first_ref, ab_ref, tree_ref, g_ref, sums_ref, later_ref, d_ref, init_ref
+):
     parts = [halves(later_ref[g]) for g in range(GROUP)]
-    arrivals[0].wait()
-    end = exact(halves(after_ref[1]), parts[1])
+    d7 = exact(halves(after_ref[1]), parts[1])
     for g in range(2, GROUP):
-        end += exact(halves(after_ref[g]), parts[g])
-    arrivals[1].wait()
+        d7 += exact(halves(after_ref[g]), parts[g])
+    d3 = transposed_map(tree_ref[5, :, :HEAD], d7, sums_ref[5])
+    d5 = transposed_map(tree_ref[3, :, :HEAD], d7, sums_ref[3])
+    d1 = transposed_map(tree_ref[1, :, :HEAD], d3, sums_ref[1])
     start = later_ref[0]
     for g in range(1, GROUP):
         start += exact(halves(first_ref[g]), parts[g])
     init_ref[...] = start
-    ends = halves(end)
-    for copy in arrivals[2:]:
-        copy.wait()
     rows = init_ref[pl.ds(pl.multiple_of(lax.axis_index("ctx") // GROUP * 16, 16), 16), :]
+    for i, d in zip((7, 5, 3, 1), (d7, d5, d3, d1)):
+        d_ref[i, :HEAD, :] = d
+        d_ref[i - 1, :HEAD, :] = transposed_map(ab_ref[i, :, :HEAD], d, g_ref[i])
     for i in range(GROUP):
-        d = end
-        if i < GROUP - 1:
-            d = exact(halves(inside_ref[i]), ends) + sums_ref[i]
-        d_ref[i, :HEAD, :] = d
         d_ref[i, HEAD:, :] = jnp.zeros((8, HEAD), F32)
         d_ref[i, HEAD : HEAD + 2, :] = rows[2 * i : 2 * i + 2]
 
@@ -483,10 +495,11 @@
         copies=1,
     )
     group_maps = swap(sent, far)
-    (starts,) = call(
+    starts, gain_row = call(
         start_kernel,
-        [(square, F32, "v")],
-        [(own_maps, "v"), (tree, "v"), (group_maps, "v"), (own_init, "v")],
+        [(square, F32, "v"), ((1, width), F32, "v")],
+        [(own_maps, "v"), (tree, "v"), (group_maps, "v"), (own_init, "v"), (gain_row, "h")],
+        copies=1,
     )
     weights = swap(starts, near)
     hidden, stats = call(
@@ -506,35 +519,39 @@
         copies=2 + parts,
     )
     own_grads = swap(local_grad, near)
+    pair = (heads, n, 2 * HEAD)
     grad_queries, u, dk_part, scaled_residual, queried = call(
         query_kernel,
-        [(flat, BF16, "a"), (tall, BF16, "a"), (tall, BF16, "a"), (tall, BF16, "a"), token],
-        [
-            (queries, "a"), (keys, "a"), (rates, "a"), (tkv, "a"), (scores, "a"),
-            (weights, "v"), (dz, "a"),
-        ],
-    )
-    (sent,) = call(
+        [(flat, BF16, "h"), (tall, BF16, "h"), (tall, BF16, "h"), (tall, BF16, "h"), token],
+        [
+            (queries, "h"), (keys, "h"), (rates, "h"), (tkv, "h"), (scores, "h"), (dz, "h"),
+            (weights, "v"),
+        ],
+        [
+            vm(flat, BF16), vm(flat, BF16), vm((heads, n), F32), vm(pair, BF16), vm(full, BF16),
+            vm(flat, BF16), vm(flat, BF16), vm(tall, BF16), vm(tall, BF16), vm(tall, BF16),
+        ],
+        copies=1 + 9 * parts,
+    )
+    after, first, adjoint_ready = call(
+        adjoint_kernel, [(square, F32, "a"), (square, F32, "a"), token], [(group_maps, "v")]
+    )
+    sent, sums = call(
         gather_kernel,
-        [(square, F32, "h")],
-        [(own_maps, "v"), (tree, "v"), (own_grads, "v"), (queried, "v")],
-        [vm((HEAD, HEAD), F32)],
-        copies=GROUP,
+        [(square, F32, "v"), ((6, HEAD, HEAD), F32, "v")],
+        [(own_maps, "v"), (tree, "h"), (own_grads, "v"), (queried, "v"), (adjoint_ready, "v")],
+        [vm((6, HEAD, HEAD), F32)],
+        copies=1,
     )
     group_grads = swap(sent, far)
-    inside, after, first = call(
-        adjoint_kernel,
-        [(square, F32, "a"), (square, F32, "a"), (square, F32, "a"), token],
-        [(own_maps, "v"), (group_maps, "v")],
-    )[:3]
-    (sums,) = call(tail_kernel, [(square, F32, "a")], [(own_maps, "v"), (own_grads, "v")])
-    ending = (GROUP, HEAD + 8, HEAD)
     (ends,) = call(
         end_kernel,
-        [(ending, F32, "v")],
-        [(after, "h"), (first, "h"), (inside, "h"), (sums, "h"), (group_grads, "v")],
-        [vm((HEAD, HEAD), F32)] + [vm(square, F32)] * 4,
-        copies=4,
+        [((GROUP, HEAD + 8, HEAD), F32, "v")],
+        [
+            (after, "v"), (first, "v"), (own_maps, "v"), (tree, "v"), (own_grads, "v"),
+            (sums, "v"), (group_grads, "v"),
+        ],
+        [vm((HEAD, HEAD), F32)],
     )
     adjoint = swap(ends, near)
     grad_keys, grad_values, grad_rates, grad_init = call(

time: 121 us -> 116 us (0.959)
  blocking collectives: 50.3 us -> 65.3 us
  Pallas kernels: 35.4 us -> 28.9 us
  waiting for transfers between devices: 17.7 us -> 11.6 us
  starting transfers between devices: 14.2 us -> 9.09 us
  local copies, waits for them, and re-layouts: 1.87 us -> 0.07 us
    all_to_all x3 -> x4, blocking collectives: 50.3 us -> 65.3 us  [swap(): return lax.all_to_all(a, 'ctx', 0, 0, axis_index_groups=groups)]
    pallas_call x12 -> x11, Pallas kernels: 35.4 us -> 28.9 us  [call(): pl.pallas_call(kernel, out_shape=results, in_specs=[pl.BlockSpec(memory_s...]
    all_to_all x3 -> x2, waiting for transfers between devices: 16.4 us -> 10.3 us  [swap(): return lax.all_to_all(a, 'ctx', 0, 0, axis_index_groups=groups)]
    all_to_all x3 -> x2, starting transfers between devices: 14.1 us -> 9 us  [swap(): return lax.all_to_all(a, 'ctx', 0, 0, axis_index_groups=groups)]
    unnamed x28 -> x30, local copies, waits for them, and re-layouts: 1.87 us -> 0.07 us
  transfers between devices with their start and end apart: 4 -> 3, of which waited for: 4 -> 3; matrix products, arithmetic and copies ran while one was open for 0% -> 0% of each run, Pallas kernels for 16% -> 12%
where the time goes in v2:
time: 116 us
  blocking collectives  65.3 us (56%)
  Pallas kernels  28.9 us (25%)
  waiting for transfers between devices  11.6 us (10%)
  starting transfers between devices  9.09 us (8%)
    all_to_all x4, blocking collectives, swap(): return lax.all_to_all(a, 'ctx', 0, 0, axis_index_groups=groups)  65.3 us
    pallas_call x11, Pallas kernels, call(): pl.pallas_call(kernel, out_shape=results, in_specs=[pl.BlockSpec(memory_s...  28.9 us
    all_to_all x2, waiting for transfers between devices, swap(): return lax.all_to_all(a, 'ctx', 0, 0, axis_index_groups=groups)  10.3 us
    all_to_all x2, starting transfers between devices, swap(): return lax.all_to_all(a, 'ctx', 0, 0, axis_index_groups=groups)  9 us
  transfers between devices with their start and end apart: 3, of which 3 were waited for; matrix products, arithmetic and copies ran while one was open for 0% of the time, Pallas kernels for 12%

profile of v2, /device:TPU:0, one launch (start us, length us, event | category | flops | bytes accessed | tf_op | source)
XLA Modules:
  0.0 115.8 jit_solution(9419485109581545622)
XLA Ops:
  0.6 4.2 %map_kernel.1 = (f32[8,128,256]{2,1,0:T(8,128)}, bf16[8,2,128,128]{3,2,1,0:T(8,128)(2,1)}, bf16[8,128,128]{2,1,0:T(8,128)(2,1)}, bf16[8,256,256]{2,1,0:T(8,128)(2,1)}) custom-call(bf16[256,1024]{1,0:T(8,128)(2,1)} %k_ref.3, bf16[256,1024]{1,0:T(8,128)(2,1)} %v_hbm.1, f32[8,256]{1,0:T(8,128)} %e_ref.3), custom_call_target="tpu_custom_call" | custom-call | flops 2000000000 | bytes 2113536 | tf_op jit(solution)/shard_map/map_kernel/pallas_call | solution.py:53
  4.9 5.5 %all-to-all-start = ((f32[8,128,256]{2,1,0:T(8,128)}), f32[8,128,256]{2,1,0:T(8,128)S(1)}, u32[]{:S(2)}, u32[]{:S(2)}) async-start(f32[8,128,256]{2,1,0:T(8,128)} %get-tuple-element.45), calls=%async_computation | async-start | bytes 2097152 | tf_op jit(solution)/shard_map/all_to_all | solution.py:448
  10.4 7.4 %prepare_kernel.1 = (bf16[8,256,128]{2,1,0:T(8,128)(2,1)}, bf16[8,128,256]{2,1,0:T(8,128)(2,1)}, f32[8,256,128]{2,1,0:T(8,128)}, bf16[8,256,256]{2,1,0:T(8,128)(...) custom-call(bf16[256,1024]{1,0:T(8,128)(2,1)} %q_hbm.1, bf16[256,1024]{1,0:T(8,128)(2,1)} %k_ref.3, ...), custom_call_target="tpu_custom_call" | custom-call | flops 2000000000 | bytes 6832128 | tf_op jit(solution)/shard_map/prepare_kernel/pallas_call | solution.py:53
  17.8 7.4 %all-to-all-done.ab_ref = f32[8,128,256]{2,1,0:T(8,128)S(1)} async-done(((f32[8,128,256]{2,1,0:T(8,128)}), f32[8,128,256]{2,1,0:T(8,128)S(1)}, u32[]{:S(2)}, u32[]{:S(2)}) %all-to-all-start) | async-done | bytes 1048608 | tf_op jit(solution)/shard_map/all_to_all | solution.py:448
  25.2 1.5 %group_kernel.1 = (f32[8,128,256]{2,1,0:T(8,128)S(1)}, f32[6,128,256]{2,1,0:T(8,128)}) custom-call(f32[8,128,256]{2,1,0:T(8,128)S(1)} %all-to-all-done.ab_ref, f32[8,128]{1,0:T(8,128)S(1)} %get-tuple-element.46.token_ref), custom_call_target="tpu_custom_call" | custom-call | flops 2000000000 | bytes 2105344 | tf_op jit(solution)/shard_map/group_kernel/pallas_call | solution.py:53
  26.7 0.0 copy-start.3
  26.7 0.0 copy-start.14
  26.7 24.4 %all_to_all.30.groups_ref = f32[8,128,256]{2,1,0:T(8,128)S(1)} all-to-all(f32[8,128,256]{2,1,0:T(8,128)S(1)} %get-tuple-element.48), channel_id=1, replica_groups={{0,16,32,48,64,80,96,112},{2,18,34,50,66,82,98,114},{4,20,36,52,68,84,1..., dimensions={0} | all-to-all | bytes 2097152 | tf_op jit(solution)/shard_map/all_to_all | solution.py:448
  51.1 0.0 copy-done.3
  51.1 0.0 copy-done.14
  51.2 0.8 start_kernel.1
  51.9 0.0 copy-start
  52.0 0.0 copy-start.13
  52.0 12.2 %all_to_all.31.w_ref = f32[8,128,128]{2,1,0:T(8,128)S(1)} all-to-all(f32[8,128,128]{2,1,0:T(8,128)S(1)} %get-tuple-element.51), channel_id=1, replica_groups={{0,2,4,6,8,10,12,14},{16,18,20,22,24,26,28,30},{32,34,36,38,40,42,44,46..., dimensions={0} | all-to-all | bytes 1048576 | tf_op jit(solution)/shard_map/all_to_all | solution.py:448
  64.1 0.0 copy-done
  64.1 0.0 copy-start.12
  64.1 0.5 hidden_kernel.1
  64.6 0.1 collective-permute-start
  64.7 1.3 %collective-permute-done.other_ref = f32[256,128]{1,0:T(8,128)S(1)} collective-permute-done((f32[256,128]{1,0:T(8,128)S(1)}, f32[256,128]{1,0:T(8,128)S(1)}, u32[]{:S(2)}, u32[]{:S(2)}) %collective-permute-start) | collective-permute-done | bytes 131104 | tf_op jit(solution)/shard_map/ppermute | solution.py:510
  66.1 1.8 %norm_kernel.1 = (bf16[256,1024]{1,0:T(8,128)(2,1)}, bf16[256,1024]{1,0:T(8,128)(2,1)}, f32[8,128,128]{2,1,0:T(8,128)}) custom-call(f32[256,1024]{1,0:T(8,128)S(1)} %get-tuple-element.52.z_ref, bf16[256,1024]{1,0:T(8,128)(2,1)S(1)} %copy-done, f32[1,1024]{1,0:T(1,128)S(1)} %get-tuple-element.50.gain_ref, f32[256,128]{1,0:T(8,128)S(1)} %get-tuple-element.53.own_ref, ...), custom_call_target="tpu_custom_call" | custom-call | flops 2000000000 | bytes 4726784 | tf_op jit(solution)/shard_map/norm_kernel/pallas_call | solution.py:53
  67.8 3.5 %all-to-all-start.3 = ((f32[8,128,128]{2,1,0:T(8,128)}), f32[8,128,128]{2,1,0:T(8,128)S(1)}, u32[]{:S(2)}, u32[]{:S(2)}) async-start(f32[8,128,128]{2,1,0:T(8,128)} %get-tuple-element.65), calls=%async_computation.3 | async-start | bytes 1048576 | tf_op jit(solution)/shard_map/all_to_all | solution.py:448
  71.3 2.5 %adjoint_kernel.1 = (f32[8,128,128]{2,1,0:T(8,128)}, f32[8,128,128]{2,1,0:T(8,128)}, f32[8,128]{1,0:T(8,128)S(1)}) custom-call(f32[8,128,256]{2,1,0:T(8,128)S(1)} %all_to_all.30.groups_ref), custom_call_target="tpu_custom_call" | custom-call | flops 2000000000 | bytes 2097152 | tf_op jit(solution)/shard_map/adjoint_kernel/pallas_call | solution.py:53
  73.8 4.6 %query_kernel.1 = (bf16[256,1024]{1,0:T(8,128)(2,1)}, bf16[8,256,128]{2,1,0:T(8,128)(2,1)}, bf16[8,256,128]{2,1,0:T(8,128)(2,1)}, bf16[8,256,128]{2,1,0:T(8,128)(2,1)}, f32[8,128]{1,0:T(8,128)S(1)}) custom-call(bf16[256,1024]{1,0:T(8,128)(2,1)} %q_hbm.1, bf16[256,1024]{1,0:T(8,128)(2,1)} %k_ref.3, f32[8,256]{1,0:T(8,128)} %e_ref.3, ...), custom_call_target="tpu_custom_call" | custom-call | flops 2000000000 | bytes 8404992 | tf_op jit(solution)/shard_map/query_kernel/pallas_call | solution.py:53
  78.4 2.9 %all-to-all-done.3.g_ref = f32[8,128,128]{2,1,0:T(8,128)S(1)} async-done(((f32[8,128,128]{2,1,0:T(8,128)}), f32[8,128,128]{2,1,0:T(8,128)S(1)}, u32[]{:S(2)}, u32[]{:S(2)}) %all-to-all-start.3) | async-done | bytes 524320 | tf_op jit(solution)/shard_map/all_to_all | solution.py:448
  81.3 1.5 %gather_kernel.1 = (f32[8,128,128]{2,1,0:T(8,128)S(1)}, f32[6,128,128]{2,1,0:T(8,128)S(1)}) custom-call(f32[8,128,256]{2,1,0:T(8,128)S(1)} %all-to-all-done.ab_ref, f32[6,128,256]{2,1,0:T(8,128)} %get-tuple-element.47.tree_ref.tree_hbm, f32[8,128,128]{2,1,0:T(8,128)S(1)} %all-to-all-done.3.g_ref, f32[8,128]{1,0:T(8,128)S(1)} %get-tuple-element.66.query_token, ...), custom_call_target="tpu_custom_call" | custom-call | flops 2000000000 | bytes 4734976 | tf_op jit(solution)/shard_map/gather_kernel/pallas_call | solution.py:53
  82.9 15.2 %all_to_all.32.later_ref = f32[8,128,128]{2,1,0:T(8,128)S(1)} all-to-all(f32[8,128,128]{2,1,0:T(8,128)S(1)} %get-tuple-element.69), channel_id=1, replica_groups={{0,16,32,48,64,80,96,112},{2,18,34,50,66,82,98,114},{4,20,36,52,68,84,1..., dimensions={0} | all-to-all | bytes 1048576 | tf_op jit(solution)/shard_map/all_to_all | solution.py:448
  98.0 0.0 copy-done.6
  98.1 1.2 %end_kernel.1 = f32[8,136,128]{2,1,0:T(8,128)S(1)} custom-call(f32[8,128,128]{2,1,0:T(8,128)S(1)} %copy-done.5, f32[8,128,128]{2,1,0:T(8,128)S(1)} %copy-done.6, f32[8,128,256]{2,1,0:T(8,128)S(1)} %all-to-all-done.ab_ref, f32[6,128,256]{2,1,0:T(8,128)S(1)} %copy-done.4, f32[8,128,128]{2,1,0:T(8,128)S(1)} %all-to-all-done.3.g_ref, ...), custom_call_target="tpu_custom_call" | custom-call | flops 2000000000 | bytes 8650752 | tf_op jit(solution)/shard_map/end_kernel/pallas_call | solution.py:53
  99.3 0.0 copy-start.1
  99.3 0.0 copy-start.2
  99.3 13.5 %all_to_all.33.d_ref = f32[8,136,128]{2,1,0:T(8,128)S(1)} all-to-all(f32[8,136,128]{2,1,0:T(8,128)S(1)} %end_kernel.1), channel_id=1, replica_groups={{0,2,4,6,8,10,12,14},{16,18,20,22,24,26,28,30},{32,34,36,38,40,42,44,46..., dimensions={0} | all-to-all | bytes 1114112 | tf_op jit(solution)/shard_map/all_to_all | solution.py:448
  112.8 3.0 %key_kernel.1 = (bf16[256,1024]{1,0:T(8,128)(2,1)}, bf16[256,1024]{1,0:T(8,128)(2,1)}, f32[8,256]{1,0:T(8,128)}, f32[8,256]{1,0:T(8,128)}) custom-call(bf16[256,1024]{1,0:T(8,128)(2,1)S(1)} %copy-done.1, f32[8,256]{1,0:T(8,128)S(1)} %copy-done.2, bf16[8,256,128]{2,1,0:T(8,128)(2,1)S(1)} %copy-done.11, bf16[8,256,128]{2,1,0:T(8,128)(2,1)S(1)} %copy-done.10, ...), custom_call_target="tpu_custom_call" | custom-call | flops 2000000000 | bytes 7421952 | tf_op jit(solution)/shard_map/key_kernel/pallas_call | solution.py:53
  (19 shorter events, 0.0 us)
Async XLA Ops:
  4.9 20.3 %all-to-all-start = ((f32[8,128,256]{2,1,0:T(8,128)}), f32[8,128,256]{2,1,0:T(8,128)S(1)}, u32[]{:S(2)}, u32[]{:S(2)}) async-start(f32[8,128,256]{2,1,0:T(8,128)} %get-tuple-element.45), calls=%async_computation | async-start | bytes 2097152 | tf_op jit(solution)/shard_map/all_to_all | solution.py:448
  26.7 24.5 %copy-start.3 = (f32[6,128,256]{2,1,0:T(8,128)S(1)}, f32[6,128,256]{2,1,0:T(8,128)}, u32[]{:S(2)}) copy-start(f32[6,128,256]{2,1,0:T(8,128)} %get-tuple-element.47.tree_ref.tree_hbm) | copy-start | bytes 2359300
  26.7 24.5 %copy-start.14 = (f32[128,128]{1,0:T(8,128)S(1)}, f32[128,128]{1,0:T(8,128)}, u32[]{:S(2)}) copy-start(f32[128,128]{1,0:T(8,128)} %get-tuple-element.49.init_ref) | copy-start | bytes 196612
  51.1 13.0 %copy-start.7 = (f32[8,256,128]{2,1,0:T(8,128)S(1)}, f32[8,256,128]{2,1,0:T(8,128)}, u32[]{:S(2)}) copy-start(f32[8,256,128]{2,1,0:T(8,128)} %get-tuple-element.44.c_ref) | copy-start | bytes 3145732
  51.9 12.2 %copy-start = (bf16[256,1024]{1,0:T(8,128)(2,1)S(1)}, bf16[256,1024]{1,0:T(8,128)(2,1)}, u32[]{:S(2)}) copy-start(bf16[256,1024]{1,0:T(8,128)(2,1)} %cot_ref.3) | copy-start | bytes 1572868
  52.0 12.2 %copy-start.13 = (bf16[8,256,128]{2,1,0:T(8,128)(2,1)S(1)}, bf16[8,256,128]{2,1,0:T(8,128)(2,1)}, u32[]{:S(2)}) copy-start(bf16[8,256,128]{2,1,0:T(8,128)(2,1)} %get-tuple-element.43.qt_ref) | copy-start | bytes 1572868
  64.1 1.9 %copy-start.12 = (bf16[8,128,256]{2,1,0:T(8,128)(2,1)S(1)}, bf16[8,128,256]{2,1,0:T(8,128)(2,1)}, u32[]{:S(2)}) copy-start(bf16[8,128,256]{2,1,0:T(8,128)(2,1)} %get-tuple-element.54.qtt_ref) | copy-start | bytes 1572868
  64.6 1.4 %collective-permute-start = (f32[256,128]{1,0:T(8,128)S(1)}, f32[256,128]{1,0:T(8,128)S(1)}, u32[]{:S(2)}, u32[]{:S(2)}) collective-permute-start(f32[256,128]{1,0:T(8,128)S(1)} %get-tuple-element.53.own_ref), channel_id=1, source_target_pairs={{0,1},{1,0},{2,3},{3,2},{4,5},{5,4},{6,7},{7,6},{8,9},{9,8},{10,11... | collective-permute-start | bytes 393224 | tf_op jit(solution)/shard_map/ppermute | solution.py:510
  67.8 13.5 %all-to-all-start.3 = ((f32[8,128,128]{2,1,0:T(8,128)}), f32[8,128,128]{2,1,0:T(8,128)S(1)}, u32[]{:S(2)}, u32[]{:S(2)}) async-start(f32[8,128,128]{2,1,0:T(8,128)} %get-tuple-element.65), calls=%async_computation.3 | async-start | bytes 1048576 | tf_op jit(solution)/shard_map/all_to_all | solution.py:448
  81.3 16.7 %copy-start.5 = (f32[8,128,128]{2,1,0:T(8,128)S(1)}, f32[8,128,128]{2,1,0:T(8,128)}, u32[]{:S(2)}) copy-start(f32[8,128,128]{2,1,0:T(8,128)} %get-tuple-element.63.after_ref) | copy-start | bytes 1572868
  81.3 16.7 %copy-start.6 = (f32[8,128,128]{2,1,0:T(8,128)S(1)}, f32[8,128,128]{2,1,0:T(8,128)}, u32[]{:S(2)}) copy-start(f32[8,128,128]{2,1,0:T(8,128)} %get-tuple-element.64.first_ref) | copy-start | bytes 1572868
  82.8 15.2 %copy-start.4 = (f32[6,128,256]{2,1,0:T(8,128)S(1)}, f32[6,128,256]{2,1,0:T(8,128)}, u32[]{:S(2)}) copy-start(f32[6,128,256]{2,1,0:T(8,128)} %get-tuple-element.47.tree_ref.tree_hbm) | copy-start | bytes 2359300
  98.0 14.8 %copy-start.9 = (bf16[8,256,128]{2,1,0:T(8,128)(2,1)S(1)}, bf16[8,256,128]{2,1,0:T(8,128)(2,1)}, u32[]{:S(2)}) copy-start(bf16[8,256,128]{2,1,0:T(8,128)(2,1)} %get-tuple-element.62.dkp_ref) | copy-start | bytes 1572868
  98.1 14.8 %copy-start.10 = (bf16[8,256,128]{2,1,0:T(8,128)(2,1)S(1)}, bf16[8,256,128]{2,1,0:T(8,128)(2,1)}, u32[]{:S(2)}) copy-start(bf16[8,256,128]{2,1,0:T(8,128)(2,1)} %get-tuple-element.60.er_ref) | copy-start | bytes 1572868
  98.1 14.7 %copy-start.11 = (bf16[8,256,128]{2,1,0:T(8,128)(2,1)S(1)}, bf16[8,256,128]{2,1,0:T(8,128)(2,1)}, u32[]{:S(2)}) copy-start(bf16[8,256,128]{2,1,0:T(8,128)(2,1)} %get-tuple-element.59.tek_ref) | copy-start | bytes 1572868
  99.3 13.5 %copy-start.1 = (bf16[256,1024]{1,0:T(8,128)(2,1)S(1)}, bf16[256,1024]{1,0:T(8,128)(2,1)}, u32[]{:S(2)}) copy-start(bf16[256,1024]{1,0:T(8,128)(2,1)} %k_ref.3) | copy-start | bytes 1572868
  99.3 13.5 %copy-start.2 = (f32[8,256]{1,0:T(8,128)S(1)}, f32[8,256]{1,0:T(8,128)}, u32[]{:S(2)}) copy-start(f32[8,256]{1,0:T(8,128)} %e_ref.3) | copy-start | bytes 24580
  99.3 13.5 %copy-start.8 = (bf16[8,256,128]{2,1,0:T(8,128)(2,1)S(1)}, bf16[8,256,128]{2,1,0:T(8,128)(2,1)}, u32[]{:S(2)}) copy-start(bf16[8,256,128]{2,1,0:T(8,128)(2,1)} %get-tuple-element.61.u_ref) | copy-start | bytes 1572868

commit v3 on v2

--- a/solution.py
+++ b/solution.py
@@ -9,6 +9,7 @@
 MB = 16
 EPSILON = 1e-06
 GROUP = 8
+PLANES = 4
 F32 = jnp.float32
 BF16 = jnp.bfloat16
 
@@ -203,27 +204,42 @@
         copy.wait()
 
 
-def group_kernel(ab_ref, token_ref, all_ref, tree_hbm, tree_ref, sems):
+def level():
+    group = lax.axis_index("ctx") // GROUP
+    return group // 2, group % 2
+
+
+def group_kernel(ab_ref, token_ref, whole_ref, tree_hbm, tree_ref, sems):
     copies = Copies(sems)
     pairs = [compose(ab_ref[2 * i], ab_ref[2 * i + 1]) for i in range(4)]
     quads = [compose(pairs[2 * i], pairs[2 * i + 1]) for i in range(2)]
     for i, a in enumerate(pairs + quads):
         tree_ref[i] = a
     tree = copies.start(tree_ref, tree_hbm)
-    whole = compose(quads[0], quads[1])
-    for i in range(GROUP):
-        all_ref[i] = whole
+    whole_ref[...] = compose(quads[0], quads[1])
     tree.wait()
+
+
+def pair_kernel(own_ref, other_ref, all_ref):
+    _, late = level()
+    own, other = own_ref[...], other_ref[...]
+    early = jnp.where(late == 1, other, own)
+    pair = compose(early, jnp.where(late == 1, own, other))
+    for i in range(PLANES):
+        all_ref[i] = pair
 
 
 def apply_map(ab, w):
     return exact(halves(ab[:, :HEAD]), halves(w)) + ab[:, HEAD:]
 
 
-def start_kernel(ab_ref, tree_ref, groups_ref, init_ref, gain_hbm, w_ref, gain_ref, sems):
+def start_kernel(
+    ab_ref, tree_ref, pairs_ref, other_ref, init_ref, gain_hbm, w_ref, gain_ref, sems
+):
     weight = Copies(sems).start(gain_hbm, gain_ref)
-    group = lax.axis_index("ctx") // GROUP
-    w0 = lax.fori_loop(0, group, lambda g, w: apply_map(groups_ref[g], w), init_ref[...])
+    plane, late = level()
+    w0 = lax.fori_loop(0, plane, lambda z, w: apply_map(pairs_ref[z], w), init_ref[...])
+    w0 = lax.fori_loop(0, late, lambda _, w: apply_map(other_ref[...], w), w0)
     w4 = apply_map(tree_ref[4], w0)
     w2 = apply_map(tree_ref[0], w0)
     w6 = apply_map(tree_ref[2], w4)
@@ -233,20 +249,27 @@
     weight.wait()
 
 
-def adjoint_kernel(groups_ref, after_ref, first_ref, token_ref):
+def adjoint_kernel(
+    pairs_ref, ab_ref, tree_ref, other_ref, after_ref, first_ref, early_ref, up_ref
+):
     eye = (
         lax.broadcasted_iota(jnp.int32, (HEAD, HEAD), 0)
         == lax.broadcasted_iota(jnp.int32, (HEAD, HEAD), 1)
     ).astype(F32)
-    token_ref[...] = jnp.zeros_like(token_ref)
     first = after = eye
-    group = lax.axis_index("ctx") // GROUP
-    for i in range(GROUP):
-        first_ref[i] = first
-        later = i > group
-        after_ref[i] = jnp.where(later, after, 0.0)
-        if i < GROUP - 1:
-            step = halves(groups_ref[i, :, :HEAD])
+    plane, late = level()
+    own = exact(halves(tree_ref[5, :, :HEAD]), halves(tree_ref[4, :, :HEAD]))
+    early_ref[...] = jnp.transpose(jnp.where(late == 1, other_ref[:, :HEAD], own))
+    for i in range(4):
+        up_ref[i] = jnp.transpose(ab_ref[2 * i, :, :HEAD])
+    for i, a in enumerate((0, 2, 4)):
+        up_ref[4 + i] = jnp.transpose(tree_ref[a, :, :HEAD])
+    for z in range(PLANES):
+        first_ref[z] = first
+        later = z > plane
+        after_ref[z] = jnp.where(later, after, 0.0)
+        if z < PLANES - 1:
+            step = halves(pairs_ref[z, :, :HEAD])
             first = exact(halves(first), step, dot_nt)
             after = jnp.where(later, exact(halves(after), step, dot_nt), eye)
 
@@ -353,35 +376,45 @@
     return exact(halves(a), halves(later), dot_tn) + own
 
 
-def gather_kernel(
-    ab_ref, tree_hbm, g_ref, query_token, adjoint_token, all_ref, sums_ref, tree_ref, sems
-):
-    tree = Copies(sems).start(tree_hbm.at[:, :, :HEAD], tree_ref)
-    pairs = [
-        transposed_map(ab_ref[2 * i, :, :HEAD], g_ref[2 * i + 1], g_ref[2 * i]) for i in range(4)
-    ]
-    tree.wait()
-    quads = [transposed_map(tree_ref[2 * i], pairs[2 * i + 1], pairs[2 * i]) for i in range(2)]
+def turned_map(a, later, own):
+    return exact(halves(a), halves(later)) + own
+
+
+def gather_kernel(up_ref, g_ref, token_ref, whole_ref, sums_ref):
+    pairs = [turned_map(up_ref[i], g_ref[2 * i + 1], g_ref[2 * i]) for i in range(4)]
+    quads = [turned_map(up_ref[4 + i], pairs[2 * i + 1], pairs[2 * i]) for i in range(2)]
     for i, a in enumerate(pairs + quads):
         sums_ref[i] = a
-    whole = transposed_map(tree_ref[4], quads[1], quads[0])
-    for i in range(GROUP):
-        all_ref[i] = whole
+    whole_ref[...] = turned_map(up_ref[6], quads[1], quads[0])
+
+
+def pair_gradient_kernel(early_ref, own_ref, other_ref, all_ref):
+    _, late = level()
+    own, other = own_ref[...], other_ref[...]
+    pair = turned_map(
+        early_ref[...], jnp.where(late == 1, own, other), jnp.where(late == 1, other, own)
+    )
+    for i in range(PLANES):
+        all_ref[i] = pair
 
 
 def end_kernel(
-    after_ref, first_ref, ab_ref, tree_ref, g_ref, sums_ref, later_ref, d_ref, init_ref
-):
-    parts = [halves(later_ref[g]) for g in range(GROUP)]
-    d7 = exact(halves(after_ref[1]), parts[1])
-    for g in range(2, GROUP):
-        d7 += exact(halves(after_ref[g]), parts[g])
+    after_ref, first_ref, ab_ref, tree_ref, g_ref, sums_ref, other_map_ref, other_ref, later_ref,
+    d_ref, init_ref,
+):
+    parts = [halves(later_ref[z]) for z in range(PLANES)]
+    _, late = level()
+    end = exact(halves(after_ref[1]), parts[1])
+    for z in range(2, PLANES):
+        end += exact(halves(after_ref[z]), parts[z])
+    inner = transposed_map(other_map_ref[:, :HEAD], end, other_ref[...])
+    d7 = jnp.where(late == 1, end, inner)
     d3 = transposed_map(tree_ref[5, :, :HEAD], d7, sums_ref[5])
     d5 = transposed_map(tree_ref[3, :, :HEAD], d7, sums_ref[3])
     d1 = transposed_map(tree_ref[1, :, :HEAD], d3, sums_ref[1])
     start = later_ref[0]
-    for g in range(1, GROUP):
-        start += exact(halves(first_ref[g]), parts[g])
+    for z in range(1, PLANES):
+        start += exact(halves(first_ref[z]), parts[z])
     init_ref[...] = start
     rows = init_ref[pl.ds(pl.multiple_of(lax.axis_index("ctx") // GROUP * 16, 16), 16), :]
     for i, d in zip((7, 5, 3, 1), (d7, d5, d3, d1)):
@@ -441,7 +474,9 @@
     heads = width // HEAD
     count = lax.axis_size("ctx") // GROUP
     near = [[g * GROUP + i for i in range(GROUP)] for g in range(count)]
-    far = [[g * GROUP + i for g in range(count)] for i in range(GROUP)]
+    stride = 2 * GROUP
+    far = [[z * stride + i for z in range(PLANES)] for i in range(stride)]
+    across = [(i, i + GROUP if i % stride < GROUP else i - GROUP) for i in range(count * GROUP)]
     gain_row = gain.reshape(1, width)
 
     def swap(a, groups):
@@ -487,18 +522,29 @@
         ],
         copies=1,
     )
-    sent, tree = call(
+    slab = (HEAD, 2 * HEAD)
+    block = (HEAD, HEAD)
+    whole, tree = call(
         group_kernel,
-        [(wide, F32, "v"), (branches, F32, "h")],
+        [(slab, F32, "v"), (branches, F32, "h")],
         [(own_maps, "v"), (prepared, "v")],
         [vm(branches, F32)],
         copies=1,
     )
-    group_maps = swap(sent, far)
+    other_map = lax.ppermute(whole, "ctx", across)
+    (sent,) = call(
+        pair_kernel,
+        [((PLANES, HEAD, 2 * HEAD), F32, "v")],
+        [(whole, "v"), (other_map, "v")],
+    )
+    pair_maps = swap(sent, far)
     starts, gain_row = call(
         start_kernel,
         [(square, F32, "v"), ((1, width), F32, "v")],
-        [(own_maps, "v"), (tree, "v"), (group_maps, "v"), (own_init, "v"), (gain_row, "h")],
+        [
+            (own_maps, "v"), (tree, "v"), (pair_maps, "v"), (other_map, "v"), (own_init, "v"),
+            (gain_row, "h"),
+        ],
         copies=1,
     )
     weights = swap(starts, near)
@@ -533,25 +579,32 @@
         ],
         copies=1 + 9 * parts,
     )
-    after, first, adjoint_ready = call(
-        adjoint_kernel, [(square, F32, "a"), (square, F32, "a"), token], [(group_maps, "v")]
-    )
-    sent, sums = call(
+    steps = (PLANES, HEAD, HEAD)
+    after, first, early, up = call(
+        adjoint_kernel,
+        [(steps, F32, "a"), (steps, F32, "a"), (block, F32, "a"), ((7, HEAD, HEAD), F32, "v")],
+        [(pair_maps, "v"), (own_maps, "v"), (tree, "a"), (other_map, "v")],
+    )
+    whole, sums = call(
         gather_kernel,
-        [(square, F32, "v"), ((6, HEAD, HEAD), F32, "v")],
-        [(own_maps, "v"), (tree, "h"), (own_grads, "v"), (queried, "v"), (adjoint_ready, "v")],
-        [vm((6, HEAD, HEAD), F32)],
-        copies=1,
-    )
-    group_grads = swap(sent, far)
+        [(block, F32, "v"), ((6, HEAD, HEAD), F32, "v")],
+        [(up, "v"), (own_grads, "v"), (queried, "v")],
+    )
+    other_grad = lax.ppermute(whole, "ctx", across)
+    (sent,) = call(
+        pair_gradient_kernel,
+        [(steps, F32, "v")],
+        [(early, "v"), (whole, "v"), (other_grad, "v")],
+    )
+    pair_grads = swap(sent, far)
     (ends,) = call(
         end_kernel,
         [((GROUP, HEAD + 8, HEAD), F32, "v")],
         [
             (after, "v"), (first, "v"), (own_maps, "v"), (tree, "v"), (own_grads, "v"),
-            (sums, "v"), (group_grads, "v"),
-        ],
-        [vm((HEAD, HEAD), F32)],
+            (sums, "v"), (other_map, "v"), (other_grad, "v"), (pair_grads, "v"),
+        ],
+        [vm(block, F32)],
     )
     adjoint = swap(ends, near)
     grad_keys, grad_values, grad_rates, grad_init = call(

time: 116 us -> 111 us (0.957)
  blocking collectives: 65.3 us -> 48.3 us
  waiting for transfers between devices: 11.6 us -> 18.3 us
  starting transfers between devices: 9.09 us -> 14.7 us
    all_to_all x4, blocking collectives: 65.3 us -> 48.3 us  [swap(): return lax.all_to_all(a, 'ctx', 0, 0, axis_index_groups=groups)]
    ppermute x0 -> x2, waiting for transfers between devices: none -> 6.89 us  [the longest x1 3.84 us: local(): other_map = lax.ppermute(whole, 'ctx', across)]
    ppermute x0 -> x2, starting transfers between devices: none -> 5.61 us  [the longest x1 2.81 us: local(): other_map = lax.ppermute(whole, 'ctx', across)]
    pallas_call x11 -> x13, Pallas kernels: 28.9 us -> 28.4 us  [call(): pl.pallas_call(kernel, out_shape=results, in_specs=[pl.BlockSpec(memory_s...]
  transfers between devices with their start and end apart: 3 -> 5, of which waited for: 3 -> 5; matrix products, arithmetic and copies ran while one was open for 0% -> 0% of each run, Pallas kernels for 12% -> 13%
where the time goes in v3:
time: 111 us
  blocking collectives  48.3 us (44%)
  Pallas kernels  28.4 us (26%)
  waiting for transfers between devices  18.3 us (16%)
  starting transfers between devices  14.7 us (13%)
    all_to_all x4, blocking collectives, swap(): return lax.all_to_all(a, 'ctx', 0, 0, axis_index_groups=groups)  48.3 us
    pallas_call x13, Pallas kernels, call(): pl.pallas_call(kernel, out_shape=results, in_specs=[pl.BlockSpec(memory_s...  28.4 us
    all_to_all x2, waiting for transfers between devices, swap(): return lax.all_to_all(a, 'ctx', 0, 0, axis_index_groups=groups)  10.1 us
    all_to_all x2, starting transfers between devices, swap(): return lax.all_to_all(a, 'ctx', 0, 0, axis_index_groups=groups)  9 us
    ppermute x1, waiting for transfers between devices, local(): other_map = lax.ppermute(whole, 'ctx', across)  3.84 us
    ppermute x1, waiting for transfers between devices, local(): other_grad = lax.ppermute(whole, 'ctx', across)  3.06 us
    ppermute x1, starting transfers between devices, local(): other_map = lax.ppermute(whole, 'ctx', across)  2.81 us
    ppermute x1, starting transfers between devices, local(): other_grad = lax.ppermute(whole, 'ctx', across)  2.79 us
  transfers between devices with their start and end apart: 5, of which 5 were waited for; matrix products, arithmetic and copies ran while one was open for 0% of the time, Pallas kernels for 13%

profile of v3, /device:TPU:0, one launch (start us, length us, event | category | flops | bytes accessed | tf_op | source)
XLA Modules:
  0.0 110.8 jit_solution(16305160920124765555)
XLA Ops:
  0.6 4.2 %map_kernel.1 = (f32[8,128,256]{2,1,0:T(8,128)}, bf16[8,2,128,128]{3,2,1,0:T(8,128)(2,1)}, bf16[8,128,128]{2,1,0:T(8,128)(2,1)}, bf16[8,256,256]{2,1,0:T(8,128)(2,1)}) custom-call(bf16[256,1024]{1,0:T(8,128)(2,1)} %k_ref.3, bf16[256,1024]{1,0:T(8,128)(2,1)} %v_hbm.1, f32[8,256]{1,0:T(8,128)} %e_ref.3), custom_call_target="tpu_custom_call" | custom-call | flops 2000000000 | bytes 2113536 | tf_op jit(solution)/shard_map/map_kernel/pallas_call | solution.py:54
  4.9 5.5 %all-to-all-start = ((f32[8,128,256]{2,1,0:T(8,128)}), f32[8,128,256]{2,1,0:T(8,128)S(1)}, u32[]{:S(2)}, u32[]{:S(2)}) async-start(f32[8,128,256]{2,1,0:T(8,128)} %get-tuple-element.46), calls=%async_computation | async-start | bytes 2097152 | tf_op jit(solution)/shard_map/all_to_all | solution.py:483
  10.4 7.4 %prepare_kernel.1 = (bf16[8,256,128]{2,1,0:T(8,128)(2,1)}, bf16[8,128,256]{2,1,0:T(8,128)(2,1)}, f32[8,256,128]{2,1,0:T(8,128)}, bf16[8,256,256]{2,1,0:T(8,128)(...) custom-call(bf16[256,1024]{1,0:T(8,128)(2,1)} %q_hbm.1, bf16[256,1024]{1,0:T(8,128)(2,1)} %k_ref.3, ...), custom_call_target="tpu_custom_call" | custom-call | flops 2000000000 | bytes 6832128 | tf_op jit(solution)/shard_map/prepare_kernel/pallas_call | solution.py:54
  17.8 7.4 %all-to-all-done.ab_ref = f32[8,128,256]{2,1,0:T(8,128)S(1)} async-done(((f32[8,128,256]{2,1,0:T(8,128)}), f32[8,128,256]{2,1,0:T(8,128)S(1)}, u32[]{:S(2)}, u32[]{:S(2)}) %all-to-all-start) | async-done | bytes 1048608 | tf_op jit(solution)/shard_map/all_to_all | solution.py:483
  25.2 1.5 %group_kernel.1 = (f32[128,256]{1,0:T(8,128)S(1)}, f32[6,128,256]{2,1,0:T(8,128)}) custom-call(f32[8,128,256]{2,1,0:T(8,128)S(1)} %all-to-all-done.ab_ref, f32[8,128]{1,0:T(8,128)S(1)} %get-tuple-element.47.token_ref), custom_call_target="tpu_custom_call" | custom-call | flops 2000000000 | bytes 2105344 | tf_op jit(solution)/shard_map/group_kernel/pallas_call | solution.py:54
  26.7 2.8 %collective-permute-start = (f32[128,256]{1,0:T(8,128)S(1)}, f32[128,256]{1,0:T(8,128)S(1)}, u32[]{:S(2)}, u32[]{:S(2)}) collective-permute-start(f32[128,256]{1,0:T(8,128)S(1)} %get-tuple-element.49.own_ref), channel_id=1, source_target_pairs={{0,16},{2,18},{4,20},{6,22},{8,24},{10,26},{12,28},{14,30},{16,0},... | collective-permute-start | bytes 393224 | tf_op jit(solution)/shard_map/ppermute | solution.py:534
  29.5 3.8 %collective-permute-done.other_ref.other_map_ref = f32[128,256]{1,0:T(8,128)S(1)} collective-permute-done((f32[128,256]{1,0:T(8,128)S(1)}, f32[128,256]{1,0:T(8,128)S(1)}, u32[]{:S(2)}, u32[]{:S(2)}) %collective-permute-start) | collective-permute-done | bytes 131104 | tf_op jit(solution)/shard_map/ppermute | solution.py:534
  33.3 0.2 pair_kernel.1
  33.6 13.6 %all_to_all.30.pairs_ref = f32[4,128,256]{2,1,0:T(8,128)S(1)} all-to-all(f32[4,128,256]{2,1,0:T(8,128)S(1)} %pair_kernel.1), channel_id=1, replica_groups={{0,32,64,96},{2,34,66,98},{4,36,68,100},{6,38,70,102},{8,40,72,104},{10..., dimensions={0} | all-to-all | bytes 1048576 | tf_op jit(solution)/shard_map/all_to_all | solution.py:483
  47.2 0.8 start_kernel.1
  48.0 0.0 copy-start
  48.0 0.0 copy-start.11
  48.0 13.0 %all_to_all.31.w_ref = f32[8,128,128]{2,1,0:T(8,128)S(1)} all-to-all(f32[8,128,128]{2,1,0:T(8,128)S(1)} %get-tuple-element.52), channel_id=1, replica_groups={{0,2,4,6,8,10,12,14},{16,18,20,22,24,26,28,30},{32,34,36,38,40,42,44,46..., dimensions={0} | all-to-all | bytes 1048576 | tf_op jit(solution)/shard_map/all_to_all | solution.py:483
  61.0 0.0 copy-start.10
  61.0 0.5 hidden_kernel.1
  61.5 0.1 collective-permute-start.1
  61.6 1.3 %collective-permute-done.1.other_ref = f32[256,128]{1,0:T(8,128)S(1)} collective-permute-done((f32[256,128]{1,0:T(8,128)S(1)}, f32[256,128]{1,0:T(8,128)S(1)}, u32[]{:S(2)}, u32[]{:S(2)}) %collective-permute-start.1) | collective-permute-done | bytes 131104 | tf_op jit(solution)/shard_map/ppermute | solution.py:556
  62.9 1.8 %norm_kernel.1 = (bf16[256,1024]{1,0:T(8,128)(2,1)}, bf16[256,1024]{1,0:T(8,128)(2,1)}, f32[8,128,128]{2,1,0:T(8,128)}) custom-call(f32[256,1024]{1,0:T(8,128)S(1)} %get-tuple-element.53.z_ref, bf16[256,1024]{1,0:T(8,128)(2,1)S(1)} %copy-done, f32[1,1024]{1,0:T(1,128)S(1)} %get-tuple-element.51.gain_ref, f32[256,128]{1,0:T(8,128)S(1)} %get-tuple-element.54.own_ref, ...), custom_call_target="tpu_custom_call" | custom-call | flops 2000000000 | bytes 4726784 | tf_op jit(solution)/shard_map/norm_kernel/pallas_call | solution.py:54
  64.7 3.5 %all-to-all-start.3 = ((f32[8,128,128]{2,1,0:T(8,128)}), f32[8,128,128]{2,1,0:T(8,128)S(1)}, u32[]{:S(2)}, u32[]{:S(2)}) async-start(f32[8,128,128]{2,1,0:T(8,128)} %get-tuple-element.66), calls=%async_computation.3 | async-start | bytes 1048576 | tf_op jit(solution)/shard_map/all_to_all | solution.py:483
  68.2 2.6 %adjoint_kernel.1 = (f32[4,128,128]{2,1,0:T(8,128)}, f32[4,128,128]{2,1,0:T(8,128)}, f32[128,128]{1,0:T(8,128)}, f32[7,128,128]{2,1,0:T(8,128)S(1)}) custom-call(f32[4,128,256]{2,1,0:T(8,128)S(1)} %all_to_all.30.pairs_ref, f32[8,128,256]{2,1,0:T(8,128)S(1)} %all-to-all-done.ab_ref, f32[6,128,256]{2,1,0:T(8,128)} %get-tuple-element.48.tree_ref, ...), custom_call_target="tpu_custom_call" | custom-call | flops 2000000000 | bytes 4980736 | tf_op jit(solution)/shard_map/adjoint_kernel/pallas_call | solution.py:54
  70.9 4.6 %query_kernel.1 = (bf16[256,1024]{1,0:T(8,128)(2,1)}, bf16[8,256,128]{2,1,0:T(8,128)(2,1)}, bf16[8,256,128]{2,1,0:T(8,128)(2,1)}, bf16[8,256,128]{2,1,0:T(8,128)(2,1)}, f32[8,128]{1,0:T(8,128)S(1)}) custom-call(bf16[256,1024]{1,0:T(8,128)(2,1)} %q_hbm.1, bf16[256,1024]{1,0:T(8,128)(2,1)} %k_ref.3, f32[8,256]{1,0:T(8,128)} %e_ref.3, ...), custom_call_target="tpu_custom_call" | custom-call | flops 2000000000 | bytes 8404992 | tf_op jit(solution)/shard_map/query_kernel/pallas_call | solution.py:54
  75.4 2.7 %all-to-all-done.3.g_ref = f32[8,128,128]{2,1,0:T(8,128)S(1)} async-done(((f32[8,128,128]{2,1,0:T(8,128)}), f32[8,128,128]{2,1,0:T(8,128)S(1)}, u32[]{:S(2)}, u32[]{:S(2)}) %all-to-all-start.3) | async-done | bytes 524320 | tf_op jit(solution)/shard_map/all_to_all | solution.py:483
  78.2 0.6 gather_kernel.1
  78.8 2.8 %collective-permute-start.2 = (f32[128,128]{1,0:T(8,128)S(1)}, f32[128,128]{1,0:T(8,128)S(1)}, u32[]{:S(2)}, u32[]{:S(2)}) collective-permute-start(f32[128,128]{1,0:T(8,128)S(1)} %get-tuple-element.70.own_ref), channel_id=1, source_target_pairs={{0,16},{2,18},{4,20},{6,22},{8,24},{10,26},{12,28},{14,30},{16,0},... | collective-permute-start | bytes 196616 | tf_op jit(solution)/shard_map/ppermute | solution.py:593
  81.6 3.1 %collective-permute-done.2.other_ref = f32[128,128]{1,0:T(8,128)S(1)} collective-permute-done((f32[128,128]{1,0:T(8,128)S(1)}, f32[128,128]{1,0:T(8,128)S(1)}, u32[]{:S(2)}, u32[]{:S(2)}) %collective-permute-start.2) | collective-permute-done | bytes 65568 | tf_op jit(solution)/shard_map/ppermute | solution.py:593
  84.6 0.2 pair_gradient_kernel.1
  84.9 9.4 %all_to_all.32.later_ref = f32[4,128,128]{2,1,0:T(8,128)S(1)} all-to-all(f32[4,128,128]{2,1,0:T(8,128)S(1)} %pair_gradient_kernel.1), channel_id=1, replica_groups={{0,32,64,96},{2,34,66,98},{4,36,68,100},{6,38,70,102},{8,40,72,104},{10..., dimensions={0} | all-to-all | bytes 524288 | tf_op jit(solution)/shard_map/all_to_all | solution.py:483
  94.3 1.0 end_kernel.1
  95.2 0.0 copy-start.1
  95.2 0.0 copy-start.2
  95.3 12.4 %all_to_all.33.d_ref = f32[8,136,128]{2,1,0:T(8,128)S(1)} all-to-all(f32[8,136,128]{2,1,0:T(8,128)S(1)} %end_kernel.1), channel_id=1, replica_groups={{0,2,4,6,8,10,12,14},{16,18,20,22,24,26,28,30},{32,34,36,38,40,42,44,46..., dimensions={0} | all-to-all | bytes 1114112 | tf_op jit(solution)/shard_map/all_to_all | solution.py:483
  107.7 3.0 %key_kernel.1 = (bf16[256,1024]{1,0:T(8,128)(2,1)}, bf16[256,1024]{1,0:T(8,128)(2,1)}, f32[8,256]{1,0:T(8,128)}, f32[8,256]{1,0:T(8,128)}) custom-call(bf16[256,1024]{1,0:T(8,128)(2,1)S(1)} %copy-done.1, f32[8,256]{1,0:T(8,128)S(1)} %copy-done.2, bf16[8,256,128]{2,1,0:T(8,128)(2,1)S(1)} %copy-done.9, bf16[8,256,128]{2,1,0:T(8,128)(2,1)S(1)} %copy-done.8, ...), custom_call_target="tpu_custom_call" | custom-call | flops 2000000000 | bytes 7421952 | tf_op jit(solution)/shard_map/key_kernel/pallas_call | solution.py:54
  (27 shorter events, 0.1 us)
Async XLA Ops:
  4.9 20.3 %all-to-all-start = ((f32[8,128,256]{2,1,0:T(8,128)}), f32[8,128,256]{2,1,0:T(8,128)S(1)}, u32[]{:S(2)}, u32[]{:S(2)}) async-start(f32[8,128,256]{2,1,0:T(8,128)} %get-tuple-element.46), calls=%async_computation | async-start | bytes 2097152 | tf_op jit(solution)/shard_map/all_to_all | solution.py:483
  26.7 6.7 %collective-permute-start = (f32[128,256]{1,0:T(8,128)S(1)}, f32[128,256]{1,0:T(8,128)S(1)}, u32[]{:S(2)}, u32[]{:S(2)}) collective-permute-start(f32[128,256]{1,0:T(8,128)S(1)} %get-tuple-element.49.own_ref), channel_id=1, source_target_pairs={{0,16},{2,18},{4,20},{6,22},{8,24},{10,26},{12,28},{14,30},{16,0},... | collective-permute-start | bytes 393224 | tf_op jit(solution)/shard_map/ppermute | solution.py:534
  33.5 13.7 %copy-start.3 = (f32[6,128,256]{2,1,0:T(8,128)S(1)}, f32[6,128,256]{2,1,0:T(8,128)}, u32[]{:S(2)}) copy-start(f32[6,128,256]{2,1,0:T(8,128)} %get-tuple-element.48.tree_ref) | copy-start | bytes 2359300
  33.6 13.7 %copy-start.14 = (f32[128,128]{1,0:T(8,128)S(1)}, f32[128,128]{1,0:T(8,128)}, u32[]{:S(2)}) copy-start(f32[128,128]{1,0:T(8,128)} %get-tuple-element.50.init_ref) | copy-start | bytes 196612
  47.2 13.8 %copy-start.5 = (f32[8,256,128]{2,1,0:T(8,128)S(1)}, f32[8,256,128]{2,1,0:T(8,128)}, u32[]{:S(2)}) copy-start(f32[8,256,128]{2,1,0:T(8,128)} %get-tuple-element.45.c_ref) | copy-start | bytes 3145732
  48.0 13.0 %copy-start = (bf16[256,1024]{1,0:T(8,128)(2,1)S(1)}, bf16[256,1024]{1,0:T(8,128)(2,1)}, u32[]{:S(2)}) copy-start(bf16[256,1024]{1,0:T(8,128)(2,1)} %cot_ref.3) | copy-start | bytes 1572868
  48.0 13.0 %copy-start.11 = (bf16[8,256,128]{2,1,0:T(8,128)(2,1)S(1)}, bf16[8,256,128]{2,1,0:T(8,128)(2,1)}, u32[]{:S(2)}) copy-start(bf16[8,256,128]{2,1,0:T(8,128)(2,1)} %get-tuple-element.44.qt_ref) | copy-start | bytes 1572868
  61.0 1.9 %copy-start.10 = (bf16[8,128,256]{2,1,0:T(8,128)(2,1)S(1)}, bf16[8,128,256]{2,1,0:T(8,128)(2,1)}, u32[]{:S(2)}) copy-start(bf16[8,128,256]{2,1,0:T(8,128)(2,1)} %get-tuple-element.55.qtt_ref) | copy-start | bytes 1572868
  61.5 1.4 %collective-permute-start.1 = (f32[256,128]{1,0:T(8,128)S(1)}, f32[256,128]{1,0:T(8,128)S(1)}, u32[]{:S(2)}, u32[]{:S(2)}) collective-permute-start(f32[256,128]{1,0:T(8,128)S(1)} %get-tuple-element.54.own_ref), channel_id=1, source_target_pairs={{0,1},{1,0},{2,3},{3,2},{4,5},{5,4},{6,7},{7,6},{8,9},{9,8},{10,11... | collective-permute-start | bytes 393224 | tf_op jit(solution)/shard_map/ppermute | solution.py:556
  64.7 13.5 %all-to-all-start.3 = ((f32[8,128,128]{2,1,0:T(8,128)}), f32[8,128,128]{2,1,0:T(8,128)S(1)}, u32[]{:S(2)}, u32[]{:S(2)}) async-start(f32[8,128,128]{2,1,0:T(8,128)} %get-tuple-element.66), calls=%async_computation.3 | async-start | bytes 1048576 | tf_op jit(solution)/shard_map/all_to_all | solution.py:483
  78.2 6.5 %copy-start.15 = (f32[128,128]{1,0:T(8,128)S(1)}, f32[128,128]{1,0:T(8,128)}, u32[]{:S(2)}) copy-start(f32[128,128]{1,0:T(8,128)} %get-tuple-element.71.early_ref) | copy-start | bytes 196612
  78.8 5.8 %collective-permute-start.2 = (f32[128,128]{1,0:T(8,128)S(1)}, f32[128,128]{1,0:T(8,128)S(1)}, u32[]{:S(2)}, u32[]{:S(2)}) collective-permute-start(f32[128,128]{1,0:T(8,128)S(1)} %get-tuple-element.70.own_ref), channel_id=1, source_target_pairs={{0,16},{2,18},{4,20},{6,22},{8,24},{10,26},{12,28},{14,30},{16,0},... | collective-permute-start | bytes 196616 | tf_op jit(solution)/shard_map/ppermute | solution.py:593
  84.6 9.6 %copy-start.4 = (f32[6,128,256]{2,1,0:T(8,128)S(1)}, f32[6,128,256]{2,1,0:T(8,128)}, u32[]{:S(2)}) copy-start(f32[6,128,256]{2,1,0:T(8,128)} %get-tuple-element.48.tree_ref) | copy-start | bytes 2359300
  84.8 9.4 %copy-start.12 = (f32[4,128,128]{2,1,0:T(8,128)S(1)}, f32[4,128,128]{2,1,0:T(8,128)}, u32[]{:S(2)}) copy-start(f32[4,128,128]{2,1,0:T(8,128)} %get-tuple-element.64.after_ref) | copy-start | bytes 786436
  84.8 9.4 %copy-start.13 = (f32[4,128,128]{2,1,0:T(8,128)S(1)}, f32[4,128,128]{2,1,0:T(8,128)}, u32[]{:S(2)}) copy-start(f32[4,128,128]{2,1,0:T(8,128)} %get-tuple-element.65.first_ref) | copy-start | bytes 786436
  94.2 13.4 %copy-start.7 = (bf16[8,256,128]{2,1,0:T(8,128)(2,1)S(1)}, bf16[8,256,128]{2,1,0:T(8,128)(2,1)}, u32[]{:S(2)}) copy-start(bf16[8,256,128]{2,1,0:T(8,128)(2,1)} %get-tuple-element.63.dkp_ref) | copy-start | bytes 1572868
  94.2 13.4 %copy-start.8 = (bf16[8,256,128]{2,1,0:T(8,128)(2,1)S(1)}, bf16[8,256,128]{2,1,0:T(8,128)(2,1)}, u32[]{:S(2)}) copy-start(bf16[8,256,128]{2,1,0:T(8,128)(2,1)} %get-tuple-element.61.er_ref) | copy-start | bytes 1572868
  94.2 13.4 %copy-start.9 = (bf16[8,256,128]{2,1,0:T(8,128)(2,1)S(1)}, bf16[8,256,128]{2,1,0:T(8,128)(2,1)}, u32[]{:S(2)}) copy-start(bf16[8,256,128]{2,1,0:T(8,128)(2,1)} %get-tuple-element.60.tek_ref) | copy-start | bytes 1572868
  95.2 12.4 %copy-start.1 = (bf16[256,1024]{1,0:T(8,128)(2,1)S(1)}, bf16[256,1024]{1,0:T(8,128)(2,1)}, u32[]{:S(2)}) copy-start(bf16[256,1024]{1,0:T(8,128)(2,1)} %k_ref.3) | copy-start | bytes 1572868
  95.2 12.4 %copy-start.2 = (f32[8,256]{1,0:T(8,128)S(1)}, f32[8,256]{1,0:T(8,128)}, u32[]{:S(2)}) copy-start(f32[8,256]{1,0:T(8,128)} %e_ref.3) | copy-start | bytes 24580
  95.3 12.4 %copy-start.6 = (bf16[8,256,128]{2,1,0:T(8,128)(2,1)S(1)}, bf16[8,256,128]{2,1,0:T(8,128)(2,1)}, u32[]{:S(2)}) copy-start(bf16[8,256,128]{2,1,0:T(8,128)(2,1)} %get-tuple-element.62.u_ref) | copy-start | bytes 1572868

commit v4 on v3

--- a/solution.py
+++ b/solution.py
@@ -209,15 +209,14 @@
     return group // 2, group % 2
 
 
-def group_kernel(ab_ref, token_ref, whole_ref, tree_hbm, tree_ref, sems):
-    copies = Copies(sems)
+def group_kernel(ab_ref, token_ref, whole_ref, tree_ref, factors_ref):
     pairs = [compose(ab_ref[2 * i], ab_ref[2 * i + 1]) for i in range(4)]
     quads = [compose(pairs[2 * i], pairs[2 * i + 1]) for i in range(2)]
     for i, a in enumerate(pairs + quads):
+        factors_ref[i] = a[:, :HEAD]
+    for i, a in enumerate((pairs[0], pairs[2], quads[0])):
         tree_ref[i] = a
-    tree = copies.start(tree_ref, tree_hbm)
     whole_ref[...] = compose(quads[0], quads[1])
-    tree.wait()
 
 
 def pair_kernel(own_ref, other_ref, all_ref):
@@ -240,9 +239,9 @@
     plane, late = level()
     w0 = lax.fori_loop(0, plane, lambda z, w: apply_map(pairs_ref[z], w), init_ref[...])
     w0 = lax.fori_loop(0, late, lambda _, w: apply_map(other_ref[...], w), w0)
-    w4 = apply_map(tree_ref[4], w0)
+    w4 = apply_map(tree_ref[2], w0)
     w2 = apply_map(tree_ref[0], w0)
-    w6 = apply_map(tree_ref[2], w4)
+    w6 = apply_map(tree_ref[1], w4)
     for i, w in zip((0, 2, 4, 6), (w0, w2, w4, w6)):
         w_ref[i] = w
         w_ref[i + 1] = apply_map(ab_ref[i], w)
@@ -250,7 +249,7 @@
 
 
 def adjoint_kernel(
-    pairs_ref, ab_ref, tree_ref, other_ref, after_ref, first_ref, early_ref, up_ref
+    pairs_ref, ab_ref, factors_ref, other_ref, after_ref, first_ref, early_ref, up_ref
 ):
     eye = (
         lax.broadcasted_iota(jnp.int32, (HEAD, HEAD), 0)
@@ -258,12 +257,12 @@
     ).astype(F32)
     first = after = eye
     plane, late = level()
-    own = exact(halves(tree_ref[5, :, :HEAD]), halves(tree_ref[4, :, :HEAD]))
+    own = exact(halves(factors_ref[5]), halves(factors_ref[4]))
     early_ref[...] = jnp.transpose(jnp.where(late == 1, other_ref[:, :HEAD], own))
     for i in range(4):
         up_ref[i] = jnp.transpose(ab_ref[2 * i, :, :HEAD])
     for i, a in enumerate((0, 2, 4)):
-        up_ref[4 + i] = jnp.transpose(tree_ref[a, :, :HEAD])
+        up_ref[4 + i] = jnp.transpose(factors_ref[a])
     for z in range(PLANES):
         first_ref[z] = first
         later = z > plane
@@ -306,13 +305,13 @@
         dz = low(inv * go - z_ref[:, columns(h)] * shift)
         dz_ref[:, columns(h)] = dz
         g_ref[h] = dot(qtt_ref[h], dz)
+        normed_ref[:, columns(h)] = low(z_ref[:, columns(h)] * inv * gain_ref[:, columns(h)])
         if h % BATCH == BATCH - 1:
             part = slice(h + 1 - BATCH, h + 1)
+            flat = span(h + 1 - BATCH, h + 1)
             copies.start(g_ref.at[part], g_hbm.at[part])
-    copies.start(dz_ref, dz_hbm)
-    for h in range(heads):
-        normed_ref[:, columns(h)] = low(z_ref[:, columns(h)] * inv * gain_ref[:, columns(h)])
-    copies.start(normed_ref, normed_hbm)
+            copies.start(dz_ref.at[:, flat], dz_hbm.at[:, flat])
+            copies.start(normed_ref.at[:, flat], normed_hbm.at[:, flat])
     for copy in copies.started:
         copy.wait()
 
@@ -399,7 +398,7 @@
 
 
 def end_kernel(
-    after_ref, first_ref, ab_ref, tree_ref, g_ref, sums_ref, other_map_ref, other_ref, later_ref,
+    after_ref, first_ref, ab_ref, factors_ref, g_ref, sums_ref, other_map_ref, other_ref, later_ref,
     d_ref, init_ref,
 ):
     parts = [halves(later_ref[z]) for z in range(PLANES)]
@@ -409,9 +408,9 @@
         end += exact(halves(after_ref[z]), parts[z])
     inner = transposed_map(other_map_ref[:, :HEAD], end, other_ref[...])
     d7 = jnp.where(late == 1, end, inner)
-    d3 = transposed_map(tree_ref[5, :, :HEAD], d7, sums_ref[5])
-    d5 = transposed_map(tree_ref[3, :, :HEAD], d7, sums_ref[3])
-    d1 = transposed_map(tree_ref[1, :, :HEAD], d3, sums_ref[1])
+    d3 = transposed_map(factors_ref[5], d7, sums_ref[5])
+    d5 = transposed_map(factors_ref[3], d7, sums_ref[3])
+    d1 = transposed_map(factors_ref[1], d3, sums_ref[1])
     start = later_ref[0]
     for z in range(1, PLANES):
         start += exact(halves(first_ref[z]), parts[z])
@@ -487,7 +486,6 @@
     tall = (heads, n, HEAD)
     full = (heads, n, n)
     flat = (n, width)
-    branches = (6, HEAD, 2 * HEAD)
     token = ((8, HEAD), F32, "v")
     parts = heads // BATCH
     vm = pltpu.VMEM
@@ -524,12 +522,10 @@
     )
     slab = (HEAD, 2 * HEAD)
     block = (HEAD, HEAD)
-    whole, tree = call(
+    whole, tree, factors = call(
         group_kernel,
-        [(slab, F32, "v"), (branches, F32, "h")],
+        [(slab, F32, "v"), ((3, HEAD, 2 * HEAD), F32, "v"), ((6, HEAD, HEAD), F32, "v")],
         [(own_maps, "v"), (prepared, "v")],
-        [vm(branches, F32)],
-        copies=1,
     )
     other_map = lax.ppermute(whole, "ctx", across)
     (sent,) = call(
@@ -562,7 +558,7 @@
             (qt_turned, "v"),
         ],
         [vm(flat, BF16), vm(flat, BF16), vm(square, F32)],
-        copies=2 + parts,
+        copies=3 * parts,
     )
     own_grads = swap(local_grad, near)
     pair = (heads, n, 2 * HEAD)
@@ -583,7 +579,7 @@
     after, first, early, up = call(
         adjoint_kernel,
         [(steps, F32, "a"), (steps, F32, "a"), (block, F32, "a"), ((7, HEAD, HEAD), F32, "v")],
-        [(pair_maps, "v"), (own_maps, "v"), (tree, "a"), (other_map, "v")],
+        [(pair_maps, "v"), (own_maps, "v"), (factors, "v"), (other_map, "v")],
     )
     whole, sums = call(
         gather_kernel,
@@ -601,7 +597,7 @@
         end_kernel,
         [((GROUP, HEAD + 8, HEAD), F32, "v")],
         [
-            (after, "v"), (first, "v"), (own_maps, "v"), (tree, "v"), (own_grads, "v"),
+            (after, "v"), (first, "v"), (own_maps, "v"), (factors, "v"), (own_grads, "v"),
             (sums, "v"), (other_map, "v"), (other_grad, "v"), (pair_grads, "v"),
         ],
         [vm(block, F32)],

time: 111 us -> 111 us (level)
  Pallas kernels: 28.4 us -> 26.5 us
    pallas_call x13, Pallas kernels: 28.4 us -> 26.5 us  [call(): pl.pallas_call(kernel, out_shape=results, in_specs=[pl.BlockSpec(memory_s...]
  transfers between devices with their start and end apart: 5 -> 5, of which waited for: 5 -> 5; matrix products, arithmetic and copies ran while one was open for 0% -> 0% of each run, Pallas kernels for 13% -> 12%
where the time goes in v4:
time: 111 us; the launch traced here: 110 us
  blocking collectives  48.3 us (44%)
  Pallas kernels  26.5 us (24%)
  waiting for transfers between devices  18.7 us (17%)
  starting transfers between devices  14.7 us (13%)
    all_to_all x4, blocking collectives, swap(): return lax.all_to_all(a, 'ctx', 0, 0, axis_index_groups=groups)  48.3 us
    pallas_call x13, Pallas kernels, call(): pl.pallas_call(kernel, out_shape=results, in_specs=[pl.BlockSpec(memory_s...  26.5 us
    all_to_all x2, waiting for transfers between devices, swap(): return lax.all_to_all(a, 'ctx', 0, 0, axis_index_groups=groups)  10.5 us
    all_to_all x2, starting transfers between devices, swap(): return lax.all_to_all(a, 'ctx', 0, 0, axis_index_groups=groups)  9 us
    ppermute x1, waiting for transfers between devices, local(): other_map = lax.ppermute(whole, 'ctx', across)  3.84 us
    ppermute x1, waiting for transfers between devices, local(): other_grad = lax.ppermute(whole, 'ctx', across)  3.06 us
    ppermute x1, starting transfers between devices, local(): other_map = lax.ppermute(whole, 'ctx', across)  2.81 us
    ppermute x1, starting transfers between devices, local(): other_grad = lax.ppermute(whole, 'ctx', across)  2.79 us
  transfers between devices with their start and end apart: 5, of which 5 were waited for; matrix products, arithmetic and copies ran while one was open for 0% of the time, Pallas kernels for 12%

profile of v4, /device:TPU:0, one launch (start us, length us, event | category | flops | bytes accessed | tf_op | source)
XLA Modules:
  0.0 110.1 jit_solution(6994331030007209358)
XLA Ops:
  0.6 4.2 %map_kernel.1 = (f32[8,128,256]{2,1,0:T(8,128)}, bf16[8,2,128,128]{3,2,1,0:T(8,128)(2,1)}, bf16[8,128,128]{2,1,0:T(8,128)(2,1)}, bf16[8,256,256]{2,1,0:T(8,128)(2,1)}) custom-call(bf16[256,1024]{1,0:T(8,128)(2,1)} %k_ref.3, bf16[256,1024]{1,0:T(8,128)(2,1)} %v_hbm.1, f32[8,256]{1,0:T(8,128)} %e_ref.3), custom_call_target="tpu_custom_call" | custom-call | flops 2000000000 | bytes 2113536 | tf_op jit(solution)/shard_map/map_kernel/pallas_call | solution.py:54
  4.9 5.5 %all-to-all-start = ((f32[8,128,256]{2,1,0:T(8,128)}), f32[8,128,256]{2,1,0:T(8,128)S(1)}, u32[]{:S(2)}, u32[]{:S(2)}) async-start(f32[8,128,256]{2,1,0:T(8,128)} %get-tuple-element.47), calls=%async_computation | async-start | bytes 2097152 | tf_op jit(solution)/shard_map/all_to_all | solution.py:482
  10.4 7.4 %prepare_kernel.1 = (bf16[8,256,128]{2,1,0:T(8,128)(2,1)}, bf16[8,128,256]{2,1,0:T(8,128)(2,1)}, f32[8,256,128]{2,1,0:T(8,128)}, bf16[8,256,256]{2,1,0:T(8,128)(...) custom-call(bf16[256,1024]{1,0:T(8,128)(2,1)} %q_hbm.1, bf16[256,1024]{1,0:T(8,128)(2,1)} %k_ref.3, ...), custom_call_target="tpu_custom_call" | custom-call | flops 2000000000 | bytes 6832128 | tf_op jit(solution)/shard_map/prepare_kernel/pallas_call | solution.py:54
  17.8 7.4 %all-to-all-done.ab_ref = f32[8,128,256]{2,1,0:T(8,128)S(1)} async-done(((f32[8,128,256]{2,1,0:T(8,128)}), f32[8,128,256]{2,1,0:T(8,128)S(1)}, u32[]{:S(2)}, u32[]{:S(2)}) %all-to-all-start) | async-done | bytes 1048608 | tf_op jit(solution)/shard_map/all_to_all | solution.py:482
  25.2 0.8 group_kernel.1
  25.9 2.8 %collective-permute-start = (f32[128,256]{1,0:T(8,128)S(1)}, f32[128,256]{1,0:T(8,128)S(1)}, u32[]{:S(2)}, u32[]{:S(2)}) collective-permute-start(f32[128,256]{1,0:T(8,128)S(1)} %get-tuple-element.50.own_ref), channel_id=1, source_target_pairs={{0,16},{2,18},{4,20},{6,22},{8,24},{10,26},{12,28},{14,30},{16,0},... | collective-permute-start | bytes 393224 | tf_op jit(solution)/shard_map/ppermute | solution.py:530
  28.8 3.8 %collective-permute-done.other_ref.other_map_ref = f32[128,256]{1,0:T(8,128)S(1)} collective-permute-done((f32[128,256]{1,0:T(8,128)S(1)}, f32[128,256]{1,0:T(8,128)S(1)}, u32[]{:S(2)}, u32[]{:S(2)}) %collective-permute-start) | collective-permute-done | bytes 131104 | tf_op jit(solution)/shard_map/ppermute | solution.py:530
  32.6 0.2 pair_kernel.1
  32.8 13.6 %all_to_all.30.pairs_ref = f32[4,128,256]{2,1,0:T(8,128)S(1)} all-to-all(f32[4,128,256]{2,1,0:T(8,128)S(1)} %pair_kernel.1), channel_id=1, replica_groups={{0,32,64,96},{2,34,66,98},{4,36,68,100},{6,38,70,102},{8,40,72,104},{10..., dimensions={0} | all-to-all | bytes 1048576 | tf_op jit(solution)/shard_map/all_to_all | solution.py:482
  46.5 0.8 start_kernel.1
  47.3 0.0 copy-start
  47.3 0.0 copy-start.9
  47.3 13.0 %all_to_all.31.w_ref = f32[8,128,128]{2,1,0:T(8,128)S(1)} all-to-all(f32[8,128,128]{2,1,0:T(8,128)S(1)} %get-tuple-element.53), channel_id=1, replica_groups={{0,2,4,6,8,10,12,14},{16,18,20,22,24,26,28,30},{32,34,36,38,40,42,44,46..., dimensions={0} | all-to-all | bytes 1048576 | tf_op jit(solution)/shard_map/all_to_all | solution.py:482
  60.3 0.0 copy-start.8
  60.3 0.5 hidden_kernel.1
  60.8 0.1 collective-permute-start.1
  60.9 1.3 %collective-permute-done.1.other_ref = f32[256,128]{1,0:T(8,128)S(1)} collective-permute-done((f32[256,128]{1,0:T(8,128)S(1)}, f32[256,128]{1,0:T(8,128)S(1)}, u32[]{:S(2)}, u32[]{:S(2)}) %collective-permute-start.1) | collective-permute-done | bytes 131104 | tf_op jit(solution)/shard_map/ppermute | solution.py:552
  62.2 1.7 %norm_kernel.1 = (bf16[256,1024]{1,0:T(8,128)(2,1)}, bf16[256,1024]{1,0:T(8,128)(2,1)}, f32[8,128,128]{2,1,0:T(8,128)}) custom-call(f32[256,1024]{1,0:T(8,128)S(1)} %get-tuple-element.54.z_ref, bf16[256,1024]{1,0:T(8,128)(2,1)S(1)} %copy-done, f32[1,1024]{1,0:T(1,128)S(1)} %get-tuple-element.52.gain_ref, f32[256,128]{1,0:T(8,128)S(1)} %get-tuple-element.55.own_ref, ...), custom_call_target="tpu_custom_call" | custom-call | flops 2000000000 | bytes 4726784 | tf_op jit(solution)/shard_map/norm_kernel/pallas_call | solution.py:54
  63.9 3.5 %all-to-all-start.3 = ((f32[8,128,128]{2,1,0:T(8,128)}), f32[8,128,128]{2,1,0:T(8,128)S(1)}, u32[]{:S(2)}, u32[]{:S(2)}) async-start(f32[8,128,128]{2,1,0:T(8,128)} %get-tuple-element.68), calls=%async_computation.3 | async-start | bytes 1048576 | tf_op jit(solution)/shard_map/all_to_all | solution.py:482
  67.4 1.5 %adjoint_kernel.1 = (f32[4,128,128]{2,1,0:T(8,128)}, f32[4,128,128]{2,1,0:T(8,128)}, f32[128,128]{1,0:T(8,128)}, f32[7,128,128]{2,1,0:T(8,128)S(1)}) custom-call(f32[4,128,256]{2,1,0:T(8,128)S(1)} %all_to_all.30.pairs_ref, f32[8,128,256]{2,1,0:T(8,128)S(1)} %all-to-all-done.ab_ref, f32[6,128,128]{2,1,0:T(8,128)S(1)} %get-tuple-element.65.factors_ref, ...), custom_call_target="tpu_custom_call" | custom-call | flops 2000000000 | bytes 4194304 | tf_op jit(solution)/shard_map/adjoint_kernel/pallas_call | solution.py:54
  68.9 0.8 copy-done.12
  69.7 4.6 %query_kernel.1 = (bf16[256,1024]{1,0:T(8,128)(2,1)}, bf16[8,256,128]{2,1,0:T(8,128)(2,1)}, bf16[8,256,128]{2,1,0:T(8,128)(2,1)}, bf16[8,256,128]{2,1,0:T(8,128)(2,1)}, f32[8,128]{1,0:T(8,128)S(1)}) custom-call(bf16[256,1024]{1,0:T(8,128)(2,1)} %q_hbm.1, bf16[256,1024]{1,0:T(8,128)(2,1)} %k_ref.3, f32[8,256]{1,0:T(8,128)} %e_ref.3, ...), custom_call_target="tpu_custom_call" | custom-call | flops 2000000000 | bytes 8404992 | tf_op jit(solution)/shard_map/query_kernel/pallas_call | solution.py:54
  74.3 3.1 %all-to-all-done.3.g_ref = f32[8,128,128]{2,1,0:T(8,128)S(1)} async-done(((f32[8,128,128]{2,1,0:T(8,128)}), f32[8,128,128]{2,1,0:T(8,128)S(1)}, u32[]{:S(2)}, u32[]{:S(2)}) %all-to-all-start.3) | async-done | bytes 524320 | tf_op jit(solution)/shard_map/all_to_all | solution.py:482
  77.4 0.6 gather_kernel.1
  78.0 2.8 %collective-permute-start.2 = (f32[128,128]{1,0:T(8,128)S(1)}, f32[128,128]{1,0:T(8,128)S(1)}, u32[]{:S(2)}, u32[]{:S(2)}) collective-permute-start(f32[128,128]{1,0:T(8,128)S(1)} %get-tuple-element.72.own_ref), channel_id=1, source_target_pairs={{0,16},{2,18},{4,20},{6,22},{8,24},{10,26},{12,28},{14,30},{16,0},... | collective-permute-start | bytes 196616 | tf_op jit(solution)/shard_map/ppermute | solution.py:589
  80.8 3.1 %collective-permute-done.2.other_ref = f32[128,128]{1,0:T(8,128)S(1)} collective-permute-done((f32[128,128]{1,0:T(8,128)S(1)}, f32[128,128]{1,0:T(8,128)S(1)}, u32[]{:S(2)}, u32[]{:S(2)}) %collective-permute-start.2) | collective-permute-done | bytes 65568 | tf_op jit(solution)/shard_map/ppermute | solution.py:589
  83.9 0.2 pair_gradient_kernel.1
  84.1 9.4 %all_to_all.32.later_ref = f32[4,128,128]{2,1,0:T(8,128)S(1)} all-to-all(f32[4,128,128]{2,1,0:T(8,128)S(1)} %pair_gradient_kernel.1), channel_id=1, replica_groups={{0,32,64,96},{2,34,66,98},{4,36,68,100},{6,38,70,102},{8,40,72,104},{10..., dimensions={0} | all-to-all | bytes 524288 | tf_op jit(solution)/shard_map/all_to_all | solution.py:482
  93.5 1.0 end_kernel.1
  94.5 0.0 copy-start.2
  94.5 12.4 %all_to_all.33.d_ref = f32[8,136,128]{2,1,0:T(8,128)S(1)} all-to-all(f32[8,136,128]{2,1,0:T(8,128)S(1)} %end_kernel.1), channel_id=1, replica_groups={{0,2,4,6,8,10,12,14},{16,18,20,22,24,26,28,30},{32,34,36,38,40,42,44,46..., dimensions={0} | all-to-all | bytes 1114112 | tf_op jit(solution)/shard_map/all_to_all | solution.py:482
  106.9 3.0 %key_kernel.1 = (bf16[256,1024]{1,0:T(8,128)(2,1)}, bf16[256,1024]{1,0:T(8,128)(2,1)}, f32[8,256]{1,0:T(8,128)}, f32[8,256]{1,0:T(8,128)}) custom-call(bf16[256,1024]{1,0:T(8,128)(2,1)S(1)} %copy-done.1, f32[8,256]{1,0:T(8,128)S(1)} %copy-done.2, bf16[8,256,128]{2,1,0:T(8,128)(2,1)S(1)} %copy-done.7, bf16[8,256,128]{2,1,0:T(8,128)(2,1)S(1)} %copy-done.6, ...), custom_call_target="tpu_custom_call" | custom-call | flops 2000000000 | bytes 7421952 | tf_op jit(solution)/shard_map/key_kernel/pallas_call | solution.py:54
  (27 shorter events, 0.1 us)
Async XLA Ops:
  4.9 20.3 %all-to-all-start = ((f32[8,128,256]{2,1,0:T(8,128)}), f32[8,128,256]{2,1,0:T(8,128)S(1)}, u32[]{:S(2)}, u32[]{:S(2)}) async-start(f32[8,128,256]{2,1,0:T(8,128)} %get-tuple-element.47), calls=%async_computation | async-start | bytes 2097152 | tf_op jit(solution)/shard_map/all_to_all | solution.py:482
  25.9 6.7 %collective-permute-start = (f32[128,256]{1,0:T(8,128)S(1)}, f32[128,256]{1,0:T(8,128)S(1)}, u32[]{:S(2)}, u32[]{:S(2)}) collective-permute-start(f32[128,256]{1,0:T(8,128)S(1)} %get-tuple-element.50.own_ref), channel_id=1, source_target_pairs={{0,16},{2,18},{4,20},{6,22},{8,24},{10,26},{12,28},{14,30},{16,0},... | collective-permute-start | bytes 393224 | tf_op jit(solution)/shard_map/ppermute | solution.py:530
  32.8 13.7 %copy-start.14 = (f32[128,128]{1,0:T(8,128)S(1)}, f32[128,128]{1,0:T(8,128)}, u32[]{:S(2)}) copy-start(f32[128,128]{1,0:T(8,128)} %get-tuple-element.51.init_ref) | copy-start | bytes 196612
  46.5 13.8 %copy-start.3 = (f32[8,256,128]{2,1,0:T(8,128)S(1)}, f32[8,256,128]{2,1,0:T(8,128)}, u32[]{:S(2)}) copy-start(f32[8,256,128]{2,1,0:T(8,128)} %get-tuple-element.46.c_ref) | copy-start | bytes 3145732
  47.3 13.0 %copy-start = (bf16[256,1024]{1,0:T(8,128)(2,1)S(1)}, bf16[256,1024]{1,0:T(8,128)(2,1)}, u32[]{:S(2)}) copy-start(bf16[256,1024]{1,0:T(8,128)(2,1)} %cot_ref.3) | copy-start | bytes 1572868
  47.3 13.0 %copy-start.9 = (bf16[8,256,128]{2,1,0:T(8,128)(2,1)S(1)}, bf16[8,256,128]{2,1,0:T(8,128)(2,1)}, u32[]{:S(2)}) copy-start(bf16[8,256,128]{2,1,0:T(8,128)(2,1)} %get-tuple-element.45.qt_ref) | copy-start | bytes 1572868
  60.3 1.9 %copy-start.8 = (bf16[8,128,256]{2,1,0:T(8,128)(2,1)S(1)}, bf16[8,128,256]{2,1,0:T(8,128)(2,1)}, u32[]{:S(2)}) copy-start(bf16[8,128,256]{2,1,0:T(8,128)(2,1)} %get-tuple-element.56.qtt_ref) | copy-start | bytes 1572868
  60.8 1.4 %collective-permute-start.1 = (f32[256,128]{1,0:T(8,128)S(1)}, f32[256,128]{1,0:T(8,128)S(1)}, u32[]{:S(2)}, u32[]{:S(2)}) collective-permute-start(f32[256,128]{1,0:T(8,128)S(1)} %get-tuple-element.55.own_ref), channel_id=1, source_target_pairs={{0,1},{1,0},{2,3},{3,2},{4,5},{5,4},{6,7},{7,6},{8,9},{9,8},{10,11... | collective-permute-start | bytes 393224 | tf_op jit(solution)/shard_map/ppermute | solution.py:552
  63.9 13.5 %all-to-all-start.3 = ((f32[8,128,128]{2,1,0:T(8,128)}), f32[8,128,128]{2,1,0:T(8,128)S(1)}, u32[]{:S(2)}, u32[]{:S(2)}) async-start(f32[8,128,128]{2,1,0:T(8,128)} %get-tuple-element.68), calls=%async_computation.3 | async-start | bytes 1048576 | tf_op jit(solution)/shard_map/all_to_all | solution.py:482
  68.9 0.8 copy-start.12
  69.7 7.7 %copy-start.13 = (f32[7,128,128]{2,1,0:T(8,128)S(1)}, f32[7,128,128]{2,1,0:T(8,128)}, u32[]{:S(2)}) copy-start(f32[7,128,128]{2,1,0:T(8,128)} %copy-done.12) | copy-start | bytes 1376260
  77.4 6.5 %copy-start.15 = (f32[128,128]{1,0:T(8,128)S(1)}, f32[128,128]{1,0:T(8,128)}, u32[]{:S(2)}) copy-start(f32[128,128]{1,0:T(8,128)} %get-tuple-element.73.early_ref) | copy-start | bytes 196612
  78.0 5.8 %collective-permute-start.2 = (f32[128,128]{1,0:T(8,128)S(1)}, f32[128,128]{1,0:T(8,128)S(1)}, u32[]{:S(2)}, u32[]{:S(2)}) collective-permute-start(f32[128,128]{1,0:T(8,128)S(1)} %get-tuple-element.72.own_ref), channel_id=1, source_target_pairs={{0,16},{2,18},{4,20},{6,22},{8,24},{10,26},{12,28},{14,30},{16,0},... | collective-permute-start | bytes 196616 | tf_op jit(solution)/shard_map/ppermute | solution.py:589
  84.1 9.4 %copy-start.10 = (f32[4,128,128]{2,1,0:T(8,128)S(1)}, f32[4,128,128]{2,1,0:T(8,128)}, u32[]{:S(2)}) copy-start(f32[4,128,128]{2,1,0:T(8,128)} %get-tuple-element.66.after_ref) | copy-start | bytes 786436
  84.1 9.4 %copy-start.11 = (f32[4,128,128]{2,1,0:T(8,128)S(1)}, f32[4,128,128]{2,1,0:T(8,128)}, u32[]{:S(2)}) copy-start(f32[4,128,128]{2,1,0:T(8,128)} %get-tuple-element.67.first_ref) | copy-start | bytes 786436
  93.5 13.4 %copy-start.5 = (bf16[8,256,128]{2,1,0:T(8,128)(2,1)S(1)}, bf16[8,256,128]{2,1,0:T(8,128)(2,1)}, u32[]{:S(2)}) copy-start(bf16[8,256,128]{2,1,0:T(8,128)(2,1)} %get-tuple-element.64.dkp_ref) | copy-start | bytes 1572868
  93.5 13.4 %copy-start.6 = (bf16[8,256,128]{2,1,0:T(8,128)(2,1)S(1)}, bf16[8,256,128]{2,1,0:T(8,128)(2,1)}, u32[]{:S(2)}) copy-start(bf16[8,256,128]{2,1,0:T(8,128)(2,1)} %get-tuple-element.62.er_ref) | copy-start | bytes 1572868
  93.5 13.4 %copy-start.7 = (bf16[8,256,128]{2,1,0:T(8,128)(2,1)S(1)}, bf16[8,256,128]{2,1,0:T(8,128)(2,1)}, u32[]{:S(2)}) copy-start(bf16[8,256,128]{2,1,0:T(8,128)(2,1)} %get-tuple-element.61.tek_ref) | copy-start | bytes 1572868
  94.5 12.4 %copy-start.1 = (bf16[256,1024]{1,0:T(8,128)(2,1)S(1)}, bf16[256,1024]{1,0:T(8,128)(2,1)}, u32[]{:S(2)}) copy-start(bf16[256,1024]{1,0:T(8,128)(2,1)} %k_ref.3) | copy-start | bytes 1572868
  94.5 12.4 %copy-start.2 = (f32[8,256]{1,0:T(8,128)S(1)}, f32[8,256]{1,0:T(8,128)}, u32[]{:S(2)}) copy-start(f32[8,256]{1,0:T(8,128)} %e_ref.3) | copy-start | bytes 24580
  94.5 12.4 %copy-start.4 = (bf16[8,256,128]{2,1,0:T(8,128)(2,1)S(1)}, bf16[8,256,128]{2,1,0:T(8,128)(2,1)}, u32[]{:S(2)}) copy-start(bf16[8,256,128]{2,1,0:T(8,128)(2,1)} %get-tuple-element.63.u_ref) | copy-start | bytes 1572868

commit v5 on v4

--- a/solution.py
+++ b/solution.py
@@ -89,8 +89,8 @@
 
 
 def map_kernel(
-    k_hbm, v_hbm, e_hbm, ab_hbm, t_hbm, n_hbm, tkv_hbm,
-    k_ref, v_ref, e_ref, ab_ref, t_ref, n_ref, tkv_ref, sems,
+    k_hbm, v_hbm, e_hbm, ab_ref, t_hbm, n_hbm, tkv_hbm,
+    k_ref, v_ref, e_ref, t_ref, n_ref, tkv_ref, sems,
 ):
     heads = e_ref.shape[0]
     half = t_ref.shape[-1]
@@ -150,47 +150,114 @@
         ab = dot(scaled[h], tkv_ref[h])
         ab_ref[h, :, :HEAD] = eye - ab[:, :HEAD]
         ab_ref[h, :, HEAD:] = ab[:, HEAD:]
-        if h % 2 == 1:
-            sent.append(copies.start(ab_ref.at[h - 1 : h + 1], ab_hbm.at[h - 1 : h + 1]))
     for copy in sent:
         copy.wait()
 
 
-def prepare_kernel(
-    q_ref, k_ref, e_ref, t_ref, n_ref, tkv_ref, init_hbm,
-    qt_ref, qtt_ref, c_ref, st_ref, tek_ref, own_hbm, token_ref, sems,
-):
-    initial = Copies(sems).start(init_hbm.at[lax.axis_index("ctx") % GROUP], own_hbm)
-    n = k_ref.shape[0]
-    half = n // 2
-    heads = e_ref.shape[0]
+def causal_scores(q, k, e):
+    n = q.shape[0]
     row = lax.broadcasted_iota(jnp.int32, (n, n), 0)
     col = lax.broadcasted_iota(jnp.int32, (n, n), 1)
-    causal = row >= col
+    return low(jnp.where(row >= col, dot_nt(q, k) * e, 0.0))
+
+
+def prepare_kernel(
+    q_hbm, k_hbm, e_hbm, tkv_hbm, init_hbm,
+    qt_hbm, qtt_hbm, c_hbm, se_hbm, own_hbm, token_ref,
+    q_ref, k_ref, e_ref, tkv_ref, qt_ref, qtt_ref, c_ref, se_ref, sems,
+):
+    heads = e_ref.shape[0]
+    copies = Copies(sems)
+    sent = [copies.start(init_hbm.at[lax.axis_index("ctx") % GROUP], own_hbm)]
+    rates = copies.start(e_hbm, e_ref)
+    arrivals = []
+    for first in range(0, heads, BATCH):
+        part = slice(first, first + BATCH)
+        flat = span(first, first + BATCH)
+        arrivals.append((
+            copies.start(q_hbm.at[:, flat], q_ref.at[:, flat]),
+            copies.start(k_hbm.at[:, flat], k_ref.at[:, flat]),
+            copies.start(tkv_hbm.at[part], tkv_ref.at[part]),
+        ))
     token_ref[...] = jnp.zeros_like(token_ref)
-    for h in range(heads):
-        q = q_ref[:, columns(h)]
-        k = k_ref[:, columns(h)]
-        e = e_ref[h : h + 1, :]
-        se = low(jnp.where(causal, dot_nt(q, k) * e, 0.0))
-        sx = dot(se, tkv_ref[h])
-        qt = q.astype(F32) - sx[:, :HEAD]
-        qt_ref[h] = low(qt)
-        qtt_ref[h] = low(jnp.transpose(qt))
-        c_ref[h] = sx[:, HEAD:]
-        top, bottom = t_ref[h, 0], t_ref[h, 1]
-        cross = low(dot(bottom, low(dot(n_ref[h], top))))
-        t = jnp.concatenate(
-            [
-                jnp.concatenate([top, jnp.zeros((half, half), BF16)], axis=1),
-                jnp.concatenate([cross, bottom], axis=1),
-            ],
-            axis=0,
-        )
-        st_ref[h] = low(-dot(se, t))
-        wide = jnp.transpose(jnp.broadcast_to(e, (HEAD, n)))
-        tek_ref[h] = low(dot_tn(t, low(k.astype(F32) * wide)))
-    initial.wait()
+    rates.wait()
+    for first, arrival in zip(range(0, heads, BATCH), arrivals):
+        batch = range(first, first + BATCH)
+        for copy in arrival:
+            copy.wait()
+        scores = [
+            causal_scores(q_ref[:, columns(h)], k_ref[:, columns(h)], e_ref[h : h + 1, :])
+            for h in batch
+        ]
+        for h, se in zip(batch, scores):
+            se_ref[h] = se
+            sx = dot(se, tkv_ref[h])
+            qt = q_ref[:, columns(h)].astype(F32) - sx[:, :HEAD]
+            qt_ref[h] = low(qt)
+            qtt_ref[h] = low(jnp.transpose(qt))
+            c_ref[h] = sx[:, HEAD:]
+        part = slice(first, first + BATCH)
+        for source, target in (
+            (qt_ref, qt_hbm), (qtt_ref, qtt_hbm), (c_ref, c_hbm), (se_ref, se_hbm)
+        ):
+            sent.append(copies.start(source.at[part], target.at[part]))
+    for copy in sent:
+        copy.wait()
+
+
+def adjoint_residual_kernel(
+    k_hbm, e_hbm, se_hbm, t_hbm, n_hbm, dz_hbm, u_hbm, tek_hbm, token_ref,
+    k_ref, e_ref, se_ref, t_ref, n_ref, dz_ref, u_ref, tek_ref, sems,
+):
+    heads, n = e_ref.shape
+    half = n // 2
+    copies = Copies(sems)
+    rates = copies.start(e_hbm, e_ref)
+    arrivals = []
+    for first in range(0, heads, BATCH):
+        part = slice(first, first + BATCH)
+        flat = span(first, first + BATCH)
+        arrivals.append((
+            copies.start(t_hbm.at[part], t_ref.at[part]),
+            copies.start(n_hbm.at[part], n_ref.at[part]),
+            copies.start(k_hbm.at[:, flat], k_ref.at[:, flat]),
+            copies.start(se_hbm.at[part], se_ref.at[part]),
+            copies.start(dz_hbm.at[:, flat], dz_ref.at[:, flat]),
+        ))
+    token_ref[...] = jnp.zeros_like(token_ref)
+    rates.wait()
+    sent = []
+    for first, arrival in zip(range(0, heads, BATCH), arrivals):
+        batch = range(first, first + BATCH)
+        wides = [jnp.transpose(jnp.broadcast_to(e_ref[h : h + 1, :], (HEAD, n))) for h in batch]
+        for copy in arrival:
+            copy.wait()
+        mids = [low(dot(n_ref[h], t_ref[h, 0])) for h in batch]
+        ys = [
+            jnp.concatenate(
+                [
+                    low(dot_tn(se_ref[h], dz_ref[:, columns(h)])),
+                    low(k_ref[:, columns(h)].astype(F32) * wide),
+                ],
+                axis=1,
+            )
+            for h, wide in zip(batch, wides)
+        ]
+        lowers = [dot_tn(t_ref[h, 1], y[half:]) for h, y in zip(batch, ys)]
+        uppers = [
+            dot_tn(t_ref[h, 0], y[:half]) + dot_tn(m, low(x))
+            for h, y, m, x in zip(batch, ys, mids, lowers)
+        ]
+        for h, upper, lower in zip(batch, uppers, lowers):
+            u_ref[h, :half] = low(-upper[:, :HEAD])
+            u_ref[h, half:] = low(-lower[:, :HEAD])
+            tek_ref[h, :half] = low(upper[:, HEAD:])
+            tek_ref[h, half:] = low(lower[:, HEAD:])
+        part = slice(first, first + BATCH)
+        for source, target in ((u_ref, u_hbm), (tek_ref, tek_hbm)):
+            sent.append(copies.start(source.at[part], target.at[part]))
+    for copy in sent:
+        copy.wait()
 
 
 def compose(early, late):
@@ -209,7 +276,7 @@
     return group // 2, group % 2
 
 
-def group_kernel(ab_ref, token_ref, whole_ref, tree_ref, factors_ref):
+def group_kernel(ab_ref, whole_ref, tree_ref, factors_ref):
     pairs = [compose(ab_ref[2 * i], ab_ref[2 * i + 1]) for i in range(4)]
     quads = [compose(pairs[2 * i], pairs[2 * i + 1]) for i in range(2)]
     for i, a in enumerate(pairs + quads):
@@ -219,7 +286,7 @@
     whole_ref[...] = compose(quads[0], quads[1])
 
 
-def pair_kernel(own_ref, other_ref, all_ref):
+def pair_kernel(own_ref, other_ref, token_ref, all_ref):
     _, late = level()
     own, other = own_ref[...], other_ref[...]
     early = jnp.where(late == 1, other, own)
@@ -317,9 +384,8 @@
 
 
 def query_kernel(
-    q_hbm, k_hbm, e_hbm, tkv_hbm, st_hbm, dz_hbm, w_ref,
-    dq_hbm, u_hbm, dk_hbm, er_hbm, token_ref,
-    q_ref, k_ref, e_ref, tkv_ref, st_ref, dz_ref, dq_ref, u_ref, dk_ref, er_ref, sems,
+    q_hbm, k_hbm, e_hbm, tkv_hbm, dz_hbm, w_ref, dq_hbm, dk_hbm, er_hbm, token_ref,
+    q_ref, k_ref, e_ref, tkv_ref, dz_ref, dq_ref, dk_ref, er_ref, sems,
 ):
     n = k_ref.shape[0]
     heads = e_ref.shape[0]
@@ -334,7 +400,6 @@
             copies.start(dz_hbm.at[:, flat], dz_ref.at[:, flat]),
             copies.start(k_hbm.at[:, flat], k_ref.at[:, flat]),
             copies.start(q_hbm.at[:, flat], q_ref.at[:, flat]),
-            copies.start(st_hbm.at[part], st_ref.at[part]),
         ))
     row = lax.broadcasted_iota(jnp.int32, (n, n), 0)
     col = lax.broadcasted_iota(jnp.int32, (n, n), 1)
@@ -361,11 +426,10 @@
                 dot_nt(dz_ref[:, columns(h)], w) + dot(ds, k_ref[:, columns(h)])
             )
             dk_ref[h] = low(dot_tn(ds, q_ref[:, columns(h)]))
-            u_ref[h] = low(dot_tn(st_ref[h], dz_ref[:, columns(h)]))
         part = slice(first, first + BATCH)
         flat = span(first, first + BATCH)
         sent.append(copies.start(dq_ref.at[:, flat], dq_hbm.at[:, flat]))
-        for source, target in ((u_ref, u_hbm), (dk_ref, dk_hbm), (er_ref, er_hbm)):
+        for source, target in ((dk_ref, dk_hbm), (er_ref, er_hbm)):
             sent.append(copies.start(source.at[part], target.at[part]))
     for copy in sent:
         copy.wait()
@@ -387,7 +451,7 @@
     whole_ref[...] = turned_map(up_ref[6], quads[1], quads[0])
 
 
-def pair_gradient_kernel(early_ref, own_ref, other_ref, all_ref):
+def pair_gradient_kernel(early_ref, own_ref, other_ref, token_ref, all_ref):
     _, late = level()
     own, other = own_ref[...], other_ref[...]
     pair = turned_map(
@@ -493,45 +557,47 @@
     half = n // 2
     inner = (heads, 2, half, half)
     corner = (heads, half, half)
+    pair = (heads, n, 2 * HEAD)
     turned = (heads, HEAD, n)
     maps, inverse, cross, tkv = call(
         map_kernel,
         [
-            (wide, F32, "h"), (inner, BF16, "h"), (corner, BF16, "h"),
+            (wide, F32, "v"), (inner, BF16, "h"), (corner, BF16, "h"),
             ((heads, n, 2 * HEAD), BF16, "h"),
         ],
         [(keys, "h"), (values, "h"), (rates, "h")],
         [
             vm(flat, BF16), vm(flat, BF16), vm((heads, n), F32),
-            vm(wide, F32), vm(inner, BF16), vm(corner, BF16), vm((heads, n, 2 * HEAD), BF16),
-        ],
-        copies=4 + 2 * parts + heads // 2,
+            vm(inner, BF16), vm(corner, BF16), vm((heads, n, 2 * HEAD), BF16),
+        ],
+        copies=4 + 2 * parts,
     )
     own_maps = swap(maps, near)
-    qt, qt_turned, offset, scores, tek, own_init, prepared = call(
+    qt, qt_turned, offset, scores, own_init, prepared = call(
         prepare_kernel,
         [
-            (tall, BF16, "a"), (turned, BF16, "a"), (tall, F32, "a"), (full, BF16, "a"),
-            (tall, BF16, "a"), ((HEAD, HEAD), F32, "h"), token,
-        ],
-        [
-            (queries, "a"), (keys, "a"), (rates, "a"), (inverse, "a"), (cross, "a"), (tkv, "a"),
-            (init_weight, "h"),
-        ],
-        copies=1,
+            (tall, BF16, "h"), (turned, BF16, "h"), (tall, F32, "h"), (full, BF16, "h"),
+            ((HEAD, HEAD), F32, "h"), token,
+        ],
+        [(queries, "h"), (keys, "h"), (rates, "h"), (tkv, "h"), (init_weight, "h")],
+        [
+            vm(flat, BF16), vm(flat, BF16), vm((heads, n), F32), vm(pair, BF16), vm(tall, BF16),
+            vm(turned, BF16), vm(tall, F32), vm(full, BF16),
+        ],
+        copies=2 + 7 * parts,
     )
     slab = (HEAD, 2 * HEAD)
     block = (HEAD, HEAD)
     whole, tree, factors = call(
         group_kernel,
         [(slab, F32, "v"), ((3, HEAD, 2 * HEAD), F32, "v"), ((6, HEAD, HEAD), F32, "v")],
-        [(own_maps, "v"), (prepared, "v")],
+        [(own_maps, "v")],
     )
     other_map = lax.ppermute(whole, "ctx", across)
     (sent,) = call(
         pair_kernel,
         [((PLANES, HEAD, 2 * HEAD), F32, "v")],
-        [(whole, "v"), (other_map, "v")],
+        [(whole, "v"), (other_map, "v"), (prepared, "v")],
     )
     pair_maps = swap(sent, far)
     starts, gain_row = call(
@@ -561,19 +627,29 @@
         copies=3 * parts,
     )
     own_grads = swap(local_grad, near)
-    pair = (heads, n, 2 * HEAD)
-    grad_queries, u, dk_part, scaled_residual, queried = call(
+    grad_queries, dk_part, scaled_residual, queried = call(
         query_kernel,
-        [(flat, BF16, "h"), (tall, BF16, "h"), (tall, BF16, "h"), (tall, BF16, "h"), token],
-        [
-            (queries, "h"), (keys, "h"), (rates, "h"), (tkv, "h"), (scores, "h"), (dz, "h"),
-            (weights, "v"),
-        ],
-        [
-            vm(flat, BF16), vm(flat, BF16), vm((heads, n), F32), vm(pair, BF16), vm(full, BF16),
-            vm(flat, BF16), vm(flat, BF16), vm(tall, BF16), vm(tall, BF16), vm(tall, BF16),
-        ],
-        copies=1 + 9 * parts,
+        [(flat, BF16, "h"), (tall, BF16, "h"), (tall, BF16, "h"), token],
+        [
+            (queries, "h"), (keys, "h"), (rates, "h"), (tkv, "h"), (dz, "h"), (weights, "v"),
+        ],
+        [
+            vm(flat, BF16), vm(flat, BF16), vm((heads, n), F32), vm(pair, BF16),
+            vm(flat, BF16), vm(flat, BF16), vm(tall, BF16), vm(tall, BF16),
+        ],
+        copies=1 + 7 * parts,
+    )
+    u, tek, settled = call(
+        adjoint_residual_kernel,
+        [(tall, BF16, "h"), (tall, BF16, "h"), token],
+        [
+            (keys, "h"), (rates, "h"), (scores, "h"), (inverse, "h"), (cross, "h"), (dz, "h"),
+        ],
+        [
+            vm(flat, BF16), vm((heads, n), F32), vm(full, BF16), vm(inner, BF16),
+            vm(corner, BF16), vm(flat, BF16), vm(tall, BF16), vm(tall, BF16),
+        ],
+        copies=1 + 7 * parts,
     )
     steps = (PLANES, HEAD, HEAD)
     after, first, early, up = call(
@@ -590,7 +666,7 @@
     (sent,) = call(
         pair_gradient_kernel,
         [(steps, F32, "v")],
-        [(early, "v"), (whole, "v"), (other_grad, "v")],
+        [(early, "v"), (whole, "v"), (other_grad, "v"), (settled, "v")],
     )
     pair_grads = swap(sent, far)
     (ends,) = call(

time: 111 us -> 109 us (0.982)
  blocking collectives: 48.3 us -> 66.9 us
  waiting for transfers between devices: 18.7 us -> 5.23 us
  starting transfers between devices: 14.7 us -> 9.21 us
    all_to_all x4 -> x5, blocking collectives: 48.3 us -> 66.9 us  [swap(): return lax.all_to_all(a, 'ctx', 0, 0, axis_index_groups=groups)]
    all_to_all x2 -> x1, waiting for transfers between devices: 10.5 us -> 3.64 us  [swap(): return lax.all_to_all(a, 'ctx', 0, 0, axis_index_groups=groups)]
    all_to_all x2 -> x1, starting transfers between devices: 9 us -> 3.5 us  [swap(): return lax.all_to_all(a, 'ctx', 0, 0, axis_index_groups=groups)]
    ppermute x1, waiting for transfers between devices: 3.84 us -> 0.25 us  [local(): other_map = lax.ppermute(whole, 'ctx', across)]
    ppermute x1, waiting for transfers between devices: 3.06 us -> 0.01 us  [local(): other_grad = lax.ppermute(whole, 'ctx', across)]
    pallas_call x13 -> x14, Pallas kernels: 26.5 us -> 25.4 us  [call(): pl.pallas_call(kernel, out_shape=results, in_specs=[pl.BlockSpec(memory_s...]
  transfers between devices with their start and end apart: 5 -> 4, of which waited for: 5 -> 3; matrix products, arithmetic and copies ran while one was open for 0% -> 0% of each run, Pallas kernels for 12% -> 12%
where the time goes in v5:
time: 109 us
  blocking collectives  66.9 us (61%)
  Pallas kernels  25.4 us (23%)
  starting transfers between devices  9.21 us (8%)
  waiting for transfers between devices  5.23 us (5%)
    all_to_all x5, blocking collectives, swap(): return lax.all_to_all(a, 'ctx', 0, 0, axis_index_groups=groups)  66.9 us
    pallas_call x14, Pallas kernels, call(): pl.pallas_call(kernel, out_shape=results, in_specs=[pl.BlockSpec(memory_s...  25.4 us
    all_to_all x1, waiting for transfers between devices, swap(): return lax.all_to_all(a, 'ctx', 0, 0, axis_index_groups=groups)  3.64 us
    all_to_all x1, starting transfers between devices, swap(): return lax.all_to_all(a, 'ctx', 0, 0, axis_index_groups=groups)  3.5 us
    ppermute x1, starting transfers between devices, local(): other_grad = lax.ppermute(whole, 'ctx', across)  2.81 us
    ppermute x1, starting transfers between devices, local(): other_map = lax.ppermute(whole, 'ctx', across)  2.81 us
  transfers between devices with their start and end apart: 4, of which 3 were waited for; matrix products, arithmetic and copies ran while one was open for 0% of the time, Pallas kernels for 12%

profile of v5, /device:TPU:0, one launch (start us, length us, event | category | flops | bytes accessed | tf_op | source)
XLA Modules:
  0.0 108.5 jit_solution(2506877011486009437)
XLA Ops:
  0.6 3.8 %map_kernel.1 = (f32[8,128,256]{2,1,0:T(8,128)S(1)}, bf16[8,2,128,128]{3,2,1,0:T(8,128)(2,1)}, bf16[8,128,128]{2,1,0:T(8,128)(2,1)}, bf16[8,256,256]{2,1,0:T(8,128)(2,1)}) custom-call(bf16[256,1024]{1,0:T(8,128)(2,1)} %k_ref.1, bf16[256,1024]{1,0:T(8,128)(2,1)} %v_hbm.1, f32[8,256]{1,0:T(8,128)} %e_ref.1), custom_call_target="tpu_custom_call" | custom-call | flops 2000000000 | bytes 2113536 | tf_op jit(solution)/shard_map/map_kernel/pallas_call | solution.py:54
  4.5 21.1 %all_to_all.30.ab_ref = f32[8,128,256]{2,1,0:T(8,128)S(1)} all-to-all(f32[8,128,256]{2,1,0:T(8,128)S(1)} %get-tuple-element.46), channel_id=1, replica_groups={{0,2,4,6,8,10,12,14},{16,18,20,22,24,26,28,30},{32,34,36,38,40,42,44,46..., dimensions={0} | all-to-all | bytes 2097152 | tf_op jit(solution)/shard_map/all_to_all | solution.py:546
  25.5 0.8 group_kernel.1
  26.3 2.8 %collective-permute-start = (f32[128,256]{1,0:T(8,128)S(1)}, f32[128,256]{1,0:T(8,128)S(1)}, u32[]{:S(2)}, u32[]{:S(2)}) collective-permute-start(f32[128,256]{1,0:T(8,128)S(1)} %get-tuple-element.48.own_ref), channel_id=1, source_target_pairs={{0,16},{2,18},{4,20},{6,22},{8,24},{10,26},{12,28},{14,30},{16,0},... | collective-permute-start | bytes 393224 | tf_op jit(solution)/shard_map/ppermute | solution.py:596
  29.1 3.5 %prepare_kernel.1 = (bf16[8,256,128]{2,1,0:T(8,128)(2,1)}, bf16[8,128,256]{2,1,0:T(8,128)(2,1)}, f32[8,256,128]{2,1,0:T(8,128)}, bf16[8,256,256]{2,1,0:T(8,128)(...) custom-call(bf16[256,1024]{1,0:T(8,128)(2,1)} %q_hbm.3, bf16[256,1024]{1,0:T(8,128)(2,1)} %k_ref.1, f32[8,256]{1,0:T(8,128)} %e_ref.1, ...), custom_call_target="tpu_custom_call" | custom-call | flops 2000000000 | bytes 5259264 | tf_op jit(solution)/shard_map/prepare_kernel/pallas_call | solution.py:54
  32.6 0.3 collective-permute-done.other_ref.other_map_ref
  32.9 0.2 pair_kernel.1
  33.1 0.0 copy-start.14
  33.1 13.3 %all_to_all.31.pairs_ref = f32[4,128,256]{2,1,0:T(8,128)S(1)} all-to-all(f32[4,128,256]{2,1,0:T(8,128)S(1)} %pair_kernel.1), channel_id=1, replica_groups={{0,32,64,96},{2,34,66,98},{4,36,68,100},{6,38,70,102},{8,40,72,104},{10..., dimensions={0} | all-to-all | bytes 1048576 | tf_op jit(solution)/shard_map/all_to_all | solution.py:546
  46.4 0.8 start_kernel.1
  47.2 0.0 copy-start
  47.2 0.0 copy-start.9
  47.3 11.2 %all_to_all.32.w_ref = f32[8,128,128]{2,1,0:T(8,128)S(1)} all-to-all(f32[8,128,128]{2,1,0:T(8,128)S(1)} %get-tuple-element.52), channel_id=1, replica_groups={{0,2,4,6,8,10,12,14},{16,18,20,22,24,26,28,30},{32,34,36,38,40,42,44,46..., dimensions={0} | all-to-all | bytes 1048576 | tf_op jit(solution)/shard_map/all_to_all | solution.py:546
  58.5 0.0 copy-start.8
  58.5 0.5 hidden_kernel.1
  59.0 0.1 collective-permute-start.1
  59.1 1.3 %collective-permute-done.1.other_ref = f32[256,128]{1,0:T(8,128)S(1)} collective-permute-done((f32[256,128]{1,0:T(8,128)S(1)}, f32[256,128]{1,0:T(8,128)S(1)}, u32[]{:S(2)}, u32[]{:S(2)}) %collective-permute-start.1) | collective-permute-done | bytes 131104 | tf_op jit(solution)/shard_map/ppermute | solution.py:618
  60.4 1.7 %norm_kernel.1 = (bf16[256,1024]{1,0:T(8,128)(2,1)}, bf16[256,1024]{1,0:T(8,128)(2,1)}, f32[8,128,128]{2,1,0:T(8,128)}) custom-call(f32[256,1024]{1,0:T(8,128)S(1)} %get-tuple-element.53.z_ref, bf16[256,1024]{1,0:T(8,128)(2,1)S(1)} %copy-done, f32[1,1024]{1,0:T(1,128)S(1)} %get-tuple-element.51.gain_ref, f32[256,128]{1,0:T(8,128)S(1)} %get-tuple-element.54.own_ref, ...), custom_call_target="tpu_custom_call" | custom-call | flops 2000000000 | bytes 4726784 | tf_op jit(solution)/shard_map/norm_kernel/pallas_call | solution.py:54
  62.2 3.5 %all-to-all-start.3 = ((f32[8,128,128]{2,1,0:T(8,128)}), f32[8,128,128]{2,1,0:T(8,128)S(1)}, u32[]{:S(2)}, u32[]{:S(2)}) async-start(f32[8,128,128]{2,1,0:T(8,128)} %get-tuple-element.69), calls=%async_computation.3 | async-start | bytes 1048576 | tf_op jit(solution)/shard_map/all_to_all | solution.py:546
  65.7 1.5 %adjoint_kernel.1 = (f32[4,128,128]{2,1,0:T(8,128)}, f32[4,128,128]{2,1,0:T(8,128)}, f32[128,128]{1,0:T(8,128)}, f32[7,128,128]{2,1,0:T(8,128)S(1)}) custom-call(f32[4,128,256]{2,1,0:T(8,128)S(1)} %all_to_all.31.pairs_ref, f32[8,128,256]{2,1,0:T(8,128)S(1)} %all_to_all.30.ab_ref, f32[6,128,128]{2,1,0:T(8,128)S(1)} %get-tuple-element.66.factors_ref, ...), custom_call_target="tpu_custom_call" | custom-call | flops 2000000000 | bytes 4194304 | tf_op jit(solution)/shard_map/adjoint_kernel/pallas_call | solution.py:54
  67.2 0.8 copy-done.12
  67.9 4.0 %query_kernel.1 = (bf16[256,1024]{1,0:T(8,128)(2,1)}, bf16[8,256,128]{2,1,0:T(8,128)(2,1)}, bf16[8,256,128]{2,1,0:T(8,128)(2,1)}, f32[8,128]{1,0:T(8,128)S(1)}) custom-call(bf16[256,1024]{1,0:T(8,128)(2,1)} %q_hbm.3, bf16[256,1024]{1,0:T(8,128)(2,1)} %k_ref.1, f32[8,256]{1,0:T(8,128)} %e_ref.1, bf16[8,256,256]{2,1,0:T(8,128)(2,1)} %get-tuple-element.43.tkv_hbm, ...), custom_call_target="tpu_custom_call" | custom-call | flops 2000000000 | bytes 6307840 | tf_op jit(solution)/shard_map/query_kernel/pallas_call | solution.py:54
  72.0 3.6 %all-to-all-done.3.g_ref = f32[8,128,128]{2,1,0:T(8,128)S(1)} async-done(((f32[8,128,128]{2,1,0:T(8,128)}), f32[8,128,128]{2,1,0:T(8,128)S(1)}, u32[]{:S(2)}, u32[]{:S(2)}) %all-to-all-start.3) | async-done | bytes 524320 | tf_op jit(solution)/shard_map/all_to_all | solution.py:546
  75.6 0.6 gather_kernel.1
  76.2 2.8 %collective-permute-start.2 = (f32[128,128]{1,0:T(8,128)S(1)}, f32[128,128]{1,0:T(8,128)S(1)}, u32[]{:S(2)}, u32[]{:S(2)}) collective-permute-start(f32[128,128]{1,0:T(8,128)S(1)} %get-tuple-element.73.own_ref), channel_id=1, source_target_pairs={{0,16},{2,18},{4,20},{6,22},{8,24},{10,26},{12,28},{14,30},{16,0},... | collective-permute-start | bytes 196616 | tf_op jit(solution)/shard_map/ppermute | solution.py:665
  79.1 3.8 %adjoint_residual_kernel.1 = (bf16[8,256,128]{2,1,0:T(8,128)(2,1)}, bf16[8,256,128]{2,1,0:T(8,128)(2,1)}, f32[8,128]{1,0:T(8,128)S(1)}) custom-call(bf16[256,1024]{1,0:T(8,128)(2,1)} %k_ref.1, f32[8,256]{1,0:T(8,128)} %e_ref.1, bf16[8,256,256]{2,1,0:T(8,128)(2,1)} %get-tuple-element.59.se_hbm, bf16[8,2,128,128]{3,2,1,0:T(8,128)(2,1)} %get-tuple-element.60.t_hbm, ...), custom_call_target="tpu_custom_call" | custom-call | flops 2000000000 | bytes 5783552 | tf_op jit(solution)/shard_map/adjoint_residual_kernel/pallas_call | solution.py:54
  82.9 0.2 pair_gradient_kernel.1
  83.1 9.5 %all_to_all.33.later_ref = f32[4,128,128]{2,1,0:T(8,128)S(1)} all-to-all(f32[4,128,128]{2,1,0:T(8,128)S(1)} %pair_gradient_kernel.1), channel_id=1, replica_groups={{0,32,64,96},{2,34,66,98},{4,36,68,100},{6,38,70,102},{8,40,72,104},{10..., dimensions={0} | all-to-all | bytes 524288 | tf_op jit(solution)/shard_map/all_to_all | solution.py:546
  92.7 1.0 end_kernel.1
  93.6 0.0 copy-start.1
  93.7 11.8 %all_to_all.34.d_ref = f32[8,136,128]{2,1,0:T(8,128)S(1)} all-to-all(f32[8,136,128]{2,1,0:T(8,128)S(1)} %end_kernel.1), channel_id=1, replica_groups={{0,2,4,6,8,10,12,14},{16,18,20,22,24,26,28,30},{32,34,36,38,40,42,44,46..., dimensions={0} | all-to-all | bytes 1114112 | tf_op jit(solution)/shard_map/all_to_all | solution.py:546
  105.6 3.0 %key_kernel.1 = (bf16[256,1024]{1,0:T(8,128)(2,1)}, bf16[256,1024]{1,0:T(8,128)(2,1)}, f32[8,256]{1,0:T(8,128)}, f32[8,256]{1,0:T(8,128)}) custom-call(bf16[256,1024]{1,0:T(8,128)(2,1)S(1)} %copy-done.1, f32[8,256]{1,0:T(8,128)S(1)} %copy-done.2, bf16[8,256,128]{2,1,0:T(8,128)(2,1)S(1)} %copy-done.7, bf16[8,256,128]{2,1,0:T(8,128)(2,1)S(1)} %copy-done.5, ...), custom_call_target="tpu_custom_call" | custom-call | flops 2000000000 | bytes 7421952 | tf_op jit(solution)/shard_map/key_kernel/pallas_call | solution.py:54
  (27 shorter events, 0.1 us)
Async XLA Ops:
  26.3 6.6 %collective-permute-start = (f32[128,256]{1,0:T(8,128)S(1)}, f32[128,256]{1,0:T(8,128)S(1)}, u32[]{:S(2)}, u32[]{:S(2)}) collective-permute-start(f32[128,256]{1,0:T(8,128)S(1)} %get-tuple-element.48.own_ref), channel_id=1, source_target_pairs={{0,16},{2,18},{4,20},{6,22},{8,24},{10,26},{12,28},{14,30},{16,0},... | collective-permute-start | bytes 393224 | tf_op jit(solution)/shard_map/ppermute | solution.py:596
  33.1 13.3 %copy-start.14 = (f32[128,128]{1,0:T(8,128)S(1)}, f32[128,128]{1,0:T(8,128)}, u32[]{:S(2)}) copy-start(f32[128,128]{1,0:T(8,128)} %get-tuple-element.50.init_ref) | copy-start | bytes 196612
  46.4 12.0 %copy-start.3 = (f32[8,256,128]{2,1,0:T(8,128)S(1)}, f32[8,256,128]{2,1,0:T(8,128)}, u32[]{:S(2)}) copy-start(f32[8,256,128]{2,1,0:T(8,128)} %get-tuple-element.45.c_ref) | copy-start | bytes 3145732
  47.2 11.2 %copy-start = (bf16[256,1024]{1,0:T(8,128)(2,1)S(1)}, bf16[256,1024]{1,0:T(8,128)(2,1)}, u32[]{:S(2)}) copy-start(bf16[256,1024]{1,0:T(8,128)(2,1)} %cot_ref.3) | copy-start | bytes 1572868
  47.2 11.2 %copy-start.9 = (bf16[8,256,128]{2,1,0:T(8,128)(2,1)S(1)}, bf16[8,256,128]{2,1,0:T(8,128)(2,1)}, u32[]{:S(2)}) copy-start(bf16[8,256,128]{2,1,0:T(8,128)(2,1)} %get-tuple-element.44.qt_ref) | copy-start | bytes 1572868
  58.5 1.9 %copy-start.8 = (bf16[8,128,256]{2,1,0:T(8,128)(2,1)S(1)}, bf16[8,128,256]{2,1,0:T(8,128)(2,1)}, u32[]{:S(2)}) copy-start(bf16[8,128,256]{2,1,0:T(8,128)(2,1)} %get-tuple-element.55.qtt_ref) | copy-start | bytes 1572868
  59.0 1.4 %collective-permute-start.1 = (f32[256,128]{1,0:T(8,128)S(1)}, f32[256,128]{1,0:T(8,128)S(1)}, u32[]{:S(2)}, u32[]{:S(2)}) collective-permute-start(f32[256,128]{1,0:T(8,128)S(1)} %get-tuple-element.54.own_ref), channel_id=1, source_target_pairs={{0,1},{1,0},{2,3},{3,2},{4,5},{5,4},{6,7},{7,6},{8,9},{9,8},{10,11... | collective-permute-start | bytes 393224 | tf_op jit(solution)/shard_map/ppermute | solution.py:618
  62.2 13.5 %all-to-all-start.3 = ((f32[8,128,128]{2,1,0:T(8,128)}), f32[8,128,128]{2,1,0:T(8,128)S(1)}, u32[]{:S(2)}, u32[]{:S(2)}) async-start(f32[8,128,128]{2,1,0:T(8,128)} %get-tuple-element.69), calls=%async_computation.3 | async-start | bytes 1048576 | tf_op jit(solution)/shard_map/all_to_all | solution.py:546
  67.1 0.8 copy-start.12
  67.9 7.7 %copy-start.13 = (f32[7,128,128]{2,1,0:T(8,128)S(1)}, f32[7,128,128]{2,1,0:T(8,128)}, u32[]{:S(2)}) copy-start(f32[7,128,128]{2,1,0:T(8,128)} %copy-done.12) | copy-start | bytes 1376260
  76.2 6.6 %collective-permute-start.2 = (f32[128,128]{1,0:T(8,128)S(1)}, f32[128,128]{1,0:T(8,128)S(1)}, u32[]{:S(2)}, u32[]{:S(2)}) collective-permute-start(f32[128,128]{1,0:T(8,128)S(1)} %get-tuple-element.73.own_ref), channel_id=1, source_target_pairs={{0,16},{2,18},{4,20},{6,22},{8,24},{10,26},{12,28},{14,30},{16,0},... | collective-permute-start | bytes 196616 | tf_op jit(solution)/shard_map/ppermute | solution.py:665
  79.0 3.8 %copy-start.15 = (f32[128,128]{1,0:T(8,128)S(1)}, f32[128,128]{1,0:T(8,128)}, u32[]{:S(2)}) copy-start(f32[128,128]{1,0:T(8,128)} %get-tuple-element.74.early_ref) | copy-start | bytes 196612
  83.1 9.5 %copy-start.10 = (f32[4,128,128]{2,1,0:T(8,128)S(1)}, f32[4,128,128]{2,1,0:T(8,128)}, u32[]{:S(2)}) copy-start(f32[4,128,128]{2,1,0:T(8,128)} %get-tuple-element.67.after_ref) | copy-start | bytes 786436
  83.1 9.5 %copy-start.11 = (f32[4,128,128]{2,1,0:T(8,128)S(1)}, f32[4,128,128]{2,1,0:T(8,128)}, u32[]{:S(2)}) copy-start(f32[4,128,128]{2,1,0:T(8,128)} %get-tuple-element.68.first_ref) | copy-start | bytes 786436
  92.7 12.9 %copy-start.5 = (bf16[8,256,128]{2,1,0:T(8,128)(2,1)S(1)}, bf16[8,256,128]{2,1,0:T(8,128)(2,1)}, u32[]{:S(2)}) copy-start(bf16[8,256,128]{2,1,0:T(8,128)(2,1)} %get-tuple-element.63.er_ref) | copy-start | bytes 1572868
  92.7 12.9 %copy-start.6 = (bf16[8,256,128]{2,1,0:T(8,128)(2,1)S(1)}, bf16[8,256,128]{2,1,0:T(8,128)(2,1)}, u32[]{:S(2)}) copy-start(bf16[8,256,128]{2,1,0:T(8,128)(2,1)} %get-tuple-element.64.u_ref) | copy-start | bytes 1572868
  92.7 12.9 %copy-start.7 = (bf16[8,256,128]{2,1,0:T(8,128)(2,1)S(1)}, bf16[8,256,128]{2,1,0:T(8,128)(2,1)}, u32[]{:S(2)}) copy-start(bf16[8,256,128]{2,1,0:T(8,128)(2,1)} %get-tuple-element.62.tek_ref) | copy-start | bytes 1572868
  93.6 11.9 %copy-start.1 = (bf16[256,1024]{1,0:T(8,128)(2,1)S(1)}, bf16[256,1024]{1,0:T(8,128)(2,1)}, u32[]{:S(2)}) copy-start(bf16[256,1024]{1,0:T(8,128)(2,1)} %k_ref.1) | copy-start | bytes 1572868
  93.7 11.9 %copy-start.2 = (f32[8,256]{1,0:T(8,128)S(1)}, f32[8,256]{1,0:T(8,128)}, u32[]{:S(2)}) copy-start(f32[8,256]{1,0:T(8,128)} %e_ref.1) | copy-start | bytes 24580
  93.7 11.9 %copy-start.4 = (bf16[8,256,128]{2,1,0:T(8,128)(2,1)S(1)}, bf16[8,256,128]{2,1,0:T(8,128)(2,1)}, u32[]{:S(2)}) copy-start(bf16[8,256,128]{2,1,0:T(8,128)(2,1)} %get-tuple-element.65.dkp_ref) | copy-start | bytes 1572868

commit v6 on v5

--- a/solution.py
+++ b/solution.py
@@ -139,13 +139,15 @@
         value.wait()
     kvs = [jnp.concatenate([ks[h], v_ref[:, columns(h)]], axis=1) for h in range(heads)]
     tops = [low(dot(t, kv[:half])) for t, kv in zip(inverses[::2], kvs)]
+    for h in range(heads):
+        tkv_ref[h, :half] = tops[h]
+    sent.append(copies.start(tkv_ref.at[:, :half], tkv_hbm.at[:, :half]))
     scaled = [low(jnp.transpose(k.astype(F32)) * e) for k, e in zip(ks, es)]
     mids = [low(kv[half:].astype(F32) + dot(c, x)) for kv, c, x in zip(kvs, crosses, tops)]
     bottoms = [low(dot(t, m)) for t, m in zip(inverses[1::2], mids)]
     for h in range(heads):
-        tkv_ref[h, :half] = tops[h]
         tkv_ref[h, half:] = bottoms[h]
-    sent.append(copies.start(tkv_ref, tkv_hbm))
+    sent.append(copies.start(tkv_ref.at[:, half:], tkv_hbm.at[:, half:]))
     for h in range(heads):
         ab = dot(scaled[h], tkv_ref[h])
         ab_ref[h, :, :HEAD] = eye - ab[:, :HEAD]
@@ -503,8 +505,8 @@
     for h in range(heads):
         gi_ref[h : h + 1, :HEAD] = d_ref[h, HEAD : HEAD + 1, :]
         gi_ref[h : h + 1, HEAD:] = d_ref[h, HEAD + 1 : HEAD + 2, :]
-    for first in range(0, heads, BATCH):
-        batch = range(first, first + BATCH)
+    for first in range(0, heads, heads):
+        batch = range(first, first + heads)
         ds = [low(d_ref[h, :HEAD, :]) for h in batch]
         both = [jnp.concatenate([low(w_ref[h]), -d], axis=1) for h, d in zip(batch, ds)]
         ers = [er_ref[h] for h in batch]
@@ -512,7 +514,7 @@
         lows = [low(u) for u in us]
         for h, u in zip(batch, lows):
             dv_ref[:, columns(h)] = -u
-        flat = span(first, first + BATCH)
+        flat = span(first, first + heads)
         copies.start(dv_ref.at[:, flat], dv_hbm.at[:, flat])
         ps = [low(u * er.astype(F32)) for u, er in zip(us, ers)]
         xs = [
@@ -526,8 +528,10 @@
         for h, dk, x, p in zip(batch, dks, xs, ps):
             e = e_ref[h : h + 1, :]
             dk_ref[:, columns(h)] = low(dk - dot(x, k_ref[:, columns(h)]))
+            if h % 2 == 1:
+                flat = span(h - 1, h + 1)
+                copies.start(dk_ref.at[:, flat], dk_hbm.at[:, flat])
             de_ref[h : h + 1, :] = dot_nt(ones, p)[0:1] / (e * e)
-        copies.start(dk_ref.at[:, flat], dk_hbm.at[:, flat])
     for copy in copies.started:
         copy.wait()
 
@@ -570,7 +574,7 @@
             vm(flat, BF16), vm(flat, BF16), vm((heads, n), F32),
             vm(inner, BF16), vm(corner, BF16), vm((heads, n, 2 * HEAD), BF16),
         ],
-        copies=4 + 2 * parts,
+        copies=5 + 2 * parts,
     )
     own_maps = swap(maps, near)
     qt, qt_turned, offset, scores, own_init, prepared = call(
@@ -687,7 +691,7 @@
             (dk_part, "v"), (weights, "v"), (adjoint, "v"),
         ],
         [vm(flat, BF16), vm(flat, BF16)],
-        copies=2 * parts,
+        copies=1 + heads // 2,
     )
     return (normed, grad_queries, grad_keys, grad_values, grad_rates, grad_init)
 

time: 109 us -> 109 us (level)
  no operation moved by 1% of the time
where the time goes in v6:
time: 109 us; the launch traced here: 108 us
  blocking collectives  66.9 us (61%)
  Pallas kernels  25.2 us (23%)
  starting transfers between devices  9.21 us (8%)
  waiting for transfers between devices  5.23 us (5%)
    all_to_all x5, blocking collectives, swap(): return lax.all_to_all(a, 'ctx', 0, 0, axis_index_groups=groups)  66.9 us
    pallas_call x14, Pallas kernels, call(): pl.pallas_call(kernel, out_shape=results, in_specs=[pl.BlockSpec(memory_s...  25.2 us
    all_to_all x1, waiting for transfers between devices, swap(): return lax.all_to_all(a, 'ctx', 0, 0, axis_index_groups=groups)  3.64 us
    all_to_all x1, starting transfers between devices, swap(): return lax.all_to_all(a, 'ctx', 0, 0, axis_index_groups=groups)  3.5 us
    ppermute x1, starting transfers between devices, local(): other_map = lax.ppermute(whole, 'ctx', across)  2.81 us
    ppermute x1, starting transfers between devices, local(): other_grad = lax.ppermute(whole, 'ctx', across)  2.81 us
  transfers between devices with their start and end apart: 4, of which 3 were waited for; matrix products, arithmetic and copies ran while one was open for 0% of the time, Pallas kernels for 12%

profile of v6, /device:TPU:0, one launch (start us, length us, event | category | flops | bytes accessed | tf_op | source)
XLA Modules:
  0.0 108.3 jit_solution(6276140206245866822)
XLA Ops:
  0.6 3.7 %map_kernel.1 = (f32[8,128,256]{2,1,0:T(8,128)S(1)}, bf16[8,2,128,128]{3,2,1,0:T(8,128)(2,1)}, bf16[8,128,128]{2,1,0:T(8,128)(2,1)}, bf16[8,256,256]{2,1,0:T(8,128)(2,1)}) custom-call(bf16[256,1024]{1,0:T(8,128)(2,1)} %k_ref.1, bf16[256,1024]{1,0:T(8,128)(2,1)} %v_hbm.1, f32[8,256]{1,0:T(8,128)} %e_ref.1), custom_call_target="tpu_custom_call" | custom-call | flops 2000000000 | bytes 2113536 | tf_op jit(solution)/shard_map/map_kernel/pallas_call | solution.py:54
  4.3 21.1 %all_to_all.30.ab_ref = f32[8,128,256]{2,1,0:T(8,128)S(1)} all-to-all(f32[8,128,256]{2,1,0:T(8,128)S(1)} %get-tuple-element.46), channel_id=1, replica_groups={{0,2,4,6,8,10,12,14},{16,18,20,22,24,26,28,30},{32,34,36,38,40,42,44,46..., dimensions={0} | all-to-all | bytes 2097152 | tf_op jit(solution)/shard_map/all_to_all | solution.py:550
  25.4 0.8 group_kernel.1
  26.2 2.8 %collective-permute-start = (f32[128,256]{1,0:T(8,128)S(1)}, f32[128,256]{1,0:T(8,128)S(1)}, u32[]{:S(2)}, u32[]{:S(2)}) collective-permute-start(f32[128,256]{1,0:T(8,128)S(1)} %get-tuple-element.48.own_ref), channel_id=1, source_target_pairs={{0,16},{2,18},{4,20},{6,22},{8,24},{10,26},{12,28},{14,30},{16,0},... | collective-permute-start | bytes 393224 | tf_op jit(solution)/shard_map/ppermute | solution.py:600
  29.0 3.5 %prepare_kernel.1 = (bf16[8,256,128]{2,1,0:T(8,128)(2,1)}, bf16[8,128,256]{2,1,0:T(8,128)(2,1)}, f32[8,256,128]{2,1,0:T(8,128)}, bf16[8,256,256]{2,1,0:T(8,128)(...) custom-call(bf16[256,1024]{1,0:T(8,128)(2,1)} %q_hbm.3, bf16[256,1024]{1,0:T(8,128)(2,1)} %k_ref.1, f32[8,256]{1,0:T(8,128)} %e_ref.1, ...), custom_call_target="tpu_custom_call" | custom-call | flops 2000000000 | bytes 5259264 | tf_op jit(solution)/shard_map/prepare_kernel/pallas_call | solution.py:54
  32.5 0.3 collective-permute-done.other_ref.other_map_ref
  32.7 0.2 pair_kernel.1
  33.0 0.0 copy-start.14
  33.0 13.3 %all_to_all.31.pairs_ref = f32[4,128,256]{2,1,0:T(8,128)S(1)} all-to-all(f32[4,128,256]{2,1,0:T(8,128)S(1)} %pair_kernel.1), channel_id=1, replica_groups={{0,32,64,96},{2,34,66,98},{4,36,68,100},{6,38,70,102},{8,40,72,104},{10..., dimensions={0} | all-to-all | bytes 1048576 | tf_op jit(solution)/shard_map/all_to_all | solution.py:550
  46.3 0.8 start_kernel.1
  47.1 0.0 copy-start
  47.1 0.0 copy-start.9
  47.1 11.2 %all_to_all.32.w_ref = f32[8,128,128]{2,1,0:T(8,128)S(1)} all-to-all(f32[8,128,128]{2,1,0:T(8,128)S(1)} %get-tuple-element.52), channel_id=1, replica_groups={{0,2,4,6,8,10,12,14},{16,18,20,22,24,26,28,30},{32,34,36,38,40,42,44,46..., dimensions={0} | all-to-all | bytes 1048576 | tf_op jit(solution)/shard_map/all_to_all | solution.py:550
  58.4 0.0 copy-start.8
  58.4 0.5 hidden_kernel.1
  58.9 0.1 collective-permute-start.1
  59.0 1.3 %collective-permute-done.1.other_ref = f32[256,128]{1,0:T(8,128)S(1)} collective-permute-done((f32[256,128]{1,0:T(8,128)S(1)}, f32[256,128]{1,0:T(8,128)S(1)}, u32[]{:S(2)}, u32[]{:S(2)}) %collective-permute-start.1) | collective-permute-done | bytes 131104 | tf_op jit(solution)/shard_map/ppermute | solution.py:622
  60.3 1.7 %norm_kernel.1 = (bf16[256,1024]{1,0:T(8,128)(2,1)}, bf16[256,1024]{1,0:T(8,128)(2,1)}, f32[8,128,128]{2,1,0:T(8,128)}) custom-call(f32[256,1024]{1,0:T(8,128)S(1)} %get-tuple-element.53.z_ref, bf16[256,1024]{1,0:T(8,128)(2,1)S(1)} %copy-done, f32[1,1024]{1,0:T(1,128)S(1)} %get-tuple-element.51.gain_ref, f32[256,128]{1,0:T(8,128)S(1)} %get-tuple-element.54.own_ref, ...), custom_call_target="tpu_custom_call" | custom-call | flops 2000000000 | bytes 4726784 | tf_op jit(solution)/shard_map/norm_kernel/pallas_call | solution.py:54
  62.0 3.5 %all-to-all-start.3 = ((f32[8,128,128]{2,1,0:T(8,128)}), f32[8,128,128]{2,1,0:T(8,128)S(1)}, u32[]{:S(2)}, u32[]{:S(2)}) async-start(f32[8,128,128]{2,1,0:T(8,128)} %get-tuple-element.69), calls=%async_computation.3 | async-start | bytes 1048576 | tf_op jit(solution)/shard_map/all_to_all | solution.py:550
  65.5 1.5 %adjoint_kernel.1 = (f32[4,128,128]{2,1,0:T(8,128)}, f32[4,128,128]{2,1,0:T(8,128)}, f32[128,128]{1,0:T(8,128)}, f32[7,128,128]{2,1,0:T(8,128)S(1)}) custom-call(f32[4,128,256]{2,1,0:T(8,128)S(1)} %all_to_all.31.pairs_ref, f32[8,128,256]{2,1,0:T(8,128)S(1)} %all_to_all.30.ab_ref, f32[6,128,128]{2,1,0:T(8,128)S(1)} %get-tuple-element.66.factors_ref, ...), custom_call_target="tpu_custom_call" | custom-call | flops 2000000000 | bytes 4194304 | tf_op jit(solution)/shard_map/adjoint_kernel/pallas_call | solution.py:54
  67.0 0.8 copy-done.12
  67.8 4.0 %query_kernel.1 = (bf16[256,1024]{1,0:T(8,128)(2,1)}, bf16[8,256,128]{2,1,0:T(8,128)(2,1)}, bf16[8,256,128]{2,1,0:T(8,128)(2,1)}, f32[8,128]{1,0:T(8,128)S(1)}) custom-call(bf16[256,1024]{1,0:T(8,128)(2,1)} %q_hbm.3, bf16[256,1024]{1,0:T(8,128)(2,1)} %k_ref.1, f32[8,256]{1,0:T(8,128)} %e_ref.1, bf16[8,256,256]{2,1,0:T(8,128)(2,1)} %get-tuple-element.43.tkv_hbm, ...), custom_call_target="tpu_custom_call" | custom-call | flops 2000000000 | bytes 6307840 | tf_op jit(solution)/shard_map/query_kernel/pallas_call | solution.py:54
  71.8 3.6 %all-to-all-done.3.g_ref = f32[8,128,128]{2,1,0:T(8,128)S(1)} async-done(((f32[8,128,128]{2,1,0:T(8,128)}), f32[8,128,128]{2,1,0:T(8,128)S(1)}, u32[]{:S(2)}, u32[]{:S(2)}) %all-to-all-start.3) | async-done | bytes 524320 | tf_op jit(solution)/shard_map/all_to_all | solution.py:550
  75.5 0.6 gather_kernel.1
  76.1 2.8 %collective-permute-start.2 = (f32[128,128]{1,0:T(8,128)S(1)}, f32[128,128]{1,0:T(8,128)S(1)}, u32[]{:S(2)}, u32[]{:S(2)}) collective-permute-start(f32[128,128]{1,0:T(8,128)S(1)} %get-tuple-element.73.own_ref), channel_id=1, source_target_pairs={{0,16},{2,18},{4,20},{6,22},{8,24},{10,26},{12,28},{14,30},{16,0},... | collective-permute-start | bytes 196616 | tf_op jit(solution)/shard_map/ppermute | solution.py:669
  78.9 3.8 %adjoint_residual_kernel.1 = (bf16[8,256,128]{2,1,0:T(8,128)(2,1)}, bf16[8,256,128]{2,1,0:T(8,128)(2,1)}, f32[8,128]{1,0:T(8,128)S(1)}) custom-call(bf16[256,1024]{1,0:T(8,128)(2,1)} %k_ref.1, f32[8,256]{1,0:T(8,128)} %e_ref.1, bf16[8,256,256]{2,1,0:T(8,128)(2,1)} %get-tuple-element.59.se_hbm, bf16[8,2,128,128]{3,2,1,0:T(8,128)(2,1)} %get-tuple-element.60.t_hbm, ...), custom_call_target="tpu_custom_call" | custom-call | flops 2000000000 | bytes 5783552 | tf_op jit(solution)/shard_map/adjoint_residual_kernel/pallas_call | solution.py:54
  82.8 0.2 pair_gradient_kernel.1
  83.0 9.5 %all_to_all.33.later_ref = f32[4,128,128]{2,1,0:T(8,128)S(1)} all-to-all(f32[4,128,128]{2,1,0:T(8,128)S(1)} %pair_gradient_kernel.1), channel_id=1, replica_groups={{0,32,64,96},{2,34,66,98},{4,36,68,100},{6,38,70,102},{8,40,72,104},{10..., dimensions={0} | all-to-all | bytes 524288 | tf_op jit(solution)/shard_map/all_to_all | solution.py:550
  92.5 1.0 end_kernel.1
  93.5 0.0 copy-start.2
  93.5 11.8 %all_to_all.34.d_ref = f32[8,136,128]{2,1,0:T(8,128)S(1)} all-to-all(f32[8,136,128]{2,1,0:T(8,128)S(1)} %end_kernel.1), channel_id=1, replica_groups={{0,2,4,6,8,10,12,14},{16,18,20,22,24,26,28,30},{32,34,36,38,40,42,44,46..., dimensions={0} | all-to-all | bytes 1114112 | tf_op jit(solution)/shard_map/all_to_all | solution.py:550
  105.4 2.9 %key_kernel.1 = (bf16[256,1024]{1,0:T(8,128)(2,1)}, bf16[256,1024]{1,0:T(8,128)(2,1)}, f32[8,256]{1,0:T(8,128)}, f32[8,256]{1,0:T(8,128)}) custom-call(bf16[256,1024]{1,0:T(8,128)(2,1)S(1)} %copy-done.1, f32[8,256]{1,0:T(8,128)S(1)} %copy-done.2, bf16[8,256,128]{2,1,0:T(8,128)(2,1)S(1)} %copy-done.7, bf16[8,256,128]{2,1,0:T(8,128)(2,1)S(1)} %copy-done.5, ...), custom_call_target="tpu_custom_call" | custom-call | flops 2000000000 | bytes 7421952 | tf_op jit(solution)/shard_map/key_kernel/pallas_call | solution.py:54
  (27 shorter events, 0.1 us)
Async XLA Ops:
  26.2 6.6 %collective-permute-start = (f32[128,256]{1,0:T(8,128)S(1)}, f32[128,256]{1,0:T(8,128)S(1)}, u32[]{:S(2)}, u32[]{:S(2)}) collective-permute-start(f32[128,256]{1,0:T(8,128)S(1)} %get-tuple-element.48.own_ref), channel_id=1, source_target_pairs={{0,16},{2,18},{4,20},{6,22},{8,24},{10,26},{12,28},{14,30},{16,0},... | collective-permute-start | bytes 393224 | tf_op jit(solution)/shard_map/ppermute | solution.py:600
  33.0 13.3 %copy-start.14 = (f32[128,128]{1,0:T(8,128)S(1)}, f32[128,128]{1,0:T(8,128)}, u32[]{:S(2)}) copy-start(f32[128,128]{1,0:T(8,128)} %get-tuple-element.50.init_ref) | copy-start | bytes 196612
  46.3 12.0 %copy-start.3 = (f32[8,256,128]{2,1,0:T(8,128)S(1)}, f32[8,256,128]{2,1,0:T(8,128)}, u32[]{:S(2)}) copy-start(f32[8,256,128]{2,1,0:T(8,128)} %get-tuple-element.45.c_ref) | copy-start | bytes 3145732
  47.1 11.2 %copy-start = (bf16[256,1024]{1,0:T(8,128)(2,1)S(1)}, bf16[256,1024]{1,0:T(8,128)(2,1)}, u32[]{:S(2)}) copy-start(bf16[256,1024]{1,0:T(8,128)(2,1)} %cot_ref.3) | copy-start | bytes 1572868
  47.1 11.2 %copy-start.9 = (bf16[8,256,128]{2,1,0:T(8,128)(2,1)S(1)}, bf16[8,256,128]{2,1,0:T(8,128)(2,1)}, u32[]{:S(2)}) copy-start(bf16[8,256,128]{2,1,0:T(8,128)(2,1)} %get-tuple-element.44.qt_ref) | copy-start | bytes 1572868
  58.4 1.9 %copy-start.8 = (bf16[8,128,256]{2,1,0:T(8,128)(2,1)S(1)}, bf16[8,128,256]{2,1,0:T(8,128)(2,1)}, u32[]{:S(2)}) copy-start(bf16[8,128,256]{2,1,0:T(8,128)(2,1)} %get-tuple-element.55.qtt_ref) | copy-start | bytes 1572868
  58.9 1.4 %collective-permute-start.1 = (f32[256,128]{1,0:T(8,128)S(1)}, f32[256,128]{1,0:T(8,128)S(1)}, u32[]{:S(2)}, u32[]{:S(2)}) collective-permute-start(f32[256,128]{1,0:T(8,128)S(1)} %get-tuple-element.54.own_ref), channel_id=1, source_target_pairs={{0,1},{1,0},{2,3},{3,2},{4,5},{5,4},{6,7},{7,6},{8,9},{9,8},{10,11... | collective-permute-start | bytes 393224 | tf_op jit(solution)/shard_map/ppermute | solution.py:622
  62.0 13.5 %all-to-all-start.3 = ((f32[8,128,128]{2,1,0:T(8,128)}), f32[8,128,128]{2,1,0:T(8,128)S(1)}, u32[]{:S(2)}, u32[]{:S(2)}) async-start(f32[8,128,128]{2,1,0:T(8,128)} %get-tuple-element.69), calls=%async_computation.3 | async-start | bytes 1048576 | tf_op jit(solution)/shard_map/all_to_all | solution.py:550
  67.0 0.8 copy-start.12
  67.8 7.7 %copy-start.13 = (f32[7,128,128]{2,1,0:T(8,128)S(1)}, f32[7,128,128]{2,1,0:T(8,128)}, u32[]{:S(2)}) copy-start(f32[7,128,128]{2,1,0:T(8,128)} %copy-done.12) | copy-start | bytes 1376260
  76.1 6.6 %collective-permute-start.2 = (f32[128,128]{1,0:T(8,128)S(1)}, f32[128,128]{1,0:T(8,128)S(1)}, u32[]{:S(2)}, u32[]{:S(2)}) collective-permute-start(f32[128,128]{1,0:T(8,128)S(1)} %get-tuple-element.73.own_ref), channel_id=1, source_target_pairs={{0,16},{2,18},{4,20},{6,22},{8,24},{10,26},{12,28},{14,30},{16,0},... | collective-permute-start | bytes 196616 | tf_op jit(solution)/shard_map/ppermute | solution.py:669
  78.9 3.8 %copy-start.15 = (f32[128,128]{1,0:T(8,128)S(1)}, f32[128,128]{1,0:T(8,128)}, u32[]{:S(2)}) copy-start(f32[128,128]{1,0:T(8,128)} %get-tuple-element.74.early_ref) | copy-start | bytes 196612
  83.0 9.5 %copy-start.10 = (f32[4,128,128]{2,1,0:T(8,128)S(1)}, f32[4,128,128]{2,1,0:T(8,128)}, u32[]{:S(2)}) copy-start(f32[4,128,128]{2,1,0:T(8,128)} %get-tuple-element.67.after_ref) | copy-start | bytes 786436
  83.0 9.5 %copy-start.11 = (f32[4,128,128]{2,1,0:T(8,128)S(1)}, f32[4,128,128]{2,1,0:T(8,128)}, u32[]{:S(2)}) copy-start(f32[4,128,128]{2,1,0:T(8,128)} %get-tuple-element.68.first_ref) | copy-start | bytes 786436
  92.5 12.9 %copy-start.5 = (bf16[8,256,128]{2,1,0:T(8,128)(2,1)S(1)}, bf16[8,256,128]{2,1,0:T(8,128)(2,1)}, u32[]{:S(2)}) copy-start(bf16[8,256,128]{2,1,0:T(8,128)(2,1)} %get-tuple-element.63.er_ref) | copy-start | bytes 1572868
  92.5 12.9 %copy-start.6 = (bf16[8,256,128]{2,1,0:T(8,128)(2,1)S(1)}, bf16[8,256,128]{2,1,0:T(8,128)(2,1)}, u32[]{:S(2)}) copy-start(bf16[8,256,128]{2,1,0:T(8,128)(2,1)} %get-tuple-element.64.u_ref) | copy-start | bytes 1572868
  92.5 12.9 %copy-start.7 = (bf16[8,256,128]{2,1,0:T(8,128)(2,1)S(1)}, bf16[8,256,128]{2,1,0:T(8,128)(2,1)}, u32[]{:S(2)}) copy-start(bf16[8,256,128]{2,1,0:T(8,128)(2,1)} %get-tuple-element.62.tek_ref) | copy-start | bytes 1572868
  93.5 11.9 %copy-start.1 = (bf16[256,1024]{1,0:T(8,128)(2,1)S(1)}, bf16[256,1024]{1,0:T(8,128)(2,1)}, u32[]{:S(2)}) copy-start(bf16[256,1024]{1,0:T(8,128)(2,1)} %k_ref.1) | copy-start | bytes 1572868
  93.5 11.9 %copy-start.2 = (f32[8,256]{1,0:T(8,128)S(1)}, f32[8,256]{1,0:T(8,128)}, u32[]{:S(2)}) copy-start(f32[8,256]{1,0:T(8,128)} %e_ref.1) | copy-start | bytes 24580
  93.5 11.9 %copy-start.4 = (bf16[8,256,128]{2,1,0:T(8,128)(2,1)S(1)}, bf16[8,256,128]{2,1,0:T(8,128)(2,1)}, u32[]{:S(2)}) copy-start(bf16[8,256,128]{2,1,0:T(8,128)(2,1)} %get-tuple-element.65.dkp_ref) | copy-start | bytes 1572868

commit v7 on v6

--- a/solution.py
+++ b/solution.py
@@ -351,12 +351,10 @@
         z_ref[:, columns(h)] = z
         squares += z * z
         products += z * (cot_ref[:, columns(h)].astype(F32) * gain_ref[:, columns(h)])
-    lane = lax.broadcasted_iota(jnp.int32, (n, HEAD), 1)
-    stats_ref[...] = jnp.where(
-        lane < HEAD // 2,
-        jnp.sum(squares, axis=1, keepdims=True),
-        jnp.sum(products, axis=1, keepdims=True),
-    )
+    ones = jnp.ones((8, HEAD), BF16)
+    sums = [dot_nt(ones, high) + dot_nt(ones, rest) for high, rest in map(halves, (squares, products))]
+    place = lax.broadcasted_iota(jnp.int32, (8, n), 0)
+    stats_ref[...] = jnp.where(place < 4, sums[0], sums[1])
 
 
 def norm_kernel(
@@ -367,8 +365,11 @@
     width = 2 * z_ref.shape[1]
     copies = Copies(sems)
     stats = own_ref[...] + other_ref[...]
-    inv = lax.rsqrt(stats[:, 0:1] / width + EPSILON)
-    shift = inv * inv * inv * stats[:, HEAD // 2 : HEAD // 2 + 1] / width
+    inv = lax.rsqrt(stats[0:1] / width + EPSILON)
+    shift = inv * inv * inv * stats[4:5] / width
+    inv, shift = (
+        jnp.transpose(jnp.broadcast_to(a, (HEAD, a.shape[1]))) for a in (inv, shift)
+    )
     for h in range(heads):
         go = cot_ref[:, columns(h)].astype(F32) * gain_ref[:, columns(h)]
         dz = low(inv * go - z_ref[:, columns(h)] * shift)
@@ -616,7 +617,7 @@
     weights = swap(starts, near)
     hidden, stats = call(
         hidden_kernel,
-        [(flat, F32, "v"), ((n, HEAD), F32, "v")],
+        [(flat, F32, "v"), ((8, n), F32, "v")],
         [(qt, "v"), (offset, "v"), (cotangent, "v"), (gain_row, "v"), (weights, "v")],
     )
     other = lax.ppermute(stats, "tensor", [(0, 1), (1, 0)])

time: 109 us -> 109 us (level)
  no operation moved by 1% of the time
where the time goes in v7:
time: 109 us; the launch traced here: 108 us
  blocking collectives  66.9 us (61%)
  Pallas kernels  25.2 us (23%)
  starting transfers between devices  9.13 us (8%)
  waiting for transfers between devices  5.11 us (5%)
    all_to_all x5, blocking collectives, swap(): return lax.all_to_all(a, 'ctx', 0, 0, axis_index_groups=groups)  66.9 us
    pallas_call x14, Pallas kernels, call(): pl.pallas_call(kernel, out_shape=results, in_specs=[pl.BlockSpec(memory_s...  25.2 us
    all_to_all x1, waiting for transfers between devices, swap(): return lax.all_to_all(a, 'ctx', 0, 0, axis_index_groups=groups)  3.66 us
    all_to_all x1, starting transfers between devices, swap(): return lax.all_to_all(a, 'ctx', 0, 0, axis_index_groups=groups)  3.5 us
    ppermute x1, starting transfers between devices, local(): other_map = lax.ppermute(whole, 'ctx', across)  2.81 us
    ppermute x1, starting transfers between devices, local(): other_grad = lax.ppermute(whole, 'ctx', across)  2.81 us
  transfers between devices with their start and end apart: 4, of which 3 were waited for; matrix products, arithmetic and copies ran while one was open for 0% of the time, Pallas kernels for 12%

profile of v7, /device:TPU:0, one launch (start us, length us, event | category | flops | bytes accessed | tf_op | source)
XLA Modules:
  0.0 108.1 jit_solution(15570915919047152458)
XLA Ops:
  0.6 3.7 %map_kernel.1 = (f32[8,128,256]{2,1,0:T(8,128)S(1)}, bf16[8,2,128,128]{3,2,1,0:T(8,128)(2,1)}, bf16[8,128,128]{2,1,0:T(8,128)(2,1)}, bf16[8,256,256]{2,1,0:T(8,128)(2,1)}) custom-call(bf16[256,1024]{1,0:T(8,128)(2,1)} %k_ref.1, bf16[256,1024]{1,0:T(8,128)(2,1)} %v_hbm.1, f32[8,256]{1,0:T(8,128)} %e_ref.1), custom_call_target="tpu_custom_call" | custom-call | flops 2000000000 | bytes 2113536 | tf_op jit(solution)/shard_map/map_kernel/pallas_call | solution.py:54
  4.3 21.1 %all_to_all.30.ab_ref = f32[8,128,256]{2,1,0:T(8,128)S(1)} all-to-all(f32[8,128,256]{2,1,0:T(8,128)S(1)} %get-tuple-element.46), channel_id=1, replica_groups={{0,2,4,6,8,10,12,14},{16,18,20,22,24,26,28,30},{32,34,36,38,40,42,44,46..., dimensions={0} | all-to-all | bytes 2097152 | tf_op jit(solution)/shard_map/all_to_all | solution.py:551
  25.4 0.8 group_kernel.1
  26.2 2.8 %collective-permute-start = (f32[128,256]{1,0:T(8,128)S(1)}, f32[128,256]{1,0:T(8,128)S(1)}, u32[]{:S(2)}, u32[]{:S(2)}) collective-permute-start(f32[128,256]{1,0:T(8,128)S(1)} %get-tuple-element.48.own_ref), channel_id=1, source_target_pairs={{0,16},{2,18},{4,20},{6,22},{8,24},{10,26},{12,28},{14,30},{16,0},... | collective-permute-start | bytes 393224 | tf_op jit(solution)/shard_map/ppermute | solution.py:601
  29.0 3.5 %prepare_kernel.1 = (bf16[8,256,128]{2,1,0:T(8,128)(2,1)}, bf16[8,128,256]{2,1,0:T(8,128)(2,1)}, f32[8,256,128]{2,1,0:T(8,128)}, bf16[8,256,256]{2,1,0:T(8,128)(...) custom-call(bf16[256,1024]{1,0:T(8,128)(2,1)} %q_hbm.3, bf16[256,1024]{1,0:T(8,128)(2,1)} %k_ref.1, f32[8,256]{1,0:T(8,128)} %e_ref.1, ...), custom_call_target="tpu_custom_call" | custom-call | flops 2000000000 | bytes 5259264 | tf_op jit(solution)/shard_map/prepare_kernel/pallas_call | solution.py:54
  32.5 0.3 collective-permute-done.other_ref.other_map_ref
  32.7 0.2 pair_kernel.1
  33.0 0.0 copy-start.14
  33.0 13.3 %all_to_all.31.pairs_ref = f32[4,128,256]{2,1,0:T(8,128)S(1)} all-to-all(f32[4,128,256]{2,1,0:T(8,128)S(1)} %pair_kernel.1), channel_id=1, replica_groups={{0,32,64,96},{2,34,66,98},{4,36,68,100},{6,38,70,102},{8,40,72,104},{10..., dimensions={0} | all-to-all | bytes 1048576 | tf_op jit(solution)/shard_map/all_to_all | solution.py:551
  46.3 0.8 start_kernel.1
  47.1 0.0 copy-start
  47.1 0.0 copy-start.9
  47.1 11.2 %all_to_all.32.w_ref = f32[8,128,128]{2,1,0:T(8,128)S(1)} all-to-all(f32[8,128,128]{2,1,0:T(8,128)S(1)} %get-tuple-element.52), channel_id=1, replica_groups={{0,2,4,6,8,10,12,14},{16,18,20,22,24,26,28,30},{32,34,36,38,40,42,44,46..., dimensions={0} | all-to-all | bytes 1048576 | tf_op jit(solution)/shard_map/all_to_all | solution.py:551
  58.4 0.0 copy-start.8
  58.4 0.6 hidden_kernel.1
  58.9 1.2 %collective-permute-done.1.other_ref = f32[8,256]{1,0:T(8,128)S(1)} collective-permute-done((f32[8,256]{1,0:T(8,128)S(1)}, f32[8,256]{1,0:T(8,128)S(1)}, u32[]{:S(2)}, u32[]{:S(2)}) %collective-permute-start.1) | collective-permute-done | bytes 8224 | tf_op jit(solution)/shard_map/ppermute | solution.py:623
  60.1 1.7 %norm_kernel.1 = (bf16[256,1024]{1,0:T(8,128)(2,1)}, bf16[256,1024]{1,0:T(8,128)(2,1)}, f32[8,128,128]{2,1,0:T(8,128)}) custom-call(f32[256,1024]{1,0:T(8,128)S(1)} %get-tuple-element.53.z_ref, bf16[256,1024]{1,0:T(8,128)(2,1)S(1)} %copy-done, f32[1,1024]{1,0:T(1,128)S(1)} %get-tuple-element.51.gain_ref, f32[8,256]{1,0:T(8,128)S(1)} %get-tuple-element.54.own_ref, ...), custom_call_target="tpu_custom_call" | custom-call | flops 2000000000 | bytes 4235264 | tf_op jit(solution)/shard_map/norm_kernel/pallas_call | solution.py:54
  61.8 3.5 %all-to-all-start.3 = ((f32[8,128,128]{2,1,0:T(8,128)}), f32[8,128,128]{2,1,0:T(8,128)S(1)}, u32[]{:S(2)}, u32[]{:S(2)}) async-start(f32[8,128,128]{2,1,0:T(8,128)} %get-tuple-element.69), calls=%async_computation.3 | async-start | bytes 1048576 | tf_op jit(solution)/shard_map/all_to_all | solution.py:551
  65.3 1.5 %adjoint_kernel.1 = (f32[4,128,128]{2,1,0:T(8,128)}, f32[4,128,128]{2,1,0:T(8,128)}, f32[128,128]{1,0:T(8,128)}, f32[7,128,128]{2,1,0:T(8,128)S(1)}) custom-call(f32[4,128,256]{2,1,0:T(8,128)S(1)} %all_to_all.31.pairs_ref, f32[8,128,256]{2,1,0:T(8,128)S(1)} %all_to_all.30.ab_ref, f32[6,128,128]{2,1,0:T(8,128)S(1)} %get-tuple-element.66.factors_ref, ...), custom_call_target="tpu_custom_call" | custom-call | flops 2000000000 | bytes 4194304 | tf_op jit(solution)/shard_map/adjoint_kernel/pallas_call | solution.py:54
  66.8 0.8 copy-done.12
  67.6 4.0 %query_kernel.1 = (bf16[256,1024]{1,0:T(8,128)(2,1)}, bf16[8,256,128]{2,1,0:T(8,128)(2,1)}, bf16[8,256,128]{2,1,0:T(8,128)(2,1)}, f32[8,128]{1,0:T(8,128)S(1)}) custom-call(bf16[256,1024]{1,0:T(8,128)(2,1)} %q_hbm.3, bf16[256,1024]{1,0:T(8,128)(2,1)} %k_ref.1, f32[8,256]{1,0:T(8,128)} %e_ref.1, bf16[8,256,256]{2,1,0:T(8,128)(2,1)} %get-tuple-element.43.tkv_hbm, ...), custom_call_target="tpu_custom_call" | custom-call | flops 2000000000 | bytes 6307840 | tf_op jit(solution)/shard_map/query_kernel/pallas_call | solution.py:54
  71.7 3.7 %all-to-all-done.3.g_ref = f32[8,128,128]{2,1,0:T(8,128)S(1)} async-done(((f32[8,128,128]{2,1,0:T(8,128)}), f32[8,128,128]{2,1,0:T(8,128)S(1)}, u32[]{:S(2)}, u32[]{:S(2)}) %all-to-all-start.3) | async-done | bytes 524320 | tf_op jit(solution)/shard_map/all_to_all | solution.py:551
  75.3 0.6 gather_kernel.1
  75.9 2.8 %collective-permute-start.2 = (f32[128,128]{1,0:T(8,128)S(1)}, f32[128,128]{1,0:T(8,128)S(1)}, u32[]{:S(2)}, u32[]{:S(2)}) collective-permute-start(f32[128,128]{1,0:T(8,128)S(1)} %get-tuple-element.73.own_ref), channel_id=1, source_target_pairs={{0,16},{2,18},{4,20},{6,22},{8,24},{10,26},{12,28},{14,30},{16,0},... | collective-permute-start | bytes 196616 | tf_op jit(solution)/shard_map/ppermute | solution.py:670
  78.7 3.8 %adjoint_residual_kernel.1 = (bf16[8,256,128]{2,1,0:T(8,128)(2,1)}, bf16[8,256,128]{2,1,0:T(8,128)(2,1)}, f32[8,128]{1,0:T(8,128)S(1)}) custom-call(bf16[256,1024]{1,0:T(8,128)(2,1)} %k_ref.1, f32[8,256]{1,0:T(8,128)} %e_ref.1, bf16[8,256,256]{2,1,0:T(8,128)(2,1)} %get-tuple-element.59.se_hbm, bf16[8,2,128,128]{3,2,1,0:T(8,128)(2,1)} %get-tuple-element.60.t_hbm, ...), custom_call_target="tpu_custom_call" | custom-call | flops 2000000000 | bytes 5783552 | tf_op jit(solution)/shard_map/adjoint_residual_kernel/pallas_call | solution.py:54
  82.6 0.2 pair_gradient_kernel.1
  82.8 9.5 %all_to_all.33.later_ref = f32[4,128,128]{2,1,0:T(8,128)S(1)} all-to-all(f32[4,128,128]{2,1,0:T(8,128)S(1)} %pair_gradient_kernel.1), channel_id=1, replica_groups={{0,32,64,96},{2,34,66,98},{4,36,68,100},{6,38,70,102},{8,40,72,104},{10..., dimensions={0} | all-to-all | bytes 524288 | tf_op jit(solution)/shard_map/all_to_all | solution.py:551
  92.4 1.0 end_kernel.1
  93.3 0.0 copy-start.1
  93.4 0.0 copy-start.2
  93.4 11.8 %all_to_all.34.d_ref = f32[8,136,128]{2,1,0:T(8,128)S(1)} all-to-all(f32[8,136,128]{2,1,0:T(8,128)S(1)} %end_kernel.1), channel_id=1, replica_groups={{0,2,4,6,8,10,12,14},{16,18,20,22,24,26,28,30},{32,34,36,38,40,42,44,46..., dimensions={0} | all-to-all | bytes 1114112 | tf_op jit(solution)/shard_map/all_to_all | solution.py:551
  105.2 2.9 %key_kernel.1 = (bf16[256,1024]{1,0:T(8,128)(2,1)}, bf16[256,1024]{1,0:T(8,128)(2,1)}, f32[8,256]{1,0:T(8,128)}, f32[8,256]{1,0:T(8,128)}) custom-call(bf16[256,1024]{1,0:T(8,128)(2,1)S(1)} %copy-done.1, f32[8,256]{1,0:T(8,128)S(1)} %copy-done.2, bf16[8,256,128]{2,1,0:T(8,128)(2,1)S(1)} %copy-done.7, bf16[8,256,128]{2,1,0:T(8,128)(2,1)S(1)} %copy-done.5, ...), custom_call_target="tpu_custom_call" | custom-call | flops 2000000000 | bytes 7421952 | tf_op jit(solution)/shard_map/key_kernel/pallas_call | solution.py:54
  (27 shorter events, 0.1 us)
Async XLA Ops:
  26.2 6.6 %collective-permute-start = (f32[128,256]{1,0:T(8,128)S(1)}, f32[128,256]{1,0:T(8,128)S(1)}, u32[]{:S(2)}, u32[]{:S(2)}) collective-permute-start(f32[128,256]{1,0:T(8,128)S(1)} %get-tuple-element.48.own_ref), channel_id=1, source_target_pairs={{0,16},{2,18},{4,20},{6,22},{8,24},{10,26},{12,28},{14,30},{16,0},... | collective-permute-start | bytes 393224 | tf_op jit(solution)/shard_map/ppermute | solution.py:601
  33.0 13.3 %copy-start.14 = (f32[128,128]{1,0:T(8,128)S(1)}, f32[128,128]{1,0:T(8,128)}, u32[]{:S(2)}) copy-start(f32[128,128]{1,0:T(8,128)} %get-tuple-element.50.init_ref) | copy-start | bytes 196612
  46.3 12.0 %copy-start.3 = (f32[8,256,128]{2,1,0:T(8,128)S(1)}, f32[8,256,128]{2,1,0:T(8,128)}, u32[]{:S(2)}) copy-start(f32[8,256,128]{2,1,0:T(8,128)} %get-tuple-element.45.c_ref) | copy-start | bytes 3145732
  47.1 11.2 %copy-start = (bf16[256,1024]{1,0:T(8,128)(2,1)S(1)}, bf16[256,1024]{1,0:T(8,128)(2,1)}, u32[]{:S(2)}) copy-start(bf16[256,1024]{1,0:T(8,128)(2,1)} %cot_ref.3) | copy-start | bytes 1572868
  47.1 11.2 %copy-start.9 = (bf16[8,256,128]{2,1,0:T(8,128)(2,1)S(1)}, bf16[8,256,128]{2,1,0:T(8,128)(2,1)}, u32[]{:S(2)}) copy-start(bf16[8,256,128]{2,1,0:T(8,128)(2,1)} %get-tuple-element.44.qt_ref) | copy-start | bytes 1572868
  58.4 1.8 %copy-start.8 = (bf16[8,128,256]{2,1,0:T(8,128)(2,1)S(1)}, bf16[8,128,256]{2,1,0:T(8,128)(2,1)}, u32[]{:S(2)}) copy-start(bf16[8,128,256]{2,1,0:T(8,128)(2,1)} %get-tuple-element.55.qtt_ref) | copy-start | bytes 1572868
  58.9 1.2 %collective-permute-start.1 = (f32[8,256]{1,0:T(8,128)S(1)}, f32[8,256]{1,0:T(8,128)S(1)}, u32[]{:S(2)}, u32[]{:S(2)}) collective-permute-start(f32[8,256]{1,0:T(8,128)S(1)} %get-tuple-element.54.own_ref), channel_id=1, source_target_pairs={{0,1},{1,0},{2,3},{3,2},{4,5},{5,4},{6,7},{7,6},{8,9},{9,8},{10,11... | collective-permute-start | bytes 24584 | tf_op jit(solution)/shard_map/ppermute | solution.py:623
  61.8 13.5 %all-to-all-start.3 = ((f32[8,128,128]{2,1,0:T(8,128)}), f32[8,128,128]{2,1,0:T(8,128)S(1)}, u32[]{:S(2)}, u32[]{:S(2)}) async-start(f32[8,128,128]{2,1,0:T(8,128)} %get-tuple-element.69), calls=%async_computation.3 | async-start | bytes 1048576 | tf_op jit(solution)/shard_map/all_to_all | solution.py:551
  66.8 0.8 copy-start.12
  67.6 7.7 %copy-start.13 = (f32[7,128,128]{2,1,0:T(8,128)S(1)}, f32[7,128,128]{2,1,0:T(8,128)}, u32[]{:S(2)}) copy-start(f32[7,128,128]{2,1,0:T(8,128)} %copy-done.12) | copy-start | bytes 1376260
  75.9 6.6 %collective-permute-start.2 = (f32[128,128]{1,0:T(8,128)S(1)}, f32[128,128]{1,0:T(8,128)S(1)}, u32[]{:S(2)}, u32[]{:S(2)}) collective-permute-start(f32[128,128]{1,0:T(8,128)S(1)} %get-tuple-element.73.own_ref), channel_id=1, source_target_pairs={{0,16},{2,18},{4,20},{6,22},{8,24},{10,26},{12,28},{14,30},{16,0},... | collective-permute-start | bytes 196616 | tf_op jit(solution)/shard_map/ppermute | solution.py:670
  78.7 3.8 %copy-start.15 = (f32[128,128]{1,0:T(8,128)S(1)}, f32[128,128]{1,0:T(8,128)}, u32[]{:S(2)}) copy-start(f32[128,128]{1,0:T(8,128)} %get-tuple-element.74.early_ref) | copy-start | bytes 196612
  82.8 9.5 %copy-start.10 = (f32[4,128,128]{2,1,0:T(8,128)S(1)}, f32[4,128,128]{2,1,0:T(8,128)}, u32[]{:S(2)}) copy-start(f32[4,128,128]{2,1,0:T(8,128)} %get-tuple-element.67.after_ref) | copy-start | bytes 786436
  82.8 9.5 %copy-start.11 = (f32[4,128,128]{2,1,0:T(8,128)S(1)}, f32[4,128,128]{2,1,0:T(8,128)}, u32[]{:S(2)}) copy-start(f32[4,128,128]{2,1,0:T(8,128)} %get-tuple-element.68.first_ref) | copy-start | bytes 786436
  92.3 12.9 %copy-start.5 = (bf16[8,256,128]{2,1,0:T(8,128)(2,1)S(1)}, bf16[8,256,128]{2,1,0:T(8,128)(2,1)}, u32[]{:S(2)}) copy-start(bf16[8,256,128]{2,1,0:T(8,128)(2,1)} %get-tuple-element.63.er_ref) | copy-start | bytes 1572868
  92.3 12.9 %copy-start.6 = (bf16[8,256,128]{2,1,0:T(8,128)(2,1)S(1)}, bf16[8,256,128]{2,1,0:T(8,128)(2,1)}, u32[]{:S(2)}) copy-start(bf16[8,256,128]{2,1,0:T(8,128)(2,1)} %get-tuple-element.64.u_ref) | copy-start | bytes 1572868
  92.4 12.9 %copy-start.7 = (bf16[8,256,128]{2,1,0:T(8,128)(2,1)S(1)}, bf16[8,256,128]{2,1,0:T(8,128)(2,1)}, u32[]{:S(2)}) copy-start(bf16[8,256,128]{2,1,0:T(8,128)(2,1)} %get-tuple-element.62.tek_ref) | copy-start | bytes 1572868
  93.3 11.9 %copy-start.1 = (bf16[256,1024]{1,0:T(8,128)(2,1)S(1)}, bf16[256,1024]{1,0:T(8,128)(2,1)}, u32[]{:S(2)}) copy-start(bf16[256,1024]{1,0:T(8,128)(2,1)} %k_ref.1) | copy-start | bytes 1572868
  93.4 11.9 %copy-start.2 = (f32[8,256]{1,0:T(8,128)S(1)}, f32[8,256]{1,0:T(8,128)}, u32[]{:S(2)}) copy-start(f32[8,256]{1,0:T(8,128)} %e_ref.1) | copy-start | bytes 24580
  93.4 11.9 %copy-start.4 = (bf16[8,256,128]{2,1,0:T(8,128)(2,1)S(1)}, bf16[8,256,128]{2,1,0:T(8,128)(2,1)}, u32[]{:S(2)}) copy-start(bf16[8,256,128]{2,1,0:T(8,128)(2,1)} %get-tuple-element.65.dkp_ref) | copy-start | bytes 1572868

commit v8 on v7

--- a/solution.py
+++ b/solution.py
@@ -135,6 +135,7 @@
         n_ref[h] = crosses[h]
     sent.append(copies.start(t_ref, t_hbm))
     sent.append(copies.start(n_ref, n_hbm))
+    scaled = [low(jnp.transpose(k.astype(F32)) * e) for k, e in zip(ks, es)]
     for _, value in arrivals:
         value.wait()
     kvs = [jnp.concatenate([ks[h], v_ref[:, columns(h)]], axis=1) for h in range(heads)]
@@ -142,7 +143,6 @@
     for h in range(heads):
         tkv_ref[h, :half] = tops[h]
     sent.append(copies.start(tkv_ref.at[:, :half], tkv_hbm.at[:, :half]))
-    scaled = [low(jnp.transpose(k.astype(F32)) * e) for k, e in zip(ks, es)]
     mids = [low(kv[half:].astype(F32) + dot(c, x)) for kv, c, x in zip(kvs, crosses, tops)]
     bottoms = [low(dot(t, m)) for t, m in zip(inverses[1::2], mids)]
     for h in range(heads):

time: 109 us -> 109 us (level)
  no operation moved by 1% of the time
where the time goes in v8:
time: 109 us; the launch traced here: 108 us
  blocking collectives  66.9 us (61%)
  Pallas kernels  25.3 us (23%)
  starting transfers between devices  9.13 us (8%)
  waiting for transfers between devices  5.12 us (5%)
    all_to_all x5, blocking collectives, swap(): return lax.all_to_all(a, 'ctx', 0, 0, axis_index_groups=groups)  66.9 us
    pallas_call x14, Pallas kernels, call(): pl.pallas_call(kernel, out_shape=results, in_specs=[pl.BlockSpec(memory_s...  25.3 us
    all_to_all x1, waiting for transfers between devices, swap(): return lax.all_to_all(a, 'ctx', 0, 0, axis_index_groups=groups)  3.66 us
    all_to_all x1, starting transfers between devices, swap(): return lax.all_to_all(a, 'ctx', 0, 0, axis_index_groups=groups)  3.5 us
    ppermute x1, starting transfers between devices, local(): other_grad = lax.ppermute(whole, 'ctx', across)  2.82 us
    ppermute x1, starting transfers between devices, local(): other_map = lax.ppermute(whole, 'ctx', across)  2.8 us
  transfers between devices with their start and end apart: 4, of which 3 were waited for; matrix products, arithmetic and copies ran while one was open for 0% of the time, Pallas kernels for 12%

profile of v8, /device:TPU:0, one launch (start us, length us, event | category | flops | bytes accessed | tf_op | source)
XLA Modules:
  0.0 108.2 jit_solution(1612822468032097660)
XLA Ops:
  0.6 3.8 %map_kernel.1 = (f32[8,128,256]{2,1,0:T(8,128)S(1)}, bf16[8,2,128,128]{3,2,1,0:T(8,128)(2,1)}, bf16[8,128,128]{2,1,0:T(8,128)(2,1)}, bf16[8,256,256]{2,1,0:T(8,128)(2,1)}) custom-call(bf16[256,1024]{1,0:T(8,128)(2,1)} %k_ref.1, bf16[256,1024]{1,0:T(8,128)(2,1)} %v_hbm.1, f32[8,256]{1,0:T(8,128)} %e_ref.1), custom_call_target="tpu_custom_call" | custom-call | flops 2000000000 | bytes 2113536 | tf_op jit(solution)/shard_map/map_kernel/pallas_call | solution.py:54
  4.4 21.1 %all_to_all.30.ab_ref = f32[8,128,256]{2,1,0:T(8,128)S(1)} all-to-all(f32[8,128,256]{2,1,0:T(8,128)S(1)} %get-tuple-element.46), channel_id=1, replica_groups={{0,2,4,6,8,10,12,14},{16,18,20,22,24,26,28,30},{32,34,36,38,40,42,44,46..., dimensions={0} | all-to-all | bytes 2097152 | tf_op jit(solution)/shard_map/all_to_all | solution.py:551
  25.4 0.8 group_kernel.1
  26.2 2.8 %collective-permute-start = (f32[128,256]{1,0:T(8,128)S(1)}, f32[128,256]{1,0:T(8,128)S(1)}, u32[]{:S(2)}, u32[]{:S(2)}) collective-permute-start(f32[128,256]{1,0:T(8,128)S(1)} %get-tuple-element.48.own_ref), channel_id=1, source_target_pairs={{0,16},{2,18},{4,20},{6,22},{8,24},{10,26},{12,28},{14,30},{16,0},... | collective-permute-start | bytes 393224 | tf_op jit(solution)/shard_map/ppermute | solution.py:601
  29.0 3.5 %prepare_kernel.1 = (bf16[8,256,128]{2,1,0:T(8,128)(2,1)}, bf16[8,128,256]{2,1,0:T(8,128)(2,1)}, f32[8,256,128]{2,1,0:T(8,128)}, bf16[8,256,256]{2,1,0:T(8,128)(...) custom-call(bf16[256,1024]{1,0:T(8,128)(2,1)} %q_hbm.3, bf16[256,1024]{1,0:T(8,128)(2,1)} %k_ref.1, f32[8,256]{1,0:T(8,128)} %e_ref.1, ...), custom_call_target="tpu_custom_call" | custom-call | flops 2000000000 | bytes 5259264 | tf_op jit(solution)/shard_map/prepare_kernel/pallas_call | solution.py:54
  32.5 0.3 collective-permute-done.other_ref.other_map_ref
  32.8 0.2 pair_kernel.1
  33.0 0.0 copy-start.14
  33.0 13.3 %all_to_all.31.pairs_ref = f32[4,128,256]{2,1,0:T(8,128)S(1)} all-to-all(f32[4,128,256]{2,1,0:T(8,128)S(1)} %pair_kernel.1), channel_id=1, replica_groups={{0,32,64,96},{2,34,66,98},{4,36,68,100},{6,38,70,102},{8,40,72,104},{10..., dimensions={0} | all-to-all | bytes 1048576 | tf_op jit(solution)/shard_map/all_to_all | solution.py:551
  46.4 0.8 start_kernel.1
  47.2 0.0 copy-start
  47.2 0.0 copy-start.9
  47.2 11.2 %all_to_all.32.w_ref = f32[8,128,128]{2,1,0:T(8,128)S(1)} all-to-all(f32[8,128,128]{2,1,0:T(8,128)S(1)} %get-tuple-element.52), channel_id=1, replica_groups={{0,2,4,6,8,10,12,14},{16,18,20,22,24,26,28,30},{32,34,36,38,40,42,44,46..., dimensions={0} | all-to-all | bytes 1048576 | tf_op jit(solution)/shard_map/all_to_all | solution.py:551
  58.4 0.0 copy-start.8
  58.4 0.6 hidden_kernel.1
  59.0 1.2 %collective-permute-done.1.other_ref = f32[8,256]{1,0:T(8,128)S(1)} collective-permute-done((f32[8,256]{1,0:T(8,128)S(1)}, f32[8,256]{1,0:T(8,128)S(1)}, u32[]{:S(2)}, u32[]{:S(2)}) %collective-permute-start.1) | collective-permute-done | bytes 8224 | tf_op jit(solution)/shard_map/ppermute | solution.py:623
  60.2 1.7 %norm_kernel.1 = (bf16[256,1024]{1,0:T(8,128)(2,1)}, bf16[256,1024]{1,0:T(8,128)(2,1)}, f32[8,128,128]{2,1,0:T(8,128)}) custom-call(f32[256,1024]{1,0:T(8,128)S(1)} %get-tuple-element.53.z_ref, bf16[256,1024]{1,0:T(8,128)(2,1)S(1)} %copy-done, f32[1,1024]{1,0:T(1,128)S(1)} %get-tuple-element.51.gain_ref, f32[8,256]{1,0:T(8,128)S(1)} %get-tuple-element.54.own_ref, ...), custom_call_target="tpu_custom_call" | custom-call | flops 2000000000 | bytes 4235264 | tf_op jit(solution)/shard_map/norm_kernel/pallas_call | solution.py:54
  61.9 3.5 %all-to-all-start.3 = ((f32[8,128,128]{2,1,0:T(8,128)}), f32[8,128,128]{2,1,0:T(8,128)S(1)}, u32[]{:S(2)}, u32[]{:S(2)}) async-start(f32[8,128,128]{2,1,0:T(8,128)} %get-tuple-element.69), calls=%async_computation.3 | async-start | bytes 1048576 | tf_op jit(solution)/shard_map/all_to_all | solution.py:551
  65.4 1.5 %adjoint_kernel.1 = (f32[4,128,128]{2,1,0:T(8,128)}, f32[4,128,128]{2,1,0:T(8,128)}, f32[128,128]{1,0:T(8,128)}, f32[7,128,128]{2,1,0:T(8,128)S(1)}) custom-call(f32[4,128,256]{2,1,0:T(8,128)S(1)} %all_to_all.31.pairs_ref, f32[8,128,256]{2,1,0:T(8,128)S(1)} %all_to_all.30.ab_ref, f32[6,128,128]{2,1,0:T(8,128)S(1)} %get-tuple-element.66.factors_ref, ...), custom_call_target="tpu_custom_call" | custom-call | flops 2000000000 | bytes 4194304 | tf_op jit(solution)/shard_map/adjoint_kernel/pallas_call | solution.py:54
  66.9 0.8 copy-done.12
  67.6 4.0 %query_kernel.1 = (bf16[256,1024]{1,0:T(8,128)(2,1)}, bf16[8,256,128]{2,1,0:T(8,128)(2,1)}, bf16[8,256,128]{2,1,0:T(8,128)(2,1)}, f32[8,128]{1,0:T(8,128)S(1)}) custom-call(bf16[256,1024]{1,0:T(8,128)(2,1)} %q_hbm.3, bf16[256,1024]{1,0:T(8,128)(2,1)} %k_ref.1, f32[8,256]{1,0:T(8,128)} %e_ref.1, bf16[8,256,256]{2,1,0:T(8,128)(2,1)} %get-tuple-element.43.tkv_hbm, ...), custom_call_target="tpu_custom_call" | custom-call | flops 2000000000 | bytes 6307840 | tf_op jit(solution)/shard_map/query_kernel/pallas_call | solution.py:54
  71.7 3.7 %all-to-all-done.3.g_ref = f32[8,128,128]{2,1,0:T(8,128)S(1)} async-done(((f32[8,128,128]{2,1,0:T(8,128)}), f32[8,128,128]{2,1,0:T(8,128)S(1)}, u32[]{:S(2)}, u32[]{:S(2)}) %all-to-all-start.3) | async-done | bytes 524320 | tf_op jit(solution)/shard_map/all_to_all | solution.py:551
  75.4 0.6 gather_kernel.1
  76.0 2.8 %collective-permute-start.2 = (f32[128,128]{1,0:T(8,128)S(1)}, f32[128,128]{1,0:T(8,128)S(1)}, u32[]{:S(2)}, u32[]{:S(2)}) collective-permute-start(f32[128,128]{1,0:T(8,128)S(1)} %get-tuple-element.73.own_ref), channel_id=1, source_target_pairs={{0,16},{2,18},{4,20},{6,22},{8,24},{10,26},{12,28},{14,30},{16,0},... | collective-permute-start | bytes 196616 | tf_op jit(solution)/shard_map/ppermute | solution.py:670
  78.8 3.8 %adjoint_residual_kernel.1 = (bf16[8,256,128]{2,1,0:T(8,128)(2,1)}, bf16[8,256,128]{2,1,0:T(8,128)(2,1)}, f32[8,128]{1,0:T(8,128)S(1)}) custom-call(bf16[256,1024]{1,0:T(8,128)(2,1)} %k_ref.1, f32[8,256]{1,0:T(8,128)} %e_ref.1, bf16[8,256,256]{2,1,0:T(8,128)(2,1)} %get-tuple-element.59.se_hbm, bf16[8,2,128,128]{3,2,1,0:T(8,128)(2,1)} %get-tuple-element.60.t_hbm, ...), custom_call_target="tpu_custom_call" | custom-call | flops 2000000000 | bytes 5783552 | tf_op jit(solution)/shard_map/adjoint_residual_kernel/pallas_call | solution.py:54
  82.6 0.2 pair_gradient_kernel.1
  82.9 9.5 %all_to_all.33.later_ref = f32[4,128,128]{2,1,0:T(8,128)S(1)} all-to-all(f32[4,128,128]{2,1,0:T(8,128)S(1)} %pair_gradient_kernel.1), channel_id=1, replica_groups={{0,32,64,96},{2,34,66,98},{4,36,68,100},{6,38,70,102},{8,40,72,104},{10..., dimensions={0} | all-to-all | bytes 524288 | tf_op jit(solution)/shard_map/all_to_all | solution.py:551
  92.4 1.0 end_kernel.1
  93.4 0.0 copy-start.1
  93.4 0.0 copy-start.2
  93.4 11.8 %all_to_all.34.d_ref = f32[8,136,128]{2,1,0:T(8,128)S(1)} all-to-all(f32[8,136,128]{2,1,0:T(8,128)S(1)} %end_kernel.1), channel_id=1, replica_groups={{0,2,4,6,8,10,12,14},{16,18,20,22,24,26,28,30},{32,34,36,38,40,42,44,46..., dimensions={0} | all-to-all | bytes 1114112 | tf_op jit(solution)/shard_map/all_to_all | solution.py:551
  105.3 2.9 %key_kernel.1 = (bf16[256,1024]{1,0:T(8,128)(2,1)}, bf16[256,1024]{1,0:T(8,128)(2,1)}, f32[8,256]{1,0:T(8,128)}, f32[8,256]{1,0:T(8,128)}) custom-call(bf16[256,1024]{1,0:T(8,128)(2,1)S(1)} %copy-done.1, f32[8,256]{1,0:T(8,128)S(1)} %copy-done.2, bf16[8,256,128]{2,1,0:T(8,128)(2,1)S(1)} %copy-done.7, bf16[8,256,128]{2,1,0:T(8,128)(2,1)S(1)} %copy-done.5, ...), custom_call_target="tpu_custom_call" | custom-call | flops 2000000000 | bytes 7421952 | tf_op jit(solution)/shard_map/key_kernel/pallas_call | solution.py:54
  (27 shorter events, 0.1 us)
Async XLA Ops:
  26.2 6.6 %collective-permute-start = (f32[128,256]{1,0:T(8,128)S(1)}, f32[128,256]{1,0:T(8,128)S(1)}, u32[]{:S(2)}, u32[]{:S(2)}) collective-permute-start(f32[128,256]{1,0:T(8,128)S(1)} %get-tuple-element.48.own_ref), channel_id=1, source_target_pairs={{0,16},{2,18},{4,20},{6,22},{8,24},{10,26},{12,28},{14,30},{16,0},... | collective-permute-start | bytes 393224 | tf_op jit(solution)/shard_map/ppermute | solution.py:601
  33.0 13.3 %copy-start.14 = (f32[128,128]{1,0:T(8,128)S(1)}, f32[128,128]{1,0:T(8,128)}, u32[]{:S(2)}) copy-start(f32[128,128]{1,0:T(8,128)} %get-tuple-element.50.init_ref) | copy-start | bytes 196612
  46.4 12.0 %copy-start.3 = (f32[8,256,128]{2,1,0:T(8,128)S(1)}, f32[8,256,128]{2,1,0:T(8,128)}, u32[]{:S(2)}) copy-start(f32[8,256,128]{2,1,0:T(8,128)} %get-tuple-element.45.c_ref) | copy-start | bytes 3145732
  47.2 11.2 %copy-start = (bf16[256,1024]{1,0:T(8,128)(2,1)S(1)}, bf16[256,1024]{1,0:T(8,128)(2,1)}, u32[]{:S(2)}) copy-start(bf16[256,1024]{1,0:T(8,128)(2,1)} %cot_ref.3) | copy-start | bytes 1572868
  47.2 11.2 %copy-start.9 = (bf16[8,256,128]{2,1,0:T(8,128)(2,1)S(1)}, bf16[8,256,128]{2,1,0:T(8,128)(2,1)}, u32[]{:S(2)}) copy-start(bf16[8,256,128]{2,1,0:T(8,128)(2,1)} %get-tuple-element.44.qt_ref) | copy-start | bytes 1572868
  58.4 1.8 %copy-start.8 = (bf16[8,128,256]{2,1,0:T(8,128)(2,1)S(1)}, bf16[8,128,256]{2,1,0:T(8,128)(2,1)}, u32[]{:S(2)}) copy-start(bf16[8,128,256]{2,1,0:T(8,128)(2,1)} %get-tuple-element.55.qtt_ref) | copy-start | bytes 1572868
  59.0 1.2 %collective-permute-start.1 = (f32[8,256]{1,0:T(8,128)S(1)}, f32[8,256]{1,0:T(8,128)S(1)}, u32[]{:S(2)}, u32[]{:S(2)}) collective-permute-start(f32[8,256]{1,0:T(8,128)S(1)} %get-tuple-element.54.own_ref), channel_id=1, source_target_pairs={{0,1},{1,0},{2,3},{3,2},{4,5},{5,4},{6,7},{7,6},{8,9},{9,8},{10,11... | collective-permute-start | bytes 24584 | tf_op jit(solution)/shard_map/ppermute | solution.py:623
  61.9 13.5 %all-to-all-start.3 = ((f32[8,128,128]{2,1,0:T(8,128)}), f32[8,128,128]{2,1,0:T(8,128)S(1)}, u32[]{:S(2)}, u32[]{:S(2)}) async-start(f32[8,128,128]{2,1,0:T(8,128)} %get-tuple-element.69), calls=%async_computation.3 | async-start | bytes 1048576 | tf_op jit(solution)/shard_map/all_to_all | solution.py:551
  66.9 0.8 copy-start.12
  67.6 7.7 %copy-start.13 = (f32[7,128,128]{2,1,0:T(8,128)S(1)}, f32[7,128,128]{2,1,0:T(8,128)}, u32[]{:S(2)}) copy-start(f32[7,128,128]{2,1,0:T(8,128)} %copy-done.12) | copy-start | bytes 1376260
  76.0 6.7 %collective-permute-start.2 = (f32[128,128]{1,0:T(8,128)S(1)}, f32[128,128]{1,0:T(8,128)S(1)}, u32[]{:S(2)}, u32[]{:S(2)}) collective-permute-start(f32[128,128]{1,0:T(8,128)S(1)} %get-tuple-element.73.own_ref), channel_id=1, source_target_pairs={{0,16},{2,18},{4,20},{6,22},{8,24},{10,26},{12,28},{14,30},{16,0},... | collective-permute-start | bytes 196616 | tf_op jit(solution)/shard_map/ppermute | solution.py:670
  78.8 3.8 %copy-start.15 = (f32[128,128]{1,0:T(8,128)S(1)}, f32[128,128]{1,0:T(8,128)}, u32[]{:S(2)}) copy-start(f32[128,128]{1,0:T(8,128)} %get-tuple-element.74.early_ref) | copy-start | bytes 196612
  82.9 9.5 %copy-start.10 = (f32[4,128,128]{2,1,0:T(8,128)S(1)}, f32[4,128,128]{2,1,0:T(8,128)}, u32[]{:S(2)}) copy-start(f32[4,128,128]{2,1,0:T(8,128)} %get-tuple-element.67.after_ref) | copy-start | bytes 786436
  82.9 9.5 %copy-start.11 = (f32[4,128,128]{2,1,0:T(8,128)S(1)}, f32[4,128,128]{2,1,0:T(8,128)}, u32[]{:S(2)}) copy-start(f32[4,128,128]{2,1,0:T(8,128)} %get-tuple-element.68.first_ref) | copy-start | bytes 786436
  92.4 12.8 %copy-start.5 = (bf16[8,256,128]{2,1,0:T(8,128)(2,1)S(1)}, bf16[8,256,128]{2,1,0:T(8,128)(2,1)}, u32[]{:S(2)}) copy-start(bf16[8,256,128]{2,1,0:T(8,128)(2,1)} %get-tuple-element.63.er_ref) | copy-start | bytes 1572868
  92.4 12.8 %copy-start.6 = (bf16[8,256,128]{2,1,0:T(8,128)(2,1)S(1)}, bf16[8,256,128]{2,1,0:T(8,128)(2,1)}, u32[]{:S(2)}) copy-start(bf16[8,256,128]{2,1,0:T(8,128)(2,1)} %get-tuple-element.64.u_ref) | copy-start | bytes 1572868
  92.4 12.8 %copy-start.7 = (bf16[8,256,128]{2,1,0:T(8,128)(2,1)S(1)}, bf16[8,256,128]{2,1,0:T(8,128)(2,1)}, u32[]{:S(2)}) copy-start(bf16[8,256,128]{2,1,0:T(8,128)(2,1)} %get-tuple-element.62.tek_ref) | copy-start | bytes 1572868
  93.4 11.9 %copy-start.1 = (bf16[256,1024]{1,0:T(8,128)(2,1)S(1)}, bf16[256,1024]{1,0:T(8,128)(2,1)}, u32[]{:S(2)}) copy-start(bf16[256,1024]{1,0:T(8,128)(2,1)} %k_ref.1) | copy-start | bytes 1572868
  93.4 11.9 %copy-start.2 = (f32[8,256]{1,0:T(8,128)S(1)}, f32[8,256]{1,0:T(8,128)}, u32[]{:S(2)}) copy-start(f32[8,256]{1,0:T(8,128)} %e_ref.1) | copy-start | bytes 24580
  93.4 11.9 %copy-start.4 = (bf16[8,256,128]{2,1,0:T(8,128)(2,1)S(1)}, bf16[8,256,128]{2,1,0:T(8,128)(2,1)}, u32[]{:S(2)}) copy-start(bf16[8,256,128]{2,1,0:T(8,128)(2,1)} %get-tuple-element.65.dkp_ref) | copy-start | bytes 1572868
